TPU v7x, 32 devices: a whole 2x2x4 slice. The times are simulated.
32 devices in a mesh: dp: 16 (over z, x, core), tp: 2 (over y).
Axes of the slice: x: 2, y: 2, z: 4, core: 2. Of those that a mesh axis runs over, the one named last changes fastest.
Arguments:
- tokens: bfloat16 [32768, 768], P(('dp', 'tp')), may hold values from -6 to 6
- neighbours: bfloat16 [512, 256, 768], P('dp', 'tp'), may hold values from -6 to 6
- nbr_index: int32 [16, 32], P('dp'), may hold values from 0 to 31, each once within a row
- lengths: int32 [16, 2], P('dp'), may hold values from 256 to 1024, as said below
- w_qkv: bfloat16 [768, 3, 768], P(None, None, 'tp'), may hold values from -0.21875 to 0.21875
- qv_bias: bfloat16 [2, 768], P(None, 'tp'), may hold values from -4 to 4
- w_out: bfloat16 [768, 768], P('tp'), may hold values from -2.5 to 2.5
- cross_q: bfloat16 [768, 768], P(None, 'tp'), may hold values from -0.21875 to 0.21875
- cross_kv: bfloat16 [768, 2, 768], P(None, None, 'tp'), may hold values from -0.21875 to 0.21875
- cross_bias: bfloat16 [2, 768], P(None, 'tp'), may hold values from -4 to 4
- cross_out: bfloat16 [768, 768], P('tp'), may hold values from -1.75 to 1.75
- out_bias: bfloat16 [2, 768], P(None, 'tp'), may hold values from -4 to 4
- ln_gain: bfloat16 [3, 768], P(None, 'tp'), may hold values from 0.5 to 1.5
- ln_bias: bfloat16 [3, 768], P(None, 'tp'), may hold values from -4 to 4
- fc_in: bfloat16 [768, 3072], P('tp'), may hold values from -0.21875 to 0.21875
- fc_in_bias: bfloat16 [3072], P('tp'), may hold values from -4 to 4
- fc_out: bfloat16 [3072, 768], P('tp'), may hold values from -0.109375 to 0.109375
- fc_out_bias: bfloat16 [768], P('tp'), may hold values from -4 to 4
- cotangent: bfloat16 [32768, 768], P(('dp', 'tp')), may hold values from -6 to 6
Outputs:
- block_out: bfloat16 [32768, 768], P(('dp', 'tp'))
- tokens_grad: float32 [32768, 768], P(('dp', 'tp'))
- neighbours_grad: float32 [512, 256, 768], P('dp', 'tp')
- w_qkv_grad: float32 [768, 3, 768], P(None, None, 'tp')
- qv_bias_grad: float32 [2, 768], P(None, 'tp')
- w_out_grad: float32 [768, 768], P('tp')
- cross_q_grad: float32 [768, 768], P(None, 'tp')
- cross_kv_grad: float32 [768, 2, 768], P(None, None, 'tp')
- cross_bias_grad: float32 [2, 768], P(None, 'tp')
- cross_out_grad: float32 [768, 768], P('tp')
- out_bias_grad: float32 [2, 768], P(None, 'tp')
- ln_gain_grad: float32 [3, 768], P(None, 'tp')
- ln_bias_grad: float32 [3, 768], P(None, 'tp')
- fc_in_grad: float32 [768, 3072], P('tp')
- fc_in_bias_grad: float32 [3072], P('tp')
- fc_out_grad: float32 [3072, 768], P('tp')
- fc_out_bias_grad: float32 [768], P('tp')
Inputs may be any that keep to these rules, and one draw needn't show every extreme that they name: `lengths`: each group has 2 slots of 1024 token positions; positions of a slot from its length on are padding. In every group one slot is full. `nbr_index`: each row is a permutation of its group's 32 neighbour blocks.
All inputs are finite; a program needn't handle non-finite values.
Results may differ from a plain program's by a relative error of at most 0.025.
Values may be sent and summed in bfloat16 or wider, within the bound.
A program may use at most 320 MiB of HBM per device.

v0:
```python
import jax
import jax.numpy as jnp
from jax import lax
from jax.sharding import PartitionSpec as P

HEAD_DIM = 64
SPAN = 64
LEN = 1024
NBR = 256


eps_norm = 1e-05
score_scale = 0.125
masked_score = -1000000000.0


def layer_norm(row_data, norm_gain, norm_bias):
    average = jnp.mean(row_data, axis=-1, keepdims=True)
    centred = row_data - average
    spread = jnp.mean(centred * centred, axis=-1, keepdims=True)
    return centred * lax.rsqrt(spread + eps_norm) * norm_gain + norm_bias


def gelu_tanh(values):
    return jax.nn.gelu(values, approximate=True)


def shift_earlier(matrix, seq_count):
    columns = matrix.shape[-1]
    shaped = matrix.reshape(seq_count, LEN, columns)
    padding = jnp.zeros((seq_count, SPAN - 1, columns), matrix.dtype)
    return jnp.concatenate([shaped[:, SPAN - 1 :], padding], axis=1)


def shift_later(matrix, seq_count):
    columns = matrix.shape[-1]
    shaped = matrix.reshape(seq_count, LEN, columns)
    padding = jnp.zeros((seq_count, SPAN - 1, columns), matrix.dtype)
    return jnp.concatenate([padding, shaped[:, : LEN - SPAN + 1]], axis=1).reshape(
        seq_count * LEN, columns
    )


def softmax_parts(scores):
    top_score = jnp.max(scores, axis=-1, keepdims=True)
    raised = jnp.exp(scores - top_score)
    row_total = jnp.sum(raised, axis=-1, keepdims=True)
    return (raised / row_total, top_score + jnp.log(row_total))


def on_device(
    tokens,
    neighbours,
    nbr_index,
    lengths,
    w_qkv,
    qv_bias,
    w_out,
    cross_q,
    cross_kv,
    cross_bias,
    cross_out,
    out_bias,
    ln_gain,
    ln_bias,
    fc_in,
    fc_in_bias,
    fc_out,
    fc_out_bias,
    cotangent,
):
    low_type = jnp.bfloat16
    wide_type = jnp.float32
    tp_size = lax.axis_size("tp")
    tok_dev = tokens.shape[0]
    group_rows = tok_dev * tp_size
    seq_count = group_rows // LEN
    head_cols = w_qkv.shape[2]
    head_count = head_cols // HEAD_DIM
    span_count = nbr_index.shape[1]
    query_block = min(512, LEN)
    seq_blocks = LEN // query_block
    block_count = seq_count * seq_blocks
    fc_in_all, fc_out_all, fc_in_b, fc_out_b, out_b, norm_gains, norm_shifts = (
        lax.all_gather(fc_in, "tp", axis=0, tiled=True),
        lax.all_gather(fc_out, "tp", axis=0, tiled=True),
        lax.all_gather(fc_in_bias, "tp", axis=0, tiled=True),
        lax.all_gather(fc_out_bias, "tp", axis=0, tiled=True),
        lax.all_gather(out_bias, "tp", axis=1, tiled=True),
        lax.all_gather(ln_gain, "tp", axis=1, tiled=True),
        lax.all_gather(ln_bias, "tp", axis=1, tiled=True),
    )
    gains = norm_gains.astype(wide_type)
    shifts = norm_shifts.astype(wide_type)
    out_wide = out_b.astype(wide_type)
    fc_in_wide = fc_in_b.astype(wide_type)
    fc_out_wide = fc_out_b.astype(wide_type)
    tokens_wide = tokens.astype(wide_type)
    normed_one = layer_norm(tokens_wide, gains[0], shifts[0])
    rows_one = lax.all_gather(normed_one.astype(low_type), "tp", axis=0, tiled=True)
    qkv_wide = jnp.einsum("td,dkc->tkc", rows_one, w_qkv, preferred_element_type=wide_type)
    qv_wide = qv_bias.astype(wide_type)
    head_shape = (seq_count, LEN, head_count, HEAD_DIM)
    seq_queries = (qkv_wide[:, 0] + qv_wide[0]).astype(low_type).reshape(head_shape)
    seq_keys = qkv_wide[:, 1].astype(low_type).reshape(head_shape)
    seq_values = (qkv_wide[:, 2] + qv_wide[1]).astype(low_type).reshape(head_shape)
    seq_lengths = lengths[0]
    places = jnp.arange(LEN, dtype=jnp.int32)

    def self_scores(block_id):
        which_seq = block_id // seq_blocks
        offset = block_id % seq_blocks * query_block
        block_queries = lax.dynamic_slice_in_dim(seq_queries[which_seq], offset, query_block, 0)
        products = jnp.einsum(
            "qhd,khd->hqk", block_queries, seq_keys[which_seq], preferred_element_type=wide_type
        )
        query_places = offset + jnp.arange(query_block, dtype=jnp.int32)
        allowed = (places[None, :] <= query_places[:, None]) & (
            places[None, :] < seq_lengths[which_seq]
        )
        return (
            which_seq,
            offset,
            block_queries,
            jnp.where(allowed[None], products * score_scale, masked_score),
        )

    def self_forward(block_id):
        which_seq, offset, block_queries, scores = self_scores(block_id)
        probs, row_lse = softmax_parts(scores)
        context = jnp.einsum(
            "hqk,khd->qhd",
            probs.astype(low_type),
            seq_values[which_seq],
            preferred_element_type=wide_type,
        )
        return (context.astype(low_type), row_lse[..., 0])

    block_ids = jnp.arange(block_count, dtype=jnp.int32)
    self_context, self_lse = lax.map(self_forward, block_ids)
    self_context = self_context.reshape(group_rows, head_cols)
    resid_one = (
        tokens_wide
        + lax.psum_scatter(
            jnp.dot(self_context, w_out, preferred_element_type=wide_type).astype(jnp.bfloat16),
            "tp",
            scatter_dimension=0,
            tiled=True,
        ).astype(jnp.float32)
        + out_wide[0]
    )
    normed_two = layer_norm(resid_one, gains[1], shifts[1])
    rows_two, nbr_rows = (
        lax.all_gather(normed_two.astype(low_type), "tp", axis=0, tiled=True),
        lax.all_gather(neighbours, "tp", axis=1, tiled=True),
    )
    cross_wide = cross_bias.astype(wide_type)
    cross_queries = (
        jnp.dot(rows_two, cross_q, preferred_element_type=wide_type) + cross_wide[0]
    ).astype(low_type)
    key_value = jnp.einsum("bnd,dkc->bnkc", nbr_rows, cross_kv, preferred_element_type=wide_type)
    block_order = nbr_index[0]
    span_shape = (span_count, NBR, head_count, HEAD_DIM)
    query_shape = (span_count, SPAN, head_count, HEAD_DIM)
    cross_keys = key_value[:, :, 0].astype(low_type)[block_order].reshape(span_shape)
    cross_values = (
        (key_value[:, :, 1] + cross_wide[1]).astype(low_type)[block_order].reshape(span_shape)
    )
    shifted_queries = shift_earlier(cross_queries, seq_count).reshape(query_shape)

    def cross_products():
        return (
            jnp.einsum(
                "cmhd,cnhd->chmn", shifted_queries, cross_keys, preferred_element_type=wide_type
            )
            * score_scale
        )

    cross_probs, cross_lse = softmax_parts(cross_products())
    span_context = jnp.einsum(
        "chmn,cnhd->cmhd",
        cross_probs.astype(low_type),
        cross_values,
        preferred_element_type=wide_type,
    )
    cross_context = shift_later(span_context.reshape(group_rows, head_cols), seq_count).astype(
        low_type
    )
    resid_two = (
        resid_one
        + lax.psum_scatter(
            jnp.dot(cross_context, cross_out, preferred_element_type=wide_type).astype(
                jnp.bfloat16
            ),
            "tp",
            scatter_dimension=0,
            tiled=True,
        ).astype(jnp.float32)
        + out_wide[1]
    )
    normed_three = layer_norm(resid_two, gains[2], shifts[2])
    rows_three = normed_three.astype(low_type)
    hidden_pre = jnp.dot(rows_three, fc_in_all, preferred_element_type=wide_type) + fc_in_wide
    hidden_act = gelu_tanh(hidden_pre).astype(low_type)
    block_out = (
        resid_two + jnp.dot(hidden_act, fc_out_all, preferred_element_type=wide_type) + fc_out_wide
    ).astype(low_type)
    grad_out = cotangent.astype(wide_type)
    fc_out_grad = jnp.einsum("tf,td->fd", hidden_act, cotangent, preferred_element_type=wide_type)
    fc_out_bias_grad = jnp.sum(grad_out, axis=0)
    act_grad = jnp.einsum("td,fd->tf", cotangent, fc_out_all, preferred_element_type=wide_type)
    gelu_back = jax.vjp(gelu_tanh, hidden_pre)[1]
    pre_grad = gelu_back(act_grad)[0].astype(low_type)
    fc_in_grad = jnp.einsum("td,tf->df", rows_three, pre_grad, preferred_element_type=wide_type)
    fc_in_bias_grad = jnp.sum(pre_grad.astype(wide_type), axis=0)
    rows_three_grad = jnp.einsum("tf,df->td", pre_grad, fc_in_all, preferred_element_type=wide_type)
    norm_three_back = jax.vjp(layer_norm, resid_two, gains[2], shifts[2])[1]
    resid_part_three, gain_three, shift_three = norm_three_back(rows_three_grad)
    resid_two_grad = grad_out + resid_part_three
    mlp_grads = (
        lax.psum_scatter(
            fc_in_grad.astype(jnp.bfloat16), "tp", scatter_dimension=0, tiled=True
        ).astype(jnp.float32),
        lax.psum_scatter(
            fc_out_grad.astype(jnp.bfloat16), "tp", scatter_dimension=0, tiled=True
        ).astype(jnp.float32),
        lax.psum_scatter(
            fc_in_bias_grad.astype(jnp.bfloat16), "tp", scatter_dimension=0, tiled=True
        ).astype(jnp.float32),
        lax.psum_scatter(
            fc_out_bias_grad.astype(jnp.bfloat16), "tp", scatter_dimension=0, tiled=True
        ).astype(jnp.float32),
    )
    cross_bias_out = jnp.sum(resid_two_grad, axis=0)
    cross_back = lax.all_gather(resid_two_grad.astype(low_type), "tp", axis=0, tiled=True)
    cross_out_grad = jnp.einsum(
        "tc,td->cd", cross_context, cross_back, preferred_element_type=wide_type
    )
    context_grad = jnp.einsum(
        "td,cd->tc", cross_back, cross_out, preferred_element_type=wide_type
    ).astype(low_type)
    span_grad = shift_earlier(context_grad, seq_count).reshape(query_shape)
    probs_again = jnp.exp(cross_products() - cross_lse)
    prob_grad = jnp.einsum(
        "cmhd,cnhd->chmn", span_grad, cross_values, preferred_element_type=wide_type
    )
    cross_delta = jnp.sum(probs_again * prob_grad, axis=-1, keepdims=True)
    cross_score_grad = (probs_again * (prob_grad - cross_delta)).astype(low_type)
    value_used = jnp.einsum(
        "chmn,cmhd->cnhd", probs_again.astype(low_type), span_grad, preferred_element_type=wide_type
    ).astype(low_type)
    key_used = (
        score_scale
        * jnp.einsum(
            "chmn,cmhd->cnhd", cross_score_grad, shifted_queries, preferred_element_type=wide_type
        )
    ).astype(low_type)
    query_spans = score_scale * jnp.einsum(
        "chmn,cnhd->cmhd", cross_score_grad, cross_keys, preferred_element_type=wide_type
    )
    cross_query_grad = shift_later(query_spans.reshape(group_rows, head_cols), seq_count).astype(
        low_type
    )
    block_zeros = jnp.zeros((span_count, NBR, head_cols), low_type)
    key_blocks = block_zeros.at[block_order].set(key_used.reshape(span_count, NBR, head_cols))
    value_blocks = block_zeros.at[block_order].set(value_used.reshape(span_count, NBR, head_cols))
    kv_grad = jnp.stack([key_blocks, value_blocks], axis=2)
    cross_kv_grad = jnp.einsum("bnd,bnkc->dkc", nbr_rows, kv_grad, preferred_element_type=wide_type)
    cross_bias_grad = jnp.stack(
        [
            jnp.sum(cross_query_grad.astype(wide_type), axis=0),
            jnp.sum(value_blocks.astype(wide_type), axis=(0, 1)),
        ]
    )
    cross_q_grad = jnp.einsum(
        "td,tc->dc", rows_two, cross_query_grad, preferred_element_type=wide_type
    )
    rows_two_part = jnp.einsum(
        "tc,dc->td", cross_query_grad, cross_q, preferred_element_type=wide_type
    )
    nbr_part = jnp.einsum("bnkc,dkc->bnd", kv_grad, cross_kv, preferred_element_type=wide_type)
    rows_two_grad, nbr_grad = (
        lax.psum_scatter(
            rows_two_part.astype(jnp.bfloat16), "tp", scatter_dimension=0, tiled=True
        ).astype(jnp.float32),
        lax.psum_scatter(
            nbr_part.astype(jnp.bfloat16), "tp", scatter_dimension=1, tiled=True
        ).astype(jnp.float32),
    )
    norm_two_back = jax.vjp(layer_norm, resid_one, gains[1], shifts[1])[1]
    resid_part_two, gain_two, shift_two = norm_two_back(rows_two_grad)
    resid_one_grad = resid_two_grad + resid_part_two
    self_bias_out = jnp.sum(resid_one_grad, axis=0)
    self_back = lax.all_gather(resid_one_grad.astype(low_type), "tp", axis=0, tiled=True)
    w_out_grad = jnp.einsum("tc,td->cd", self_context, self_back, preferred_element_type=wide_type)
    context_back = (
        jnp.einsum("td,cd->tc", self_back, w_out, preferred_element_type=wide_type)
        .astype(low_type)
        .reshape(head_shape)
    )

    def self_backward(block_id):
        which_seq, offset, block_queries, scores = self_scores(block_id)
        probs = jnp.exp(scores - self_lse[block_id][..., None])
        block_grad = lax.dynamic_slice_in_dim(context_back[which_seq], offset, query_block, 0)
        weight_grad = jnp.einsum(
            "qhd,khd->hqk", block_grad, seq_values[which_seq], preferred_element_type=wide_type
        )
        self_delta = jnp.sum(probs * weight_grad, axis=-1, keepdims=True)
        score_grad = (probs * (weight_grad - self_delta)).astype(low_type)
        query_part = score_scale * jnp.einsum(
            "hqk,khd->qhd", score_grad, seq_keys[which_seq], preferred_element_type=wide_type
        )
        key_part = score_scale * jnp.einsum(
            "hqk,qhd->khd", score_grad, block_queries, preferred_element_type=wide_type
        )
        value_part = jnp.einsum(
            "hqk,qhd->khd", probs.astype(low_type), block_grad, preferred_element_type=wide_type
        )
        return (query_part, key_part, value_part)

    query_parts, key_parts, value_parts = lax.map(self_backward, block_ids)
    query_grad = query_parts.reshape(group_rows, head_cols).astype(low_type)
    key_grad = (
        jnp.sum(key_parts.reshape(seq_count, seq_blocks, LEN, head_cols), axis=1)
        .reshape(group_rows, head_cols)
        .astype(low_type)
    )
    value_grad = (
        jnp.sum(value_parts.reshape(seq_count, seq_blocks, LEN, head_cols), axis=1)
        .reshape(group_rows, head_cols)
        .astype(low_type)
    )
    qkv_grad = jnp.stack([query_grad, key_grad, value_grad], axis=1)
    w_qkv_grad = jnp.einsum("td,tkc->dkc", rows_one, qkv_grad, preferred_element_type=wide_type)
    qv_bias_grad = jnp.stack(
        [
            jnp.sum(query_grad.astype(wide_type), axis=0),
            jnp.sum(value_grad.astype(wide_type), axis=0),
        ]
    )
    rows_one_grad = lax.psum_scatter(
        jnp.einsum("tkc,dkc->td", qkv_grad, w_qkv, preferred_element_type=wide_type).astype(
            jnp.bfloat16
        ),
        "tp",
        scatter_dimension=0,
        tiled=True,
    ).astype(jnp.float32)
    norm_one_back = jax.vjp(layer_norm, tokens_wide, gains[0], shifts[0])[1]
    resid_part_one, gain_one, shift_one = norm_one_back(rows_one_grad)
    tokens_grad = resid_one_grad + resid_part_one
    out_bias_grad = jnp.stack([self_bias_out, cross_bias_out])
    gain_grad = jnp.stack([gain_one, gain_two, gain_three])
    shift_grad = jnp.stack([shift_one, shift_two, shift_three])
    shared_grads = (
        lax.psum_scatter(out_bias_grad, "tp", scatter_dimension=1, tiled=True),
        lax.psum_scatter(gain_grad, "tp", scatter_dimension=1, tiled=True),
        lax.psum_scatter(shift_grad, "tp", scatter_dimension=1, tiled=True),
    )
    summed = lax.psum(
        (
            w_qkv_grad,
            qv_bias_grad,
            w_out_grad,
            cross_q_grad,
            cross_kv_grad,
            cross_bias_grad,
            cross_out_grad,
            shared_grads[0],
            shared_grads[1],
            shared_grads[2],
            mlp_grads[0],
            mlp_grads[1],
            mlp_grads[2],
            mlp_grads[3],
        ),
        "dp",
    )
    fc_grads = (summed[10], summed[11], summed[12], summed[13])
    return (
        block_out,
        tokens_grad,
        nbr_grad,
        summed[0],
        summed[1],
        summed[2],
        summed[3],
        summed[4],
        summed[5],
        summed[6],
        summed[7],
        summed[8],
        summed[9],
        fc_grads[0],
        fc_grads[2],
        fc_grads[1],
        fc_grads[3],
    )


def solution(mesh):
    return jax.shard_map(
        on_device,
        mesh=mesh,
        in_specs=(
            P(("dp", "tp"), None),
            P("dp", "tp", None),
            P("dp", None),
            P("dp", None),
            P(None, None, "tp"),
            P(None, "tp"),
            P("tp", None),
            P(None, "tp"),
            P(None, None, "tp"),
            P(None, "tp"),
            P("tp", None),
            P(None, "tp"),
            P(None, "tp"),
            P(None, "tp"),
            P("tp", None),
            P("tp"),
            P("tp", None),
            P("tp"),
            P(("dp", "tp"), None),
        ),
        out_specs=(
            P(("dp", "tp"), None),
            P(("dp", "tp"), None),
            P("dp", "tp", None),
            P(None, None, "tp"),
            P(None, "tp"),
            P("tp", None),
            P(None, "tp"),
            P(None, None, "tp"),
            P(None, "tp"),
            P("tp", None),
            P(None, "tp"),
            P(None, "tp"),
            P(None, "tp"),
            P("tp", None),
            P("tp"),
            P("tp", None),
            P("tp"),
        ),
        check_vma=False,
    )
```

profile of v0, /device:TPU:1, one launch (start us, length us, event | category | flops | bytes accessed | tf_op | source)
XLA Modules:
  0.0 1791.2 jit_solution(169531618785034152)
XLA Ops:
  21.5 48.6 %all-gather.10.cloned.1.call-done = bf16[2048,768]{1,0:T(8,128)(2,1)} async-done(((bf16[1024,768]{1,0:T(8,128)(2,1)}), bf16[2048,768]{1,0:T(8,128)(2,1)}) %all-gather.10.cloned.1.call-update) | async-done | bytes 3145744 | tf_op jit(solution)/shard_map/all_gather | solution.py:100
  70.1 6.2 fusion.96
  83.2 5.6 squeeze.82
  104.3 5.6 squeeze.80
  114.6 70.9 %while.36 = (s32[]{:T(128)}, bf16[4,512,6,64]{1,3,2,0:T(8,128)(2,1)}, f32[4,6,512]{2,1,0:T(8,128)}, s32[4]{0:T(128)S(1)}, bf16[2,1024,6,64]{1,3,2,0:T(8,128)(2,1...) while((s32[]{:T(128)}, ...), condition=%wide.region_5.6_spmd.clone.clone, body=%wide.region_2.5_spmd.clone.clone.sunk | while | flops 844298752 | bytes 48613900 | solution.py:140
  197.8 39.6 %reduce-scatter.17.cloned.1.call-done = bf16[1024,768]{1,0:T(8,128)(2,1)} async-done(((bf16[2048,768]{1,0:T(8,128)(2,1)}), bf16[1024,768]{1,0:T(8,128)(2,1)}) %reduce-scatter.17.cloned.1.call-update) | async-done | bytes 1572880 | tf_op jit(solution)/shard_map/reduce_scatter | solution.py:144
  243.8 43.8 %all-gather.14.cloned.1.call-done = bf16[2048,768]{1,0:T(8,128)(2,1)} async-done(((bf16[1024,768]{1,0:T(8,128)(2,1)}), bf16[2048,768]{1,0:T(8,128)(2,1)}) %all-gather.14.cloned.1.call-update) | async-done | bytes 3145744 | tf_op jit(solution)/shard_map/all_gather | solution.py:154
  302.5 6.3 reshape.433
  308.8 132.9 %all-gather.12.cloned.1.call-done = bf16[32,256,768]{2,1,0:T(8,128)(2,1)} async-done(((bf16[32,128,768]{2,1,0:T(8,128)(2,1)}), bf16[32,256,768]{2,1,0:T(8,128)(2,1)}) %all-gather.12.cloned.1.call-update) | async-done | bytes 12582928 | tf_op jit(solution)/shard_map/all_gather | solution.py:155
  441.6 17.8 fusion.65
  459.4 8.2 fusion.71
  467.6 8.8 fusion.62
  476.4 6.8 gather_fusion.1
  483.2 6.9 gather_fusion
  490.1 8.7 copy.95
  498.8 9.0 copy.97
  507.8 9.4 multiply_reduce_fusion.2
  524.5 6.9 convert_bitcast_fusion
  535.1 6.1 reshape_reshape.7
  554.9 38.8 %reduce-scatter.19.cloned.1.call-done = bf16[1024,768]{1,0:T(8,128)(2,1)} async-done(((bf16[2048,768]{1,0:T(8,128)(2,1)}), bf16[1024,768]{1,0:T(8,128)(2,1)}) %reduce-scatter.19.cloned.1.call-update) | async-done | bytes 1572880 | tf_op jit(solution)/shard_map/reduce_scatter | solution.py:191
  598.7 59.1 %all-gather.16.cloned.1.call-done = bf16[768,3072]{1,0:T(8,128)(2,1)} async-done(((bf16[384,3072]{1,0:T(8,128)(2,1)}), bf16[768,3072]{1,0:T(8,128)(2,1)}) %all-gather.16.cloned.1.call-update) | async-done | bytes 4718608 | tf_op jit(solution)/shard_map/all_gather | solution.py:85
  657.9 11.6 fusion.127
  669.5 52.6 %all-gather.18.cloned.1.call-done = bf16[3072,768]{1,0:T(8,128)(2,1)} async-done(((bf16[1536,768]{1,0:T(8,128)(2,1)}), bf16[3072,768]{1,0:T(8,128)(2,1)}) %all-gather.18.cloned.1.call-update) | async-done | bytes 4718608 | tf_op jit(solution)/shard_map/all_gather | solution.py:86
  722.1 18.7 %fusion.132 = (bf16[3072]{0:T(1024)(128)(2,1)}, bf16[1024,3072]{1,0:T(8,128)(2,1)}) fusion(f32[1024,3072]{1,0:T(8,128)} %fusion.127, f32[3072]{0:T(1024)S(1)} %bitcast.290, bf16[1024,768]{1,0:T(8,128)(2,1)} %param.41, bf16[3072,768]{1,0:T(8,128)(2,1)} %all-gather.18.cloned.1.call-done), kind=kOutput, calls=%fused_computation.235 | convolution fusion | flops 4901041152 | bytes 25184256 | tf_op jit(solution)/shard_map/td,fd->tf/dot_general | solution.py:211
  740.8 8.4 multiply_reduce_fusion.3
  754.5 44.0 %all-gather.20.cloned.1.call-done = bf16[2048,768]{1,0:T(8,128)(2,1)} async-done(((bf16[1024,768]{1,0:T(8,128)(2,1)}), bf16[2048,768]{1,0:T(8,128)(2,1)}) %all-gather.20.cloned.1.call-update) | async-done | bytes 3145744 | tf_op jit(solution)/shard_map/all_gather | solution.py:235
  813.0 6.2 reshape.436
  819.2 12.4 multiply_reduce_fusion.1
  831.6 10.2 multiply_convert_fusion.2
  841.9 6.8 multiply_bitcast_fusion
  852.4 6.3 reshape_reshape.8
  858.7 8.0 convert_reduce_fusion.4
  872.0 43.4 %reduce-scatter.21.cloned.1.call-done = bf16[1024,768]{1,0:T(8,128)(2,1)} async-done(((bf16[2048,768]{1,0:T(8,128)(2,1)}), bf16[1024,768]{1,0:T(8,128)(2,1)}) %reduce-scatter.21.cloned.1.call-update) | async-done | bytes 1572880 | tf_op jit(solution)/shard_map/reduce_scatter | solution.py:283
  928.3 45.0 %all-gather.22.cloned.1.call-done = bf16[2048,768]{1,0:T(8,128)(2,1)} async-done(((bf16[1024,768]{1,0:T(8,128)(2,1)}), bf16[2048,768]{1,0:T(8,128)(2,1)}) %all-gather.22.cloned.1.call-update) | async-done | bytes 3145744 | tf_op jit(solution)/shard_map/all_gather | solution.py:294
  985.7 139.0 %while.37 = (s32[]{:T(128)}, bf16[4,512,6,64]{1,3,2,0:T(8,128)(2,1)}, f32[4,1024,6,64]{1,3,2,0:T(8,128)}, f32[4,1024,6,64]{1,3,2,0:T(8,128)}, s32[4]{0:T(128)S(1...) while((s32[]{:T(128)}, ...), condition=%wide.region_22.23_spmd.clone.clone, body=%wide.region_20.22_spmd.clone.clone.sunk | while | flops 2062088704 | bytes 129600184 | solution.py:322
  1000.6 7.3 multiply_reduce_fusion.8
  1007.9 7.0 multiply_convert_fusion.7
  1035.3 7.3 multiply_reduce_fusion.8
  1042.6 7.0 multiply_convert_fusion.7
  1069.8 7.3 multiply_reduce_fusion.8
  1077.2 7.0 multiply_convert_fusion.7
  1104.5 7.3 multiply_reduce_fusion.8
  1111.8 7.0 multiply_convert_fusion.7
  1128.5 5.4 reduce_sum.326
  1146.2 8.3 bitcast_convert_fusion.1
  1155.3 10.4 convolution_convert_fusion.1
  1167.1 12.4 convolution_convert_fusion
  1180.3 9.0 fusion.83
  1189.3 8.7 copy.115
  1198.0 10.1 multiply_convert_fusion.1
  1208.1 8.6 copy.113
  1220.3 20.2 %scatter_fusion.1 = bf16[32,256,384]{2,1,0:T(8,128)(2,1)} fusion(bf16[32,256,384]{2,1,0:T(8,128)(2,1)} %broadcast_in_dim.142.clone, s32[32]{0:T(128)S(1)} %copy-done.73, bf16[32,256,384]{2,1,0:T(8,128)(2,1)} %copy.115), kind=kCustom, calls=%fused_computation.3 | custom fusion | bytes 18874496 | tf_op jit(solution)/shard_map/scatter | solution.py:266
  1244.1 20.4 %scatter_fusion = bf16[32,256,384]{2,1,0:T(8,128)(2,1)} fusion(bf16[32,256,384]{2,1,0:T(8,128)(2,1)} %broadcast_in_dim.142.clone.1, s32[32]{0:T(128)S(1)} %copy-done.73, bf16[32,256,384]{2,1,0:T(8,128)(2,1)} %copy.113), kind=kCustom, calls=%fused_computation.2 | custom fusion | bytes 18874496 | tf_op jit(solution)/shard_map/scatter | solution.py:265
  1269.0 6.1 fusion.134
  1275.2 16.5 fusion.107
  1292.7 9.5 fusion.94
  1312.8 16.2 bitcast_convert_fusion
  1340.5 13.4 add_convert_fusion
  1362.6 169.1 %all-reduce.12.cloned.1.call-done = (f32[768,3,384]{2,0,1:T(8,128)}, f32[384,768]{1,0:T(8,128)}, f32[768,384]{1,0:T(8,128)}, f32[768,2,384]{0,2,1:T(8,128)}, f32[384,768]{1,0:T(8,128)}) async-done(((f32[768,3,384]{2,0,1:T(8,128)}, f32[384,768]{1,0:T(8,128)}, f32[768,384]{1,0:T(8,128)}, f32[768,2,384]{0,2,1:T(8,128)}, f32[384,768]{1,0:T(8,128)}), (f32[768,3,384]{2,0,1:T(8,128)}, f32[384,768]{1,0:T(8,128)}, ...) | async-done | bytes 9437200 | tf_op jit(solution)/shard_map/psum | solution.py:361
  1531.7 5.3 copy.119
  1541.1 6.1 reduce-scatter.33.cloned.1.call-done
  1548.2 14.3 reduce-scatter.35.cloned.1.call-done
  1563.5 206.1 %all-reduce.13 = (f32[2,384]{1,0:T(2,128)}, f32[2,384]{1,0:T(2,128)}, f32[2,384]{1,0:T(2,128)}, f32[3,384]{1,0:T(4,128)}, f32[3,384]{1,0:T(4,128)}, /*index=5*/f...) all-reduce(f32[2,384]{1,0:T(2,128)S(1)} %get-tuple-element.673, ...), channel_id=1, replica_groups=mesh['dp'=16,'tp'=2] {'dp'}, use_global_device_ids=true, to_apply=%region_34.35 | all-reduce | flops 2365824 | bytes 14208000 | tf_op jit(solution)/shard_map/psum | solution.py:361
  1769.7 9.3 convert_element_type.300
  (479 shorter events, 354.8 us)
Async XLA Ops:
  7.2 62.9 %copy-start = (bf16[768,3,384]{2,0,1:T(8,128)(2,1)S(1)}, bf16[768,3,384]{2,0,1:T(8,128)(2,1)}, u32[]{:S(2)}) copy-start(bf16[768,3,384]{2,0,1:T(8,128)(2,1)} %param.27) | copy-start | bytes 5308420
  7.2 12.2 copy-start.2
  7.2 8.4 copy-start.80
  7.2 62.9 %all-gather.10.cloned.1.call-start = ((), (), s32[]{:S(2)}) async-start(), calls=%async_computation.10 | async-start | bytes 4718592 | tf_op jit(solution)/shard_map/all_gather | solution.py:100
  9.1 10.3 copy-start.41
  9.1 12.2 copy-start.81
  11.2 8.2 copy-start.49
  21.2 216.2 %reduce-scatter.17.cloned.1.call-start = ((), (), s32[]{:S(2)}) async-start(), calls=%async_computation.11 | async-start | bytes 4718592 | tf_op jit(solution)/shard_map/reduce_scatter | solution.py:144
  109.9 4.7 copy-start.91
  185.6 4.8 copy-start.89
  193.9 43.5 %copy-start.3 = (bf16[1024,768]{1,0:T(8,128)(2,1)S(1)}, bf16[1024,768]{1,0:T(8,128)(2,1)}, u32[]{:S(2)}) copy-start(bf16[1024,768]{1,0:T(8,128)(2,1)} %param.23) | copy-start | bytes 4718596
  193.9 93.8 %all-gather.14.cloned.1.call-start = ((), (), s32[]{:S(2)}) async-start(), calls=%async_computation.13 | async-start | bytes 4718592 | tf_op jit(solution)/shard_map/all_gather | solution.py:154
  242.6 199.0 %all-gather.12.cloned.1.call-start = ((), (), s32[]{:S(2)}) async-start(), calls=%async_computation.12 | async-start | bytes 18874368 | tf_op jit(solution)/shard_map/all_gather | solution.py:155
  243.2 350.6 %reduce-scatter.19.cloned.1.call-start = ((), (), s32[]{:S(2)}) async-start(), calls=%async_computation.14 | async-start | bytes 4718592 | tf_op jit(solution)/shard_map/reduce_scatter | solution.py:191
  517.1 6.4 copy-start.1
  517.2 6.4 copy-start.36
  517.2 7.3 copy-start.16
  521.0 10.4 copy-start.40
  541.3 5.5 copy-start.87
  550.3 107.6 %all-gather.16.cloned.1.call-start = ((), (), s32[]{:S(2)}) async-start(), calls=%async_computation.15 | async-start | bytes 7077888 | tf_op jit(solution)/shard_map/all_gather | solution.py:85
  550.9 171.2 %all-gather.18.cloned.1.call-start = ((), (), s32[]{:S(2)}) async-start(), calls=%async_computation.16 | async-start | bytes 7077888 | tf_op jit(solution)/shard_map/all_gather | solution.py:86
  551.6 246.9 %all-gather.20.cloned.1.call-start = ((), (), s32[]{:S(2)}) async-start(), calls=%async_computation.17 | async-start | bytes 4718592 | tf_op jit(solution)/shard_map/all_gather | solution.py:235
  554.9 167.2 %copy-start.68 = (f32[2,1,1536]{2,1,0:T(1,128)}, f32[2,1,1536]{2,1,0:T(1,128)S(1)}, u32[]{:S(2)}) copy-start(f32[2,1,1536]{2,1,0:T(1,128)S(1)} %convert_element_type.316) | copy-start | bytes 36868
  596.6 61.3 %copy-start.63 = (f32[768]{0:T(1024)S(1)}, f32[768]{0:T(1024)}, u32[]{:S(2)}) copy-start(f32[768]{0:T(1024)} %get-tuple-element.584) | copy-start | bytes 9220
  596.6 61.3 %copy-start.77 = (f32[768]{0:T(1024)S(1)}, f32[768]{0:T(1024)}, u32[]{:S(2)}) copy-start(f32[768]{0:T(1024)} %get-tuple-element.587) | copy-start | bytes 9220
  596.6 152.7 %copy-start.53 = (f32[1024]{0:T(1024)}, f32[1024]{0:T(1024)S(1)}, u32[]{:S(2)}) copy-start(f32[1024]{0:T(1024)S(1)} %broadcast_multiply_fusion) | copy-start | bytes 12292
  598.7 150.5 %copy-start.61 = (f32[1024]{0:T(1024)}, f32[1024]{0:T(1024)S(1)}, u32[]{:S(2)}) copy-start(f32[1024]{0:T(1024)S(1)} %fusion.116) | copy-start | bytes 12292
  722.1 18.7 %copy-start.11 = (f32[1024,768]{1,0:T(8,128)S(1)}, f32[1024,768]{1,0:T(8,128)}, u32[]{:S(2)}) copy-start(f32[1024,768]{1,0:T(8,128)} %copy-done.10) | copy-start | bytes 9437188
  722.1 18.7 %copy-start.85 = (bf16[768,3072]{1,0:T(8,128)(2,1)S(1)}, bf16[768,3072]{1,0:T(8,128)(2,1)}, u32[]{:S(2)}) copy-start(bf16[768,3072]{1,0:T(8,128)(2,1)} %all-gather.16.cloned.1.call-done) | copy-start | bytes 14155780
  753.5 162.0 %reduce-scatter.21.cloned.1.call-start = ((), (), s32[]{:S(2)}) async-start(), calls=%async_computation.18 | async-start | bytes 4718592 | tf_op jit(solution)/shard_map/reduce_scatter | solution.py:283
  754.5 77.1 %copy-start.29 = (f32[32,6,64]{2,1,0:T(8,128)}, f32[32,6,64]{2,1,0:T(8,128)S(1)}, u32[]{:S(2)}) copy-start(f32[32,6,64]{2,1,0:T(8,128)S(1)} %log_add_fusion) | copy-start | bytes 147460
  841.9 6.9 copy-start.9
  858.7 9.7 copy-start.88
  871.9 43.5 %copy-start.44 = (f32[1024]{0:T(1024)S(1)}, f32[1024]{0:T(1024)}, u32[]{:S(2)}) copy-start(f32[1024]{0:T(1024)} %copy-done.43) | copy-start | bytes 12292
  871.9 43.5 %copy-start.48 = (f32[768]{0:T(1024)S(1)}, f32[768]{0:T(1024)}, u32[]{:S(2)}) copy-start(f32[768]{0:T(1024)} %get-tuple-element.585) | copy-start | bytes 9220
  872.0 47.4 %copy-start.58 = (f32[1024]{0:T(1024)S(1)}, f32[1024]{0:T(1024)}, u32[]{:S(2)}) copy-start(f32[1024]{0:T(1024)} %copy-done.57) | copy-start | bytes 12292
  872.0 47.4 %copy-start.52 = (f32[1024]{0:T(1024)S(1)}, f32[1024]{0:T(1024)}, u32[]{:S(2)}) copy-start(f32[1024]{0:T(1024)} %copy-done.51) | copy-start | bytes 12292
  872.0 101.3 %all-gather.22.cloned.1.call-start = ((), (), s32[]{:S(2)}) async-start(), calls=%async_computation.19 | async-start | bytes 4718592 | tf_op jit(solution)/shard_map/all_gather | solution.py:294
  928.2 377.2 %reduce-scatter.23.cloned.1.call-start = ((), (), s32[]{:S(2)}) async-start(), calls=%async_computation.20 | async-start | bytes 4718592 | tf_op jit(solution)/shard_map/reduce_scatter | solution.py:342
  978.7 7.0 copy-start.6
  978.7 7.0 copy-start.92
  1007.9 7.0 copy-start.26
  1030.7 4.5 copy-start.18
  1042.6 7.0 copy-start.26
  1065.3 4.5 copy-start.18
  1077.2 7.0 copy-start.26
  1111.8 7.0 copy-start.26
  1128.5 8.0 copy-start.24
  1154.6 203.3 %reduce-scatter.27.cloned.1.call-start = ((), (), s32[]{:S(2)}) async-start(), calls=%async_computation.22 | async-start | bytes 7077888 | tf_op jit(solution)/shard_map/reduce_scatter | solution.py:221
  1165.7 192.2 %reduce-scatter.29.cloned.1.call-start = ((), (), s32[]{:S(2)}) async-start(), calls=%async_computation.23 | async-start | bytes 7077888 | tf_op jit(solution)/shard_map/reduce_scatter | solution.py:224
  1179.4 178.5 %reduce-scatter.31.cloned.1.call-start = ((), (), s32[]{:S(2)}) async-start(), calls=%async_computation.24 | async-start | bytes 589824
  1244.1 20.5 %copy-start.34 = (bf16[48,8,2,1024]{3,1,2,0:T(8,128)(2,1)S(1)}, bf16[48,8,2,1024]{3,1,2,0:T(8,128)(2,1)}, u32[]{:S(2)}) copy-start(bf16[48,8,2,1024]{3,1,2,0:T(8,128)(2,1)} %copy-done.33) | copy-start | bytes 4718596
  1264.5 10.6 slice-start
  1264.5 10.6 copy-start.15
  1269.0 6.1 slice-start.1
  1275.1 16.5 copy-start.60
  1292.6 9.6 copy-start.32
  1292.6 239.0 %all-reduce.12.cloned.1.call-start = ((), (), s32[]{:S(2)}) async-start(), calls=%async_computation.27 | async-start | bytes 18874368 | tf_op jit(solution)/shard_map/psum | solution.py:361
  1292.7 9.6 copy-start.86
  1304.7 242.5 %reduce-scatter.33.cloned.1.call-start = ((), (), s32[]{:S(2)}) async-start(), calls=%async_computation.25 | async-start | bytes 589824
  1311.7 250.8 %reduce-scatter.35.cloned.1.call-start = ((), (), s32[]{:S(2)}) async-start(), calls=%async_computation.26 | async-start | bytes 589824
  1312.8 456.9 %reduce-scatter.25.cloned.1.call-start = ((), (), s32[]{:S(2)}) async-start(), calls=%async_computation.21 | async-start | bytes 18874368 | tf_op jit(solution)/shard_map/reduce_scatter | solution.py:286
  1329.0 7.5 copy-start.71
  1769.6 9.3 copy-start.28
  (65 other events, 153.6 us)
Sparse Core Ops, SparseCore 0:
  21.3 48.7 all-gather.9
  194.0 43.3 reduce-scatter.16
  242.7 44.9 all-gather.13
  289.2 152.4 all-gather.11
  550.4 43.3 reduce-scatter.18
  595.2 62.6 all-gather.15
  659.4 62.6 all-gather.17
  753.6 44.9 all-gather.19
  872.1 43.3 reduce-scatter.20
  928.3 44.9 all-gather.21
  1154.7 43.3 reduce-scatter.22
  1200.8 59.9 reduce-scatter.26
  1263.9 59.9 reduce-scatter.28
  1326.6 13.1 reduce-scatter.30
  1345.5 186.0 all-reduce.11
  1533.8 13.3 reduce-scatter.32
  1549.4 13.1 reduce-scatter.34
  1564.7 144.4 reduce-scatter.24
where the time goes:
time: 1810 us; the launch traced here: 1790 us
  waiting for transfers between devices  740 us (41%)
  matrix products  356 us (20%)
  local copies, waits for them, and re-layouts  267 us (15%)
  blocking collectives  226 us (12%)
  other arithmetic  157 us (9%)
  loops' own time  27.6 us (2%)
    psum x1, blocking collectives, on_device(): lax.psum((w_qkv_grad, qv_bias_grad, w_out_grad, cross_q_grad, cross_kv_gr...  206 us
    psum x1, waiting for transfers between devices, on_device(): lax.psum((w_qkv_grad, qv_bias_grad, w_out_grad, cross_q_grad, cross_kv_gr...  169 us
    all_gather x1, waiting for transfers between devices, on_device(): lax.all_gather(neighbours, 'tp', axis=1, tiled=True)  133 us
    all_gather x1, waiting for transfers between devices, on_device(): lax.all_gather(fc_in, 'tp', axis=0, tiled=True)  59.1 us
    unnamed x205, local copies, waits for them, and re-layouts  53.1 us
    all_gather x1, waiting for transfers between devices, on_device(): lax.all_gather(fc_out, 'tp', axis=0, tiled=True)  52.6 us
    all_gather x1, waiting for transfers between devices, on_device(): lax.all_gather(normed_one.astype(low_type), 'tp', axis=0, tiled=True)  48.6 us
    all_gather x1, waiting for transfers between devices, on_device(): lax.all_gather(resid_one_grad.astype(low_type), 'tp', axis=0, tiled=True)  45 us
  transfers between devices with their start and end apart: 18, of which 13 were waited for; matrix products, arithmetic and copies ran while one was open for 14% of the time, Pallas kernels for 0%

commit v1 on v0

v1 whole, which is shorter than its diff:
```python
import functools

import jax
import jax.numpy as jnp
from jax import lax
from jax.experimental import pallas as pl
from jax.experimental.pallas import tpu as pltpu
from jax.sharding import PartitionSpec as P

HEAD = 64
SPAN = 64
LEN = 1024
NBR = 256
EPS = 1e-05
BF = jnp.bfloat16
F32 = jnp.float32
DEAD = -1e30
VMEM_LIMIT = 60 * 1024 * 1024

NN = (((1,), (0,)), ((), ()))
NT = (((1,), (1,)), ((), ()))
TN = (((0,), (0,)), ((), ()))


def mm(a, b, dims=NN):
    return lax.dot_general(a, b, dims, preferred_element_type=F32)


def iota(shape, dim):
    return lax.broadcasted_iota(jnp.int32, shape, dim)


def cost(flops, nbytes, exps=0):
    return pl.CostEstimate(flops=flops, bytes_accessed=nbytes, transcendentals=exps)


def params(n=1):
    return pltpu.CompilerParams(
        dimension_semantics=("arbitrary",) * n, vmem_limit_bytes=VMEM_LIMIT
    )


def self_fwd_kernel(len_ref, q_ref, k_ref, v_ref, o_ref, lse_ref):
    bq = 256
    length = len_ref[0]
    low = iota((LEN, 128), 1) < HEAD
    q = q_ref[...] * 0.125
    k = k_ref[...]
    v = v_ref[...]
    one = jnp.ones_like(v)
    zero = jnp.zeros_like(q)
    qs = (jnp.where(low, q, zero), jnp.where(low, zero, q))
    vs = (jnp.where(low, v, one), jnp.where(low, one, v))
    dead = jnp.where(iota((1, LEN), 1) < length, 0.0, DEAD).astype(F32)
    tri = iota((bq, bq), 1) <= iota((bq, bq), 0)
    low_q = low[:bq]
    for i in range(LEN // bq):
        nk = (i + 1) * bq
        outs, lses = [], []
        for h in range(2):
            s = mm(qs[h][i * bq : nk], k[:nk], NT) + dead[:, :nk]
            last = jnp.where(tri, s[:, nk - bq :], DEAD)
            s = jnp.concatenate([s[:, : nk - bq], last], axis=1) if i else last
            m = jnp.max(s, axis=1, keepdims=True)
            p = jnp.exp(s - m).astype(BF)
            o = mm(p, vs[h][:nk])
            total = pltpu.roll(o, HEAD, 1)
            outs.append(o / total)
            lses.append(m + jnp.log(total))
        o_ref[i * bq : nk, :] = jnp.where(low_q, outs[0], outs[1]).astype(BF)
        both = jnp.where(low_q, lses[0], lses[1]).T
        lse_ref[0, 0:1, i * bq : nk] = both[0:1]
        lse_ref[0, 1:2, i * bq : nk] = both[HEAD : HEAD + 1]


def self_fwd(qkv, length):
    pairs = qkv.shape[1] // 3 // 128
    block = lambda part: pl.BlockSpec((LEN, 128), lambda i, n: (0, part * pairs + i))
    return pl.pallas_call(
        self_fwd_kernel,
        grid_spec=pltpu.PrefetchScalarGridSpec(
            num_scalar_prefetch=1,
            grid=(pairs,),
            in_specs=[block(0), block(1), block(2)],
            out_specs=[
                pl.BlockSpec((LEN, 128), lambda i, n: (0, i)),
                pl.BlockSpec((1, 8, LEN), lambda i, n: (i, 0, 0)),
            ],
        ),
        out_shape=[
            jax.ShapeDtypeStruct((LEN, pairs * 128), BF),
            jax.ShapeDtypeStruct((pairs, 8, LEN), F32),
        ],
        compiler_params=params(),
        cost_estimate=cost(pairs * 2 * 4 * LEN * LEN * 128, pairs * 8 * LEN * 128),
    )(length, qkv, qkv, qkv)


def self_bwd_kernel(len_ref, q_ref, k_ref, v_ref, f_ref, o_ref, lse_ref, d_ref, dq_ref):
    bk = 256
    length = len_ref[0]
    low = iota((LEN, 128), 1) < HEAD
    q = q_ref[...] * 0.125
    k = k_ref[...]
    v = v_ref[...]
    f = f_ref[...]
    zero = jnp.zeros_like(q)
    qs = (jnp.where(low, q, zero), jnp.where(low, zero, q))
    fs = (jnp.where(low, f, zero), jnp.where(low, zero, f))
    prod = (f.astype(F32) * o_ref[...].astype(F32)).T
    deltas = (
        jnp.sum(prod[:HEAD], axis=0, keepdims=True),
        jnp.sum(prod[HEAD:], axis=0, keepdims=True),
    )
    k_t = k.T
    tri = iota((bk, bk), 0) <= iota((bk, bk), 1)
    for j in range(LEN // bk):
        lo = j * bk
        live = lo + iota((bk, 1), 0) < length
        dk = jnp.zeros((bk, 128), F32)
        dv = jnp.zeros((bk, 128), F32)
        for h in range(2):
            s = mm(k[lo : lo + bk], qs[h][lo:], NT)
            p = jnp.exp(s - lse_ref[0, h : h + 1, lo:])
            first = jnp.where(tri, p[:, :bk], 0.0)
            p = jnp.concatenate([first, p[:, bk:]], axis=1) if lo + bk < LEN else first
            if j:
                p = jnp.where(live, p, 0.0)
            dp = mm(v[lo : lo + bk], fs[h][lo:], NT)
            ds = (p * (dp - deltas[h][:, lo:])).astype(BF)
            dv += mm(p.astype(BF), fs[h][lo:])
            dk += mm(ds, qs[h][lo:])
            part = mm(k_t[h * HEAD : (h + 1) * HEAD, lo : lo + bk], ds)
            rows = slice(h * HEAD, (h + 1) * HEAD)
            if j:
                dq_ref[rows, lo:] += part
            else:
                dq_ref[rows, :] = part
        d_ref[1, lo : lo + bk, :] = dk.astype(BF)
        d_ref[2, lo : lo + bk, :] = dv.astype(BF)
    d_ref[0] = (dq_ref[...].T * 0.125).astype(BF)


def self_bwd(qkv, back, ctx, lse, length):
    pairs = qkv.shape[1] // 3 // 128
    block = lambda part: pl.BlockSpec((LEN, 128), lambda i, n: (0, part * pairs + i))
    return pl.pallas_call(
        self_bwd_kernel,
        grid_spec=pltpu.PrefetchScalarGridSpec(
            num_scalar_prefetch=1,
            grid=(pairs,),
            in_specs=[
                block(0),
                block(1),
                block(2),
                pl.BlockSpec((LEN, 128), lambda i, n: (0, i)),
                pl.BlockSpec((LEN, 128), lambda i, n: (0, i)),
                pl.BlockSpec((1, 8, LEN), lambda i, n: (i, 0, 0)),
            ],
            out_specs=pl.BlockSpec((3, LEN, 128), lambda i, n: (0, 0, i)),
            scratch_shapes=[pltpu.VMEM((128, LEN), F32)],
        ),
        out_shape=jax.ShapeDtypeStruct((3, LEN, pairs * 128), BF),
        compiler_params=params(),
        cost_estimate=cost(pairs * 2 * 10 * LEN * LEN * 128, pairs * 16 * LEN * 128),
    )(length, qkv, qkv, qkv, back, ctx, lse)


def spread(rows, mask):
    four = jnp.concatenate([rows] * 4, axis=0)
    return jnp.where(mask, four, jnp.zeros_like(four))


def gathered(rows, lanes):
    out = jnp.where(lanes == 0, rows[:SPAN], 0.0)
    for g in range(1, 4):
        out = jnp.where(lanes == g, rows[g * SPAN : (g + 1) * SPAN], out)
    return out


def cross_fwd_kernel(q_ref, own_ref, oth_ref, o_ref):
    width = q_ref.shape[1]
    mask = iota((256, 256), 0) // SPAN == iota((256, 256), 1) // HEAD
    lanes = iota((SPAN, 256), 1) // HEAD
    for t in range(width // 256):
        lo = t * 256
        q4 = spread(q_ref[:, lo : lo + 256] * 0.125, mask)
        k = jnp.concatenate([own_ref[:, lo : lo + 256], oth_ref[:, lo : lo + 256]], axis=0)
        lo += width
        v = jnp.concatenate([own_ref[:, lo : lo + 256], oth_ref[:, lo : lo + 256]], axis=0)
        s = mm(q4, k, NT)
        p = jnp.exp(s - jnp.max(s, axis=1, keepdims=True))
        total = jnp.sum(p, axis=1, keepdims=True)
        o = mm(p.astype(BF), v) / total
        o_ref[:, t * 256 : (t + 1) * 256] = gathered(o, lanes).astype(BF)


def cross_fwd(q, own, oth):
    width = q.shape[1]
    spans = q.shape[0] // SPAN
    rows = own.shape[0] // spans
    return pl.pallas_call(
        cross_fwd_kernel,
        grid=(spans,),
        in_specs=[
            pl.BlockSpec((SPAN, width), lambda i: (i, 0)),
            pl.BlockSpec((rows, 2 * width), lambda i: (i, 0)),
            pl.BlockSpec((rows, 2 * width), lambda i: (i, 0)),
        ],
        out_specs=pl.BlockSpec((SPAN, width), lambda i: (i, 0)),
        out_shape=jax.ShapeDtypeStruct(q.shape, BF),
        compiler_params=params(),
        cost_estimate=cost(spans * 3 * 4 * 256**3, spans * 1000000),
    )(q, own, oth)


def cross_bwd_kernel(q_ref, own_ref, oth_ref, e_ref, dq_ref, down_ref, doth_ref):
    width = q_ref.shape[1]
    half = own_ref.shape[0]
    mask = iota((256, 256), 0) // SPAN == iota((256, 256), 1) // HEAD
    lanes = iota((SPAN, 256), 1) // HEAD
    for t in range(width // 256):
        at = slice(t * 256, (t + 1) * 256)
        at_v = slice(width + t * 256, width + (t + 1) * 256)
        q4 = spread(q_ref[:, at] * 0.125, mask)
        e4 = spread(e_ref[:, at], mask)
        k = jnp.concatenate([own_ref[:, at], oth_ref[:, at]], axis=0)
        v = jnp.concatenate([own_ref[:, at_v], oth_ref[:, at_v]], axis=0)
        s = mm(k, q4, NT)
        p = jnp.exp(s - jnp.max(s, axis=0, keepdims=True))
        p = p * (1.0 / jnp.sum(p, axis=0, keepdims=True))
        dp = mm(v, e4, NT)
        delta = jnp.sum(p * dp, axis=0, keepdims=True)
        ds = (p * (dp - delta)).astype(BF)
        dk = mm(ds, q4).astype(BF)
        dv = mm(p.astype(BF), e4).astype(BF)
        down_ref[:, at] = dk[:half]
        doth_ref[:, at] = dk[half:]
        down_ref[:, at_v] = dv[:half]
        doth_ref[:, at_v] = dv[half:]
        dq_ref[:, at] = (gathered(mm(ds, k, TN), lanes) * 0.125).astype(BF)


def cross_bwd(q, own, oth, e):
    width = q.shape[1]
    spans = q.shape[0] // SPAN
    rows = own.shape[0] // spans
    row = pl.BlockSpec((SPAN, width), lambda i: (i, 0))
    kv = pl.BlockSpec((rows, 2 * width), lambda i: (i, 0))
    return pl.pallas_call(
        cross_bwd_kernel,
        grid=(spans,),
        in_specs=[row, kv, kv, row],
        out_specs=[row, kv, kv],
        out_shape=[
            jax.ShapeDtypeStruct(q.shape, BF),
            jax.ShapeDtypeStruct(own.shape, BF),
            jax.ShapeDtypeStruct(oth.shape, BF),
        ],
        compiler_params=params(),
        cost_estimate=cost(spans * 3 * 10 * 256**3, spans * 2000000),
    )(q, own, oth, e)


def pick_kernel(keep_ref, send_ref, a_ref, b_ref, keep_out, send_out):
    keep_out[...] = a_ref[...]
    send_out[...] = b_ref[...]


def pick_blocks(neighbours, keep, send):
    count = keep.shape[0]
    one = (1,) + neighbours.shape[1:]
    out = pl.BlockSpec(one, lambda i, a, b: (i, 0, 0))
    return pl.pallas_call(
        pick_kernel,
        grid_spec=pltpu.PrefetchScalarGridSpec(
            num_scalar_prefetch=2,
            grid=(count,),
            in_specs=[
                pl.BlockSpec(one, lambda i, a, b: (a[i], 0, 0)),
                pl.BlockSpec(one, lambda i, a, b: (b[i], 0, 0)),
            ],
            out_specs=[out, out],
        ),
        out_shape=[jax.ShapeDtypeStruct((count,) + neighbours.shape[1:], BF)] * 2,
        compiler_params=params(),
        cost_estimate=cost(0, 4 * neighbours.size),
    )(keep, send, neighbours, neighbours)


def place_kernel(order_ref, a_ref, b_ref, out_ref):
    half = pl.num_programs(0) // 2

    @pl.when(pl.program_id(0) < half)
    def _():
        out_ref[...] = a_ref[...]

    @pl.when(pl.program_id(0) >= half)
    def _():
        out_ref[...] = b_ref[...].astype(F32)


def place_blocks(order, mine, theirs):
    count = order.shape[0]
    half = count // 2
    one = (1,) + mine.shape[1:]
    return pl.pallas_call(
        place_kernel,
        grid_spec=pltpu.PrefetchScalarGridSpec(
            num_scalar_prefetch=1,
            grid=(count,),
            in_specs=[
                pl.BlockSpec(one, lambda i, o: (jnp.minimum(i, half - 1), 0, 0)),
                pl.BlockSpec(one, lambda i, o: (jnp.maximum(i - half, 0), 0, 0)),
            ],
            out_specs=pl.BlockSpec(one, lambda i, o: (o[i], 0, 0)),
        ),
        out_shape=jax.ShapeDtypeStruct((count,) + mine.shape[1:], F32),
        compiler_params=params(),
        cost_estimate=cost(0, 8 * mine.size),
    )(order, mine, theirs)


GELU_A = 0.7978845608028654
GELU_B = 0.044715


def feed_kernel(
    h_ref, g_ref, r_ref, win_ref, bin_ref, wout_ref, bout_ref,
    out_ref, dh_ref, gin_ref, gout_ref, gbin_ref, h_t, acc, dacc,
):
    step = pl.program_id(0)

    @pl.when(step == 0)
    def _():
        h_t[...] = h_ref[...].T

    win = win_ref[...]
    wout = wout_ref[...]
    pre = mm(h_ref[...], win) + bin_ref[...]
    dact = mm(g_ref[...], wout, NT)
    square = pre * pre
    th = jnp.tanh(GELU_A * pre * (1.0 + GELU_B * square))
    half = 0.5 * (1.0 + th)
    act = (pre * half).astype(BF)
    slope = half + 0.5 * pre * (1.0 - th * th) * (GELU_A * (1.0 + 3.0 * GELU_B * square))
    dpre_wide = dact * slope
    dpre = dpre_wide.astype(BF)
    gbin_ref[0:1, :] = jnp.sum(dpre.astype(F32), axis=0, keepdims=True)
    gout_ref[...] = mm(act, g_ref[...], TN).astype(BF)
    gin_ref[0] = mm(h_t[...], dpre).astype(BF)
    part = mm(act, wout)
    dpart = mm(dpre, win, NT)

    @pl.when(step == 0)
    def _():
        acc[...] = part
        dacc[...] = dpart

    @pl.when(step > 0)
    def _():
        acc[...] += part
        dacc[...] += dpart

    @pl.when(step == pl.num_programs(0) - 1)
    def _():
        out_ref[...] = (r_ref[...] + acc[...] + bout_ref[...]).astype(BF)
        dh_ref[...] = dacc[...]


def feed(h, g, r, w_in, b_in, w_out, b_out):
    rows, d = h.shape
    ff = w_in.shape[1]
    bf = 384
    per = d // bf
    whole = pl.BlockSpec((rows, d), lambda i: (0, 0))
    return pl.pallas_call(
        feed_kernel,
        grid=(ff // bf,),
        in_specs=[
            whole,
            whole,
            whole,
            pl.BlockSpec((d, bf), lambda i: (0, i)),
            pl.BlockSpec((1, bf), lambda i: (0, i)),
            pl.BlockSpec((bf, d), lambda i: (i, 0)),
            pl.BlockSpec((1, d), lambda i: (0, 0)),
        ],
        out_specs=[
            whole,
            whole,
            pl.BlockSpec((1, d, bf), lambda i: (lax.div(i, per), 0, lax.rem(i, per))),
            pl.BlockSpec((bf, d), lambda i: (i, 0)),
            pl.BlockSpec((8, bf), lambda i: (0, i)),
        ],
        out_shape=[
            jax.ShapeDtypeStruct((rows, d), BF),
            jax.ShapeDtypeStruct((rows, d), F32),
            jax.ShapeDtypeStruct((ff // d, d, d), BF),
            jax.ShapeDtypeStruct((ff, d), BF),
            jax.ShapeDtypeStruct((8, ff), F32),
        ],
        scratch_shapes=[
            pltpu.VMEM((d, rows), BF),
            pltpu.VMEM((rows, d), F32),
            pltpu.VMEM((rows, d), F32),
        ],
        compiler_params=params(),
        cost_estimate=cost(12 * rows * d * ff, 8 * d * ff),
    )(h, g, r, w_in, b_in, w_out, b_out)


def norm(rows, gain, bias):
    mean = jnp.mean(rows, axis=-1, keepdims=True)
    centred = rows - mean
    spread_ = jnp.mean(centred * centred, axis=-1, keepdims=True)
    return centred * lax.rsqrt(spread_ + EPS) * gain + bias


def norm_back(rows, gain, grad):
    mean = jnp.mean(rows, axis=-1, keepdims=True)
    centred = rows - mean
    rstd = lax.rsqrt(jnp.mean(centred * centred, axis=-1, keepdims=True) + EPS)
    hat = centred * rstd
    scaled = grad * gain
    inner = jnp.mean(scaled * hat, axis=-1, keepdims=True)
    back = rstd * (scaled - jnp.mean(scaled, axis=-1, keepdims=True) - hat * inner)
    return back, jnp.sum(grad * hat, axis=0), jnp.sum(grad, axis=0)


class Links:
    def __init__(self, dp, tp):
        self.dp = dp
        self.bits = dp.bit_length() - 1
        self.me = lax.axis_index("dp")
        self.half = lax.axis_index("tp")
        self.swap = [(i, tp - 1 - i) for i in range(tp)]

    def other(self, x):
        return lax.ppermute(x, "tp", self.swap)

    def across(self, x, bit):
        return lax.ppermute(x, "dp", [(i, i ^ (1 << bit)) for i in range(self.dp)])

    def flag(self, bit):
        return (self.me >> bit) & 1

    def joined(self, mine, theirs, flag, axis=0):
        return jnp.where(
            flag == 0,
            jnp.concatenate([mine, theirs], axis=axis),
            jnp.concatenate([theirs, mine], axis=axis),
        )

    def fetch(self, w):
        rows = w.shape[0] // 4
        core, chip = self.flag(0), self.flag(1)
        part = lax.dynamic_slice_in_dim(w, (2 * core + chip) * rows, rows, 0)
        part = self.other(part)
        part = self.joined(part, self.across(part, 1), chip)
        return self.joined(part, self.across(part, 0), core)


class Chain:
    def __init__(self, rows, cols, order):
        self.rows, self.cols, self.order = rows, cols, order
        self.shapes, self.plan = [], []
        size, parts, split = rows, 2, []
        for step in order:
            if step == "tp":
                self.plan.append(("tp", None, size))
                self.shapes.append((1, size, cols))
                parts = 1
            elif (size // 2) % 16 == 0:
                size //= 2
                self.plan.append(("split", step, size))
                self.shapes.append((parts, size, cols))
                split.append((step, size))
            else:
                self.plan.append(("add", step, size))
                self.shapes.append((parts, size, cols))
        self.last = size
        self.back = list(reversed(split))
        self.count = len(self.plan) + len(self.back)

    def scratch(self):
        return [pltpu.VMEM((2, self.rows // 2, self.cols), BF)] + [
            pltpu.VMEM(shape, BF) for shape in self.shapes
        ]

    def bind(self, own, oth, out, acc, recv, send_sem, recv_sem, local_sem):
        self.own, self.oth, self.out, self.acc, self.recv = own, oth, out, acc, recv
        self.send_sem, self.recv_sem, self.local_sem = send_sem, recv_sem, local_sem
        me = lax.axis_index("dp")
        self.me = me
        flag = lambda bit: lax.rem(lax.div(me, 1 << bit), 2)
        self.flag = flag
        self.offsets, at = [], 0
        first = True
        for kind, bit, size in self.plan:
            self.offsets.append(at)
            if kind == "split" and not first:
                at = at + flag(bit) * size
            first = False
        self.at = at
        self.start_of = flag(self.order[0]) * (self.rows // 2)
        self.both = [True] * len(self.plan)
        seen = False
        for i, (kind, _, _) in enumerate(self.plan):
            self.both[i] = not seen
            seen = seen or kind == "tp"
        return self

    def partner(self, bit):
        return {"dp": self.me + (1 - 2 * self.flag(bit)) * (1 << bit)}

    def remote(self, src, dst, sem, where):
        return pltpu.make_async_remote_copy(
            src_ref=src,
            dst_ref=dst,
            send_sem=self.send_sem.at[sem],
            recv_sem=self.recv_sem.at[sem],
            device_id=where,
            device_id_type=pl.DeviceIdType.MESH,
        )

    def copies(self, i):
        n = len(self.plan)
        ds = lambda at, size: pl.ds(pl.multiple_of(at, 16), size)
        if i == 0:
            _, bit, size = self.plan[0]
            f = self.flag(bit)
            keep, send = ds(f * size, size), ds((1 - f) * size, size)
            where = self.partner(bit)
            return [
                self.remote(self.own.at[send], self.recv[0].at[0], 0, where),
                self.remote(self.oth.at[send], self.recv[0].at[1], self.count, where),
            ], [
                pltpu.make_async_copy(self.own.at[keep], self.acc.at[0], self.local_sem.at[0]),
                pltpu.make_async_copy(self.oth.at[keep], self.acc.at[1], self.local_sem.at[1]),
            ]
        if i < n:
            kind, bit, size = self.plan[i]
            at = self.offsets[i]
            if kind == "tp":
                where = {"tp": 1 - lax.axis_index("tp")}
                return [self.remote(self.acc.at[1, ds(at, size)], self.recv[i].at[0], i, where)], []
            if kind == "split":
                at = at + (1 - self.flag(bit)) * size
            src = self.acc.at[:, ds(at, size)] if self.both[i] else self.acc.at[0:1, ds(at, size)]
            return [self.remote(src, self.recv[i], i, self.partner(bit))], []
        k = i - n
        here = self.start_of + self.at
        mine = self.acc.at[0, ds(self.at, self.last)]
        if k == 0:
            dst = self.out.at[ds(here, self.last)]
            return [self.remote(mine, dst, i, self.partner(self.back[0][0]))], [
                pltpu.make_async_copy(mine, dst, self.local_sem.at[2])
            ]
        for bit, size in self.back[:k]:
            here = here - self.flag(bit) * size
        size = 2 * self.back[k - 1][1]
        region = self.out.at[ds(here, size)]
        return [self.remote(region, region, i, self.partner(self.back[k][0]))], []

    def start(self, i):
        remote, local = self.copies(i)
        for copy in remote + local:
            copy.start()

    def finish(self, i):
        remote, local = self.copies(i)
        for copy in remote + local:
            copy.wait()
        if i >= len(self.plan):
            return
        kind, bit, size = self.plan[i]
        at = self.offsets[i]
        if kind == "split" and i:
            at = at + self.flag(bit) * size
        parts = self.shapes[i][0]
        acc, recv = self.acc, self.recv[i]
        rows = next(r for r in (96, 48, 32, 16) if size % r == 0)

        def body(j, carry):
            to = pl.ds(pl.multiple_of(at + j * rows, 16), rows)
            fr = pl.ds(pl.multiple_of(j * rows, 16), rows)
            for part in range(parts):
                acc[part, to, :] = acc[part, to, :] + recv[part, fr, :]
            return carry

        lax.fori_loop(0, size // rows, body, 0)


def greet(bits):
    me = lax.axis_index("dp")
    barrier = pltpu.get_barrier_semaphore()
    for bit in range(bits):
        to = me + (1 - 2 * lax.rem(lax.div(me, 1 << bit), 2)) * (1 << bit)
        pl.semaphore_signal(
            barrier, inc=1, device_id={"dp": to}, device_id_type=pl.DeviceIdType.MESH
        )
    pl.semaphore_signal(
        barrier,
        inc=1,
        device_id={"tp": 1 - lax.axis_index("tp")},
        device_id_type=pl.DeviceIdType.MESH,
    )
    pl.semaphore_wait(barrier, bits + 1)


def reduce_kernel(chains, bits, *refs):
    n = len(chains)
    ins, outs, rest = refs[: 2 * n], refs[2 * n : 3 * n], list(refs[3 * n :])
    send_sem, recv_sem, local_sem = rest[-3:]
    for c, chain in enumerate(chains):
        size = 1 + len(chain.plan)
        acc, *recv = rest[:size]
        rest = rest[size:]
        chain.bind(
            ins[2 * c], ins[2 * c + 1], outs[c], acc, recv,
            send_sem.at[c], recv_sem.at[c], local_sem.at[c],
        )
    greet(bits)
    for chain in chains:
        chain.start(0)
    for i in range(max(c.count for c in chains)):
        for chain in chains:
            if i < chain.count:
                chain.finish(i)
                if i + 1 < chain.count:
                    chain.start(i + 1)


def reduce_all(grads, dp, orders):
    bits = dp.bit_length() - 1
    chains = [Chain(g[0].shape[0], g[0].shape[1], o) for g, o in zip(grads, orders)]
    most = max(c.count for c in chains) + 1
    flat = [x for g in grads for x in g]
    anywhere = pl.BlockSpec(memory_space=pl.ANY)
    return pl.pallas_call(
        functools.partial(reduce_kernel, chains, bits),
        in_specs=[anywhere] * len(flat),
        out_specs=[anywhere] * len(grads),
        out_shape=[jax.ShapeDtypeStruct(g[0].shape, BF) for g in grads],
        scratch_shapes=[s for c in chains for s in c.scratch()]
        + [
            pltpu.SemaphoreType.DMA((len(chains), most)),
            pltpu.SemaphoreType.DMA((len(chains), most)),
            pltpu.SemaphoreType.DMA((len(chains), 3)),
        ],
        compiler_params=pltpu.CompilerParams(
            collective_id=0, has_side_effects=True, vmem_limit_bytes=VMEM_LIMIT
        ),
        cost_estimate=cost(0, sum(2 * x.size for x in flat)),
    )(*flat)


def shift_earlier(x):
    pad = jnp.zeros((SPAN - 1, x.shape[1]), x.dtype)
    return jnp.concatenate([x[SPAN - 1 :], pad], axis=0)


def shift_later(x):
    pad = jnp.zeros((SPAN - 1, x.shape[1]), x.dtype)
    return jnp.concatenate([pad, x[: x.shape[0] - SPAN + 1]], axis=0)


def on_device(
    tokens, neighbours, nbr_index, lengths, w_qkv, qv_bias, w_out, cross_q, cross_kv,
    cross_bias, cross_out, out_bias, ln_gain, ln_bias, fc_in, fc_in_bias, fc_out,
    fc_out_bias, cotangent,
):
    tp = lax.axis_size("tp")
    link = Links(lax.axis_size("dp"), tp)
    half = link.half
    d = tokens.shape[1]
    hc = w_qkv.shape[2]
    spans = nbr_index.shape[1] // tp
    length = lax.dynamic_slice_in_dim(lengths[0], half, 1)

    small = jnp.concatenate(
        [x.reshape(-1) for x in (fc_in_bias, fc_out_bias, out_bias, ln_gain, ln_bias, qv_bias, cross_bias)]
    ).reshape(-1, 128)
    small_oth = link.other(small).reshape(-1)
    small = small.reshape(-1)
    ffh = fc_in_bias.shape[0]

    def whole(at, count, width, natural=True):
        a = small[at : at + count * width].reshape(count, width)
        b = small_oth[at : at + count * width].reshape(count, width)
        if natural:
            return link.joined(a, b, half, 1).astype(F32), at + count * width
        return (a.astype(F32), b.astype(F32)), at + count * width

    b_in, at = whole(0, 1, ffh)
    b_out, at = whole(at, 1, hc)
    out_b, at = whole(at, 2, hc)
    gains, at = whole(at, 3, hc)
    shifts, at = whole(at, 3, hc)
    qv_b, at = whole(at, 2, hc, False)
    cross_b, at = whole(at, 2, hc, False)

    qkv_own = w_qkv.reshape(d, 3 * hc)
    qkv_oth = link.fetch(qkv_own)
    wo = jnp.concatenate([w_out, link.fetch(w_out)], axis=0)
    cq_w = jnp.concatenate([cross_q, link.fetch(cross_q)], axis=1)
    kv_own = cross_kv.reshape(d, 2 * hc)
    kv_oth = link.fetch(kv_own)
    kv_w = jnp.concatenate([kv_own[:, :hc], kv_oth[:, :hc], kv_own[:, hc:], kv_oth[:, hc:]], axis=1)
    co_w = jnp.concatenate([cross_out, link.fetch(cross_out)], axis=0)
    fin = link.joined(fc_in, link.fetch(fc_in), half)
    fout = link.joined(fc_out, link.fetch(fc_out), half)

    order = nbr_index[0]
    keep = lax.dynamic_slice_in_dim(order, half * spans, spans)
    send = lax.dynamic_slice_in_dim(order, (1 - half) * spans, spans)
    nbr_own, nbr_send = pick_blocks(neighbours, keep, send)
    nbr_oth = link.other(nbr_send)
    nbr_own = nbr_own.reshape(-1, d)
    nbr_oth = nbr_oth.reshape(-1, d)

    tok = tokens.astype(F32)
    h1 = norm(tok, gains[0], shifts[0]).astype(BF)

    def project(w, which):
        bias = jnp.concatenate([qv_b[which][0], jnp.zeros((hc,), F32), qv_b[which][1]])
        return (mm(h1, w) + bias).astype(BF)

    p_own = project(qkv_own, 0)
    ctx_own, lse_own = self_fwd(p_own, length)
    p_oth = project(qkv_oth, 1)
    ctx_oth, lse_oth = self_fwd(p_oth, length)
    ctx = jnp.concatenate([ctx_own, ctx_oth], axis=1)
    r1 = tok + mm(ctx, wo) + out_b[0]
    h2 = norm(r1, gains[1], shifts[1]).astype(BF)
    cb = [jnp.concatenate([cross_b[0][i], cross_b[1][i]]) for i in range(2)]
    cq = shift_earlier((mm(h2, cq_w) + cb[0]).astype(BF))
    kv_b = jnp.concatenate([jnp.zeros((d,), F32), cb[1]])
    ckv_own = (mm(nbr_own, kv_w) + kv_b).astype(BF)
    ckv_oth = (mm(nbr_oth, kv_w) + kv_b).astype(BF)
    cctx = shift_later(cross_fwd(cq, ckv_own, ckv_oth))
    r2 = r1 + mm(cctx, co_w) + out_b[1]
    h3 = norm(r2, gains[2], shifts[2]).astype(BF)
    block_out, d_h3, g_in, g_out, g_bin = feed(h3, cotangent, r2, fin, b_in, fout, b_out)

    cot = cotangent.astype(F32)
    split = lambda x: [
        lax.dynamic_slice_in_dim(x, at * (x.shape[-2] // tp), x.shape[-2] // tp, x.ndim - 2).reshape(-1, d)
        for at in (half, 1 - half)
    ]
    back3, gain3, shift3 = norm_back(r2, gains[2], d_h3)
    d_r2 = cot + back3
    z2 = d_r2.astype(BF)
    e = mm(z2, co_w, NT).astype(BF)
    g_co = mm(cctx, z2, TN).astype(BF)
    d_cq, d_own, d_oth = cross_bwd(cq, ckv_own, ckv_oth, shift_earlier(e))
    d_cq = shift_later(d_cq)
    n_oth = mm(d_oth, kv_w, NT).astype(BF).reshape(spans, -1, d)
    n_back = link.other(n_oth)
    n_own = mm(d_own, kv_w, NT).reshape(spans, -1, d)
    nbr_grad = place_blocks(jnp.concatenate([keep, send]), n_own, n_back)
    g_kv = (mm(nbr_own, d_own, TN) + mm(nbr_oth, d_oth, TN)).astype(BF)
    g_cq = mm(h2, d_cq, TN).astype(BF)
    back2, gain2, shift2 = norm_back(r1, gains[1], mm(d_cq, cq_w, NT))
    d_r1 = d_r2 + back2
    z1 = d_r1.astype(BF)
    f = mm(z1, wo, NT).astype(BF)
    g_wo = mm(ctx, z1, TN).astype(BF)
    dq_own = self_bwd(p_own, f[:, :hc], ctx_own, lse_own, length)
    dq_oth = self_bwd(p_oth, f[:, hc:], ctx_oth, lse_oth, length)
    flat = lambda x: jnp.concatenate([x[0], x[1], x[2]], axis=1)
    dq_own_f, dq_oth_f = flat(dq_own), flat(dq_oth)
    g_qkv = [
        jnp.concatenate([mm(h1, part[i], TN).astype(BF) for i in range(3)], axis=0)
        for part in (dq_own, dq_oth)
    ]
    sides = (slice(0, hc), slice(hc, d))
    g_kvs = [jnp.concatenate([g_kv[:, s], g_kv[:, d:][:, s]], axis=0) for s in sides]
    g_rest = [
        jnp.concatenate(
            [g_cq[:, s], g_wo[s][:, :hc], g_wo[s][:, hc:], g_co[s][:, :hc], g_co[s][:, hc:]], axis=0
        )
        for s in sides
    ]
    others = list(range(2, link.bits))
    x_first = [0, 1] + others + ["tp"]
    z_first = [0] + others + [1, "tp"]
    y_first = [0, "tp", 1] + others
    s_in, s_out, s_qkv, s_kv, s_rest = reduce_all(
        [split(g_in), split(g_out), g_qkv, g_kvs, g_rest],
        link.dp,
        [x_first, z_first, y_first, z_first, x_first],
    )
    wide_rows = lambda x, n: jnp.concatenate(
        [x[i * (x.shape[0] // n) : (i + 1) * (x.shape[0] // n)] for i in range(n)], axis=1
    ).astype(F32)
    fc_in_grad = wide_rows(s_in, s_in.shape[0] // hc)
    fc_out_grad = s_out.astype(F32)
    qkv_grad = wide_rows(s_qkv, 3).reshape(d, 3, hc)
    cross_kv_grad = wide_rows(s_kv, 2).reshape(d, 2, hc)
    cross_q_grad = s_rest[:d].astype(F32)
    wo_grad = wide_rows(s_rest[d : 2 * d], 2)
    co_grad = wide_rows(s_rest[2 * d :], 2)
    d_h1 = mm(dq_own_f, qkv_own, NT) + mm(dq_oth_f, qkv_oth, NT)
    back1, gain1, shift1 = norm_back(tok, gains[0], d_h1)
    tokens_grad = d_r1 + back1

    wide = lambda x: jnp.sum(x.astype(F32), axis=0)
    natural = [
        g_bin[0],
        wide(cot),
        wide(d_r1),
        wide(d_r2),
        gain1,
        gain2,
        gain3,
        shift1,
        shift2,
        shift3,
    ]
    relative = [wide(dq_own[0]), wide(dq_oth[0]), wide(dq_own[2]), wide(dq_oth[2])]
    cqs, cvs = wide(d_cq), wide(d_own[:, d:]) + wide(d_oth[:, d:])
    relative += [cqs[:hc], cqs[hc:], cvs[:hc], cvs[hc:]]
    for i in range(0, len(relative), 2):
        natural.append(link.joined(relative[i], relative[i + 1], half))
    sums = lax.psum(jnp.concatenate(natural).reshape(-1, 128), ("dp", "tp")).reshape(-1)
    ff = ffh * tp
    gb_in = lax.dynamic_slice_in_dim(sums[:ff], half * ffh, ffh)
    rest = lax.dynamic_slice_in_dim(sums[ff:].reshape(-1, d), half * hc, hc, 1)
    return (
        block_out,
        tokens_grad,
        nbr_grad,
        qkv_grad,
        rest[9:11],
        wo_grad,
        cross_q_grad,
        cross_kv_grad,
        rest[11:13],
        co_grad,
        rest[1:3],
        rest[3:6],
        rest[6:9],
        fc_in_grad,
        gb_in,
        fc_out_grad,
        rest[0],
    )


def solution(mesh):
    return jax.shard_map(
        on_device,
        mesh=mesh,
        in_specs=(
            P(("dp", "tp"), None),
            P("dp", "tp", None),
            P("dp", None),
            P("dp", None),
            P(None, None, "tp"),
            P(None, "tp"),
            P("tp", None),
            P(None, "tp"),
            P(None, None, "tp"),
            P(None, "tp"),
            P("tp", None),
            P(None, "tp"),
            P(None, "tp"),
            P(None, "tp"),
            P("tp", None),
            P("tp"),
            P("tp", None),
            P("tp"),
            P(("dp", "tp"), None),
        ),
        out_specs=(
            P(("dp", "tp"), None),
            P(("dp", "tp"), None),
            P("dp", "tp", None),
            P(None, None, "tp"),
            P(None, "tp"),
            P("tp", None),
            P(None, "tp"),
            P(None, None, "tp"),
            P(None, "tp"),
            P("tp", None),
            P(None, "tp"),
            P(None, "tp"),
            P(None, "tp"),
            P("tp", None),
            P("tp"),
            P("tp", None),
            P("tp"),
        ),
        check_vma=False,
    )
```

time: 1810 us -> 758 us (0.42)
  waiting for transfers between devices: 740 us -> 65.7 us
  Pallas kernels: 0 us -> 370 us
  matrix products: 356 us -> 101 us
  local copies, waits for them, and re-layouts: 267 us -> 75.7 us
  blocking collectives: 226 us -> 38.8 us
  other arithmetic: 157 us -> 63.6 us
  starting transfers between devices: 0.74 us -> 30.1 us
  loops' own time: 27.6 us -> 0 us
    all_gather x7 -> x0, waiting for transfers between devices: 426 us -> none  [the longest x1 133 us: on_device(): lax.all_gather(neighbours, 'tp', axis=1, tiled=True)]
    pallas_call x0 -> x10, Pallas kernels: none -> 370 us  [the longest x1 182 us: reduce_all(): pl.pallas_call(functools.partial(reduce_kernel, chains, bits), in_specs=[...]
    dot_general x55 -> x25, matrix products: 356 us -> 101 us  [mm(): return lax.dot_general(a, b, dims, preferred_element_type=F32)]
    psum x1 -> x0, waiting for transfers between devices: 169 us -> none  [on_device(): lax.psum((w_qkv_grad, qv_bias_grad, w_out_grad, cross_q_grad, cross_kv_gr...]
    psum x1, blocking collectives: 206 us -> 38.8 us  [on_device(): lax.psum(jnp.concatenate(natural).reshape(-1, 128), ('dp', 'tp'))]
    reduce_scatter x7 -> x0, waiting for transfers between devices: 122 us -> none  [the longest x1 43.4 us: on_device(): lax.psum_scatter(rows_two_part.astype(jnp.bfloat16), 'tp', scatter_dimens...]
    ppermute x0 -> x24, waiting for transfers between devices: none -> 65.7 us  [the longest x10 39.7 us: other(): return lax.ppermute(x, 'tp', self.swap)]
    reduce_sum x25 -> x12, other arithmetic: 73.2 us -> 14.7 us  [the longest x7 8.82 us: on_device(): wide = lambda x: jnp.sum(x.astype(F32), axis=0)]
  transfers between devices with their start and end apart: 18 -> 24, of which waited for: 13 -> 7; matrix products, arithmetic and copies ran while one was open for 14% -> 13% of each run, Pallas kernels for 0% -> 5%
where the time goes in v1:
time: 758 us; the launch traced here: 747 us
  Pallas kernels  370 us (49%)
  matrix products  101 us (13%)
  local copies, waits for them, and re-layouts  75.7 us (10%)
  waiting for transfers between devices  65.7 us (9%)
  other arithmetic  63.6 us (8%)
  blocking collectives  38.8 us (5%)
  starting transfers between devices  30.1 us (4%)
    pallas_call x1, Pallas kernels, reduce_all(): pl.pallas_call(functools.partial(reduce_kernel, chains, bits), in_specs=[...  182 us
    dot_general x25, matrix products, mm(): return lax.dot_general(a, b, dims, preferred_element_type=F32)  101 us
    pallas_call x1, Pallas kernels, feed(): pl.pallas_call(feed_kernel, grid=(ff // bf,), in_specs=[whole, whole, who...  53.9 us
    ppermute x10, waiting for transfers between devices, other(): return lax.ppermute(x, 'tp', self.swap)  39.7 us
    psum x1, blocking collectives, on_device(): lax.psum(jnp.concatenate(natural).reshape(-1, 128), ('dp', 'tp'))  38.8 us
    pallas_call x2, Pallas kernels, self_bwd(): pl.pallas_call(self_bwd_kernel, grid_spec=pltpu.PrefetchScalarGridSpec(nu...  31.4 us
    unnamed x236, local copies, waits for them, and re-layouts  31.2 us
    ppermute x14, waiting for transfers between devices, across(): return lax.ppermute(x, 'dp', [(i, i ^ 1 << bit) for i in range(self.dp)])  26 us
  transfers between devices with their start and end apart: 24, of which 7 were waited for; matrix products, arithmetic and copies ran while one was open for 13% of the time, Pallas kernels for 5%

profile of v1, /device:TPU:1, one launch (start us, length us, event | category | flops | bytes accessed | tf_op | source)
XLA Modules:
  0.0 747.2 jit_solution(3013575592502304633)
XLA Ops:
  14.3 2.1 collective-permute-start
  22.0 1.9 constant_dynamic-slice_fusion.6
  31.1 2.6 copy.41
  35.1 1.9 constant_dynamic-slice_fusion.5
  38.2 2.0 copy.42
  40.3 12.0 %shard_map.316 = (bf16[16,128,768]{2,1,0:T(8,128)(2,1)}, bf16[16,128,768]{2,1,0:T(8,128)(2,1)}) custom-call(s32[16]{0:T(128)} %copy-done.88, s32[16]{0:T(128)} %copy-done.87, bf16[32,128,768]{2,1,0:T(8,128)(2,1)} %b_ref.1, bf16[32,128,768]{2,1,0:T(8,128)(2,1)} %b_ref.1), custom_call_target="tpu_custom_call" | custom-call | bytes 12582912 | tf_op jit(solution)/shard_map/pallas_call | solution.py:274
  56.5 3.7 add_convert_fusion.4.q_ref.k_ref.v_ref
  60.2 13.0 %shard_map.314 = (bf16[1024,384]{1,0:T(8,128)(2,1)}, f32[3,8,1024]{2,1,0:T(8,128)}) custom-call(s32[1]{0:T(128)} %bitcast.len_ref, bf16[1024,1152]{1,0:T(8,128)(2,1)} %add_convert_fusion.4.q_ref.k_ref.v_ref, bf16[1024,1152]{1,0:T(8,128)(2,1)} %add_convert_fusion.4.q_ref.k_ref.v_ref, bf16[1024,1152]{1,0:T(8,128)(2,1)} %add_convert_fusion.4.q_ref.k_ref.v_ref), custom_call_target="tpu_custom_call" | custom-call | flops 3221225472 | bytes 3145728 | tf_op jit(solution)/shard_map/pallas_call | solution.py:79
  73.2 2.2 constant_dynamic-update-slice_fusion.1
  82.2 4.7 collective-permute-start.6
  97.2 2.9 collective-permute-done.11
  101.4 2.1 collective-permute-start.12
  106.9 2.8 collective-permute-done.2
  110.0 1.8 collective-permute-start.3
  111.7 10.6 %collective-permute-done.18 = bf16[96,3072]{1,0:T(8,128)(2,1)S(1)} collective-permute-done((bf16[96,3072]{1,0:T(8,128)(2,1)}, bf16[96,3072]{1,0:T(8,128)(2,1)S(1)}, u32[]{:S(2)}, u32[]{:S(2)}) %collective-permute-start.18) | collective-permute-done | bytes 589856 | tf_op jit(solution)/shard_map/ppermute | solution.py:443
  123.8 1.8 collective-permute-start.19
  126.2 8.7 %collective-permute-done.21 = bf16[384,768]{1,0:T(8,128)(2,1)S(1)} collective-permute-done((bf16[384,768]{1,0:T(8,128)(2,1)S(1)}, bf16[384,768]{1,0:T(8,128)(2,1)S(1)}, u32[]{:S(2)}, u32[]{:S(2)}) %collective-permute-start.21) | collective-permute-done | bytes 589856 | tf_op jit(solution)/shard_map/ppermute | solution.py:443
  137.4 7.4 add_convert_fusion.1.own_ref
  145.8 3.6 add_convert_fusion.3.q_ref.k_ref.v_ref
  149.4 13.0 %shard_map.315 = (bf16[1024,384]{1,0:T(8,128)(2,1)}, f32[3,8,1024]{2,1,0:T(8,128)}) custom-call(s32[1]{0:T(128)} %bitcast.len_ref, bf16[1024,1152]{1,0:T(8,128)(2,1)} %add_convert_fusion.3.q_ref.k_ref.v_ref, bf16[1024,1152]{1,0:T(8,128)(2,1)} %add_convert_fusion.3.q_ref.k_ref.v_ref, bf16[1024,1152]{1,0:T(8,128)(2,1)} %add_convert_fusion.3.q_ref.k_ref.v_ref), custom_call_target="tpu_custom_call" | custom-call | flops 3221225472 | bytes 3145728 | tf_op jit(solution)/shard_map/pallas_call | solution.py:79
  162.4 2.1 constant_dynamic-update-slice_fusion
  164.5 3.1 fusion.83
  173.0 2.8 maximum_select_fusion.3
  175.8 2.2 maximum_select_fusion.2
  178.2 3.2 maximum_select_fusion.1.wout_ref
  181.4 4.1 maximum_select_fusion.win_ref
  185.4 9.4 %add_convert_fusion.oth_ref = bf16[2048,1536]{1,0:T(8,128)(2,1)} fusion(bf16[2048,768]{1,0:T(8,128)(2,1)} %bitcast.10, f32[1536]{0:T(1024)S(1)} %pad_maximum_fusion.16, bf16[768,384]{1,0:T(8,128)(2,1)S(1)} %copy-done.61, bf16[768,384]{1,0:T(8,128)(2,1)S(1)} %copy-done.53, bf16[768,384]{1,0:T(8,128)(2,1)S(1)} %copy-done.57, bf16[768,384]{1,0:T(8,128)(2,1)S(1)} %copy-done.49), kind=kOutput, calls=%fused_computation | convolution fusion | flops 4847566848 | bytes 11802624 | tf_op jit(solution)/shard_map/dot_general | solution.py:26
  194.8 17.8 %shard_map.317 = bf16[1024,768]{1,0:T(8,128)(2,1)} custom-call(bf16[1024,768]{1,0:T(8,128)(2,1)} %concatenate.310.q_ref, bf16[2048,1536]{1,0:T(8,128)(2,1)} %add_convert_fusion.1.own_ref, bf16[2048,1536]{1,0:T(8,128)(2,1)} %add_convert_fusion.oth_ref), custom_call_target="tpu_custom_call" | custom-call | flops 3221225472 | bytes 16000000 | tf_op jit(solution)/shard_map/pallas_call | solution.py:202
  214.3 3.9 fusion.84
  218.8 1.8 add_convert_fusion.5.h_ref
  220.6 53.9 %shard_map.318 = (bf16[1024,768]{1,0:T(8,128)(2,1)}, f32[1024,768]{1,0:T(8,128)}, bf16[4,768,768]{2,1,0:T(8,128)(2,1)}, bf16[3072,768]{1,0:T(8,128)(2,1)}, f32[8,3072]{1,0:T(8,128)}) custom-call(bf16[1024,768]{1,0:T(8,128)(2,1)} %add_convert_fusion.5.h_ref, bf16[1024,768]{1,0:T(8,128)(2,1)} %g_ref.1, f32[1024,768]{1,0:T(8,128)} %copy-done.2, ...), custom_call_target="tpu_custom_call" | custom-call | flops 28991029248 | bytes 18874368 | tf_op jit(solution)/shard_map/pallas_call | solution.py:377
  274.4 3.9 multiply_reduce_fusion
  279.1 2.7 fusion.70
  281.9 2.6 convolution_convert_fusion.2
  287.6 25.9 %shard_map.319 = (bf16[1024,768]{1,0:T(8,128)(2,1)}, bf16[2048,1536]{1,0:T(8,128)(2,1)}, bf16[2048,1536]{1,0:T(8,128)(2,1)}) custom-call(bf16[1024,768]{1,0:T(8,128)(2,1)} %concatenate.310.q_ref, bf16[2048,1536]{1,0:T(8,128)(2,1)} %add_convert_fusion.1.own_ref, bf16[2048,1536]{1,0:T(8,128)(2,1)} %add_convert_fusion.oth_ref, bf16[1024,768]{1,0:T(8,128)(2,1)} %concatenate.343.e_ref), custom_call_target="tpu_custom_call" | custom-call | flops 8053063680 | bytes 32000000 | tf_op jit(solution)/shard_map/pallas_call | solution.py:250
  315.3 2.5 convolution_convert_fusion.4
  318.3 2.3 multiply_reduce_fusion.1
  322.0 2.5 convolution_convert_fusion.3
  327.3 15.7 %shard_map.321 = bf16[3,1024,384]{2,1,0:T(8,128)(2,1)} custom-call(s32[1]{0:T(128)} %bitcast.len_ref, bf16[1024,1152]{1,0:T(8,128)(2,1)} %add_convert_fusion.3.q_ref.k_ref.v_ref, bf16[1024,1152]{1,0:T(8,128)(2,1)} %add_convert_fusion.3.q_ref.k_ref.v_ref, bf16[1024,1152]{1,0:T(8,128)(2,1)} %add_convert_fusion.3.q_ref.k_ref.v_ref, ...), custom_call_target="tpu_custom_call" | custom-call | flops 8053063680 | bytes 6291456 | tf_op jit(solution)/shard_map/pallas_call | solution.py:147
  344.6 3.1 convolution_convert_fusion.5
  347.7 1.9 convolution_convert_fusion.6
  349.5 1.8 convolution_convert_fusion.7
  352.5 15.7 %shard_map.320 = bf16[3,1024,384]{2,1,0:T(8,128)(2,1)} custom-call(s32[1]{0:T(128)} %bitcast.len_ref, bf16[1024,1152]{1,0:T(8,128)(2,1)} %add_convert_fusion.4.q_ref.k_ref.v_ref, bf16[1024,1152]{1,0:T(8,128)(2,1)} %add_convert_fusion.4.q_ref.k_ref.v_ref, bf16[1024,1152]{1,0:T(8,128)(2,1)} %add_convert_fusion.4.q_ref.k_ref.v_ref, ...), custom_call_target="tpu_custom_call" | custom-call | flops 8053063680 | bytes 6291456 | tf_op jit(solution)/shard_map/pallas_call | solution.py:147
  369.9 3.1 convolution_convert_fusion.8
  373.0 1.8 convolution_convert_fusion.9
  374.8 1.8 convolution_convert_fusion.10
  380.2 2.2 fusion.16
  382.5 4.7 fusion.12
  387.3 38.8 %psum.7 = f32[102,128]{1,0:T(8,128)S(1)} all-reduce(f32[102,128]{1,0:T(8,128)S(1)} %bitcast.116), channel_id=1, replica_groups=mesh['dp'=16,'tp'=2] {'dp','tp'}, use_global_device_ids=true, to_apply=%region_28.29 | all-reduce | flops 13056 | bytes 104448 | tf_op jit(solution)/shard_map/psum | solution.py:827
  426.2 9.8 %fusion.85 = f32[768,1536]{1,0:T(8,128)} fusion(bf16[2048,768]{1,0:T(8,128)(2,1)} %bitcast.120, bf16[2048,1536]{1,0:T(8,128)(2,1)} %get-tuple-element.45), kind=kOutput, calls=%fused_computation.255 | convolution fusion | flops 4831838208 | bytes 14155776 | tf_op jit(solution)/shard_map/dot_general | solution.py:26
  435.9 9.3 %convolution_convert_fusion = bf16[2048,768]{1,0:T(8,128)(2,1)} fusion(bf16[2048,1536]{1,0:T(8,128)(2,1)} %get-tuple-element.46, bf16[768,384]{1,0:T(8,128)(2,1)S(1)} %copy-done.62, bf16[768,384]{1,0:T(8,128)(2,1)S(1)} %copy-done.54, bf16[768,384]{1,0:T(8,128)(2,1)S(1)} %copy-done.58, bf16[768,384]{1,0:T(8,128)(2,1)S(1)} %copy-done.50), kind=kOutput, calls=%fused_computation.20 | convolution fusion | flops 4842848256 | bytes 11796480 | tf_op jit(solution)/shard_map/dot_general | solution.py:26
  445.3 8.9 %add_convert_fusion.2 = bf16[768,1536]{1,0:T(8,128)(2,1)S(1)} fusion(f32[768,1536]{1,0:T(8,128)} %fusion.85, bf16[2048,768]{1,0:T(8,128)(2,1)} %bitcast.10, bf16[2048,1536]{1,0:T(8,128)(2,1)} %get-tuple-element.46), kind=kOutput, calls=%fused_computation.9 | convolution fusion | flops 4834197504 | bytes 16515072 | tf_op jit(solution)/shard_map/dot_general | solution.py:26
  464.8 2.6 constant_dynamic-slice_fusion.1
  467.4 2.5 constant_dynamic-slice_fusion.3
  469.9 182.3 %shard_map.323 = (bf16[1536,768]{1,0:T(8,128)(2,1)}, bf16[1536,768]{1,0:T(8,128)(2,1)}, bf16[2304,384]{1,0:T(8,128)(2,1)}, bf16[1536,384]{1,0:T(8,128)(2,1)}, bf16[2304,384]{1,0:T(8,128)(2,1)}) custom-call(bf16[1536,768]{1,0:T(8,128)(2,1)} %bitcast.98, bf16[1536,768]{1,0:T(8,128)(2,1)} %bitcast.97, bf16[1536,768]{1,0:T(8,128)(2,1)} %get-tuple-element.139.refs_2_, ...), custom_call_target="tpu_custom_call" | custom-call | bytes 18874368 | tf_op jit(solution)/shard_map/pallas_call | solution.py:641
  652.2 1.8 slice_bitcast_fusion.10
  660.5 2.1 maximum_convert_fusion.1
  663.9 3.2 copy.44
  667.2 2.5 convert_element_type.195
  671.6 3.0 maximum_convert_fusion
  676.1 2.4 fusion.11
  680.2 6.9 fusion.69
  687.1 38.7 %collective-permute-done.23.b_ref = bf16[16,128,768]{2,1,0:T(8,128)(2,1)} collective-permute-done((bf16[16,128,768]{2,1,0:T(8,128)(2,1)S(1)}, bf16[16,128,768]{2,1,0:T(8,128)(2,1)}, u32[]{:S(2)}, u32[]{:S(2)}) %collective-permute-start.23) | collective-permute-done | bytes 3145760 | tf_op jit(solution)/shard_map/ppermute | solution.py:440
  725.8 21.1 %shard_map.322 = f32[32,128,768]{2,1,0:T(8,128)} custom-call(s32[32]{0:T(128)} %pad_add_fusion.order_ref, f32[16,128,768]{2,1,0:T(8,128)} %bitcast.99, bf16[16,128,768]{2,1,0:T(8,128)(2,1)} %collective-permute-done.23.b_ref), custom_call_target="tpu_custom_call" | custom-call | bytes 12582912 | tf_op jit(solution)/shard_map/pallas_call | solution.py:307
  (392 shorter events, 109.8 us)
Async XLA Ops:
  0.7 51.7 %copy-start = (s32[1,2]{1,0:T(1,128)S(1)}, s32[1,2]{1,0:T(1,128)}, u32[]{:S(2)}) copy-start(s32[1,2]{1,0:T(1,128)} %param.22) | copy-start | bytes 28
  0.7 26.1 %copy-start.29 = (bf16[768,2,384]{2,1,0:T(2,128)(2,1)S(1)}, bf16[768,2,384]{2,1,0:T(2,128)(2,1)}, u32[]{:S(2)}) copy-start(bf16[768,2,384]{2,1,0:T(2,128)(2,1)} %param.27) | copy-start | bytes 3538948
  14.3 38.7 %collective-permute-start = (bf16[51,128]{1,0:T(8,128)(2,1)}, bf16[51,128]{1,0:T(8,128)(2,1)S(1)}, u32[]{:S(2)}, u32[]{:S(2)}) collective-permute-start(bf16[51,128]{1,0:T(8,128)(2,1)} %bitcast.1), channel_id=1, source_target_pairs={{0,1},{1,0},{2,3},{3,2},{4,5},{5,4},{6,7},{7,6},{8,9},{9,8},{10,11... | collective-permute-start | bytes 39176 | tf_op jit(solution)/shard_map/ppermute | solution.py:440
  17.3 59.8 %collective-permute-start.14 = (bf16[96,768]{1,0:T(8,128)(2,1)S(1)}, bf16[96,768]{1,0:T(8,128)(2,1)}, u32[]{:S(2)}, u32[]{:S(2)}) collective-permute-start(bf16[96,768]{1,0:T(8,128)(2,1)S(1)} %constant_dynamic-slice_fusion.7), channel_id=1, source_target_pairs={{0,1},{1,0},{2,3},{3,2},{4,5},{5,4},{6,7},{7,6},{8,9},{9,8},{10,11... | collective-permute-start | bytes 442376 | tf_op jit(solution)/shard_map/ppermute | solution.py:440
  19.0 58.0 %collective-permute-start.7 = (bf16[192,384]{1,0:T(8,128)(2,1)}, bf16[192,384]{1,0:T(8,128)(2,1)}, u32[]{:S(2)}, u32[]{:S(2)}) collective-permute-start(bf16[192,384]{1,0:T(8,128)(2,1)} %constant_dynamic-slice_fusion.11), channel_id=1, source_target_pairs={{0,1},{1,0},{2,3},{3,2},{4,5},{5,4},{6,7},{7,6},{8,9},{9,8},{10,11... | collective-permute-start | bytes 442376 | tf_op jit(solution)/shard_map/ppermute | solution.py:440
  22.0 53.5 %collective-permute-start.4 = (bf16[96,768]{1,0:T(8,128)(2,1)}, bf16[96,768]{1,0:T(8,128)(2,1)}, u32[]{:S(2)}, u32[]{:S(2)}) collective-permute-start(bf16[96,768]{1,0:T(8,128)(2,1)} %constant_dynamic-slice_fusion.12), channel_id=1, source_target_pairs={{0,1},{1,0},{2,3},{3,2},{4,5},{5,4},{6,7},{7,6},{8,9},{9,8},{10,11... | collective-permute-start | bytes 442376 | tf_op jit(solution)/shard_map/ppermute | solution.py:440
  23.9 71.0 %collective-permute-start.17 = (bf16[96,3072]{1,0:T(8,128)(2,1)}, bf16[96,3072]{1,0:T(8,128)(2,1)}, u32[]{:S(2)}, u32[]{:S(2)}) collective-permute-start(bf16[96,3072]{1,0:T(8,128)(2,1)} %constant_dynamic-slice_fusion.6), channel_id=1, source_target_pairs={{0,1},{1,0},{2,3},{3,2},{4,5},{5,4},{6,7},{7,6},{8,9},{9,8},{10,11... | collective-permute-start | bytes 1769480 | tf_op jit(solution)/shard_map/ppermute | solution.py:440
  30.4 24.6 %copy-start.66 = (f32[1024]{0:T(1024)}, f32[1024]{0:T(1024)S(1)}, u32[]{:S(2)}) copy-start(f32[1024]{0:T(1024)S(1)} %broadcast_multiply_fusion.8) | copy-start | bytes 12292
  31.0 23.9 %copy-start.68 = (f32[1024]{0:T(1024)}, f32[1024]{0:T(1024)S(1)}, u32[]{:S(2)}) copy-start(f32[1024]{0:T(1024)S(1)} %add_rsqrt_fusion.2) | copy-start | bytes 12292
  31.1 6.0 copy-start.89
  31.1 6.6 copy-start.86
  31.1 7.1 copy-start.77
  33.7 22.7 %copy-start.16 = (bf16[768,3,384]{0,2,1:T(8,128)(2,1)}, bf16[768,3,384]{0,2,1:T(8,128)(2,1)S(1)}, u32[]{:S(2)}) copy-start(bf16[768,3,384]{0,2,1:T(8,128)(2,1)S(1)} %copy.41) | copy-start | bytes 5308420
  40.3 12.8 %copy-start.78 = (bf16[3,384]{1,0:T(4,128)(2,1)S(1)}, bf16[3,384]{1,0:T(4,128)(2,1)}, u32[]{:S(2)}) copy-start(bf16[3,384]{1,0:T(4,128)(2,1)} %param.31) | copy-start | bytes 6916
  40.3 12.8 %copy-start.79 = (bf16[3,384]{1,0:T(4,128)(2,1)S(1)}, bf16[3,384]{1,0:T(4,128)(2,1)}, u32[]{:S(2)}) copy-start(bf16[3,384]{1,0:T(4,128)(2,1)} %param.32) | copy-start | bytes 6916
  53.0 36.4 %collective-permute-start.10 = (bf16[192,768]{1,0:T(8,128)(2,1)}, bf16[192,768]{1,0:T(8,128)(2,1)}, u32[]{:S(2)}, u32[]{:S(2)}) collective-permute-start(bf16[192,768]{1,0:T(8,128)(2,1)} %constant_dynamic-slice_fusion.8), channel_id=1, source_target_pairs={{0,1},{1,0},{2,3},{3,2},{4,5},{5,4},{6,7},{7,6},{8,9},{9,8},{10,11... | collective-permute-start | bytes 884744 | tf_op jit(solution)/shard_map/ppermute | solution.py:440
  53.1 7.0 copy-start.70
  55.6 4.5 copy-start.22
  60.1 15.3 %copy-start.81 = (bf16[6,128]{1,0:T(8,128)(2,1)S(1)}, bf16[6,128]{1,0:T(8,128)(2,1)}, u32[]{:S(2)}) copy-start(bf16[6,128]{1,0:T(8,128)(2,1)} %get-tuple-element.188) | copy-start | bytes 4612
  60.1 15.3 %copy-start.84 = (bf16[2,384]{1,0:T(2,128)(2,1)S(1)}, bf16[2,384]{1,0:T(2,128)(2,1)}, u32[]{:S(2)}) copy-start(bf16[2,384]{1,0:T(2,128)(2,1)} %param.30) | copy-start | bytes 4612
  60.1 17.0 %copy-start.80 = (f32[384]{0:T(512)S(1)}, f32[384]{0:T(512)}, u32[]{:S(2)}) copy-start(f32[384]{0:T(512)} %get-tuple-element.130) | copy-start | bytes 4612
  60.1 17.0 %copy-start.83 = (f32[384]{0:T(512)S(1)}, f32[384]{0:T(512)}, u32[]{:S(2)}) copy-start(f32[384]{0:T(512)} %get-tuple-element.196) | copy-start | bytes 4612
  60.2 17.0 %copy-start.64 = (bf16[192,1152]{1,0:T(8,128)(2,1)S(1)}, bf16[192,1152]{1,0:T(8,128)(2,1)}, u32[]{:S(2)}) copy-start(bf16[192,1152]{1,0:T(8,128)(2,1)} %copy.42) | copy-start | bytes 1327108
  73.2 16.2 %copy-start.82 = (f32[384]{0:T(512)S(1)}, f32[384]{0:T(512)}, u32[]{:S(2)}) copy-start(f32[384]{0:T(512)} %get-tuple-element.197) | copy-start | bytes 4612
  73.2 16.2 %copy-start.43 = (bf16[384,768]{1,0:T(8,128)(2,1)S(1)}, bf16[384,768]{1,0:T(8,128)(2,1)}, u32[]{:S(2)}) copy-start(bf16[384,768]{1,0:T(8,128)(2,1)} %constant_dynamic-slice_fusion.5) | copy-start | bytes 1769476
  73.2 17.8 %copy-start.85 = (bf16[1,384]{1,0:T(2,128)(2,1)S(1)}, bf16[1,384]{1,0:T(2,128)(2,1)}, u32[]{:S(2)}) copy-start(bf16[1,384]{1,0:T(2,128)(2,1)} %concatenate.339) | copy-start | bytes 2308
  75.5 4.3 collective-permute-start.5
  77.0 5.2 collective-permute-start.8
  77.1 14.4 %collective-permute-start.1 = (bf16[192,1152]{1,0:T(8,128)(2,1)S(1)}, bf16[192,1152]{1,0:T(8,128)(2,1)S(1)}, u32[]{:S(2)}, u32[]{:S(2)}) collective-permute-start(bf16[192,1152]{1,0:T(8,128)(2,1)S(1)} %copy-done.64), channel_id=1, source_target_pairs={{0,1},{1,0},{2,3},{3,2},{4,5},{5,4},{6,7},{7,6},{8,9},{9,8},{10,11... | collective-permute-start | bytes 1327112 | tf_op jit(solution)/shard_map/ppermute | solution.py:440
  79.7 8.2 %collective-permute-start.15 = (bf16[96,768]{1,0:T(8,128)(2,1)}, bf16[96,768]{1,0:T(8,128)(2,1)S(1)}, u32[]{:S(2)}, u32[]{:S(2)}) collective-permute-start(bf16[96,768]{1,0:T(8,128)(2,1)} %collective-permute-done.14), channel_id=1, source_target_pairs={{0,4},{2,6},{4,0},{6,2},{8,12},{10,14},{12,8},{14,10},{16,20},{18,... | collective-permute-start | bytes 442376 | tf_op jit(solution)/shard_map/ppermute | solution.py:443
  82.2 11.6 %collective-permute-start.6 = (bf16[192,768]{1,0:T(8,128)(2,1)S(1)}, bf16[192,768]{1,0:T(8,128)(2,1)S(1)}, u32[]{:S(2)}, u32[]{:S(2)}) collective-permute-start(bf16[192,768]{1,0:T(8,128)(2,1)S(1)} %maximum_select_fusion.15), channel_id=1, source_target_pairs={{0,2},{2,0},{4,6},{6,4},{8,10},{10,8},{12,14},{14,12},{16,18},{18,... | collective-permute-start | bytes 884744 | tf_op jit(solution)/shard_map/ppermute | solution.py:443
  88.0 6.5 collective-permute-start.9
  89.4 15.0 %collective-permute-start.20 = (bf16[384,768]{1,0:T(8,128)(2,1)S(1)}, bf16[384,768]{1,0:T(8,128)(2,1)S(1)}, u32[]{:S(2)}, u32[]{:S(2)}) collective-permute-start(bf16[384,768]{1,0:T(8,128)(2,1)S(1)} %copy-done.43), channel_id=1, source_target_pairs={{0,1},{1,0},{2,3},{3,2},{4,5},{5,4},{6,7},{7,6},{8,9},{9,8},{10,11... | collective-permute-start | bytes 1769480 | tf_op jit(solution)/shard_map/ppermute | solution.py:440
  91.5 8.5 %collective-permute-start.11 = (bf16[192,768]{1,0:T(8,128)(2,1)}, bf16[192,768]{1,0:T(8,128)(2,1)S(1)}, u32[]{:S(2)}, u32[]{:S(2)}) collective-permute-start(bf16[192,768]{1,0:T(8,128)(2,1)} %collective-permute-done.10), channel_id=1, source_target_pairs={{0,4},{2,6},{4,0},{6,2},{8,12},{10,14},{12,8},{14,10},{16,20},{18,... | collective-permute-start | bytes 884744 | tf_op jit(solution)/shard_map/ppermute | solution.py:443
  93.8 7.6 %collective-permute-start.16 = (bf16[192,768]{1,0:T(8,128)(2,1)S(1)}, bf16[192,768]{1,0:T(8,128)(2,1)S(1)}, u32[]{:S(2)}, u32[]{:S(2)}) collective-permute-start(bf16[192,768]{1,0:T(8,128)(2,1)S(1)} %maximum_select_fusion.17), channel_id=1, source_target_pairs={{0,2},{2,0},{4,6},{6,4},{8,10},{10,8},{12,14},{14,12},{16,18},{18,... | collective-permute-start | bytes 884744 | tf_op jit(solution)/shard_map/ppermute | solution.py:443
  94.4 15.2 %collective-permute-start.2 = (bf16[192,1152]{1,0:T(8,128)(2,1)S(1)}, bf16[192,1152]{1,0:T(8,128)(2,1)S(1)}, u32[]{:S(2)}, u32[]{:S(2)}) collective-permute-start(bf16[192,1152]{1,0:T(8,128)(2,1)S(1)} %collective-permute-done.1), channel_id=1, source_target_pairs={{0,4},{2,6},{4,0},{6,2},{8,12},{10,14},{12,8},{14,10},{16,20},{18,... | collective-permute-start | bytes 1327112 | tf_op jit(solution)/shard_map/ppermute | solution.py:443
  94.9 27.4 %collective-permute-start.18 = (bf16[96,3072]{1,0:T(8,128)(2,1)}, bf16[96,3072]{1,0:T(8,128)(2,1)S(1)}, u32[]{:S(2)}, u32[]{:S(2)}) collective-permute-start(bf16[96,3072]{1,0:T(8,128)(2,1)} %collective-permute-done.17), channel_id=1, source_target_pairs={{0,4},{2,6},{4,0},{6,2},{8,12},{10,14},{12,8},{14,10},{16,20},{18,... | collective-permute-start | bytes 1769480 | tf_op jit(solution)/shard_map/ppermute | solution.py:443
  100.1 85.3 %collective-permute-start.13 = (bf16[16,128,768]{2,1,0:T(8,128)(2,1)}, bf16[16,128,768]{2,1,0:T(8,128)(2,1)}, u32[]{:S(2)}, u32[]{:S(2)}) collective-permute-start(bf16[16,128,768]{2,1,0:T(8,128)(2,1)} %get-tuple-element.39), channel_id=1, source_target_pairs={{0,1},{1,0},{2,3},{3,2},{4,5},{5,4},{6,7},{7,6},{8,9},{9,8},{10,11... | collective-permute-start | bytes 9437192 | tf_op jit(solution)/shard_map/ppermute | solution.py:440
  101.4 24.2 %collective-permute-start.12 = (bf16[384,768]{1,0:T(8,128)(2,1)S(1)}, bf16[384,768]{1,0:T(8,128)(2,1)S(1)}, u32[]{:S(2)}, u32[]{:S(2)}) collective-permute-start(bf16[384,768]{1,0:T(8,128)(2,1)S(1)} %maximum_select_fusion.11), channel_id=1, source_target_pairs={{0,2},{2,0},{4,6},{6,4},{8,10},{10,8},{12,14},{14,12},{16,18},{18,... | collective-permute-start | bytes 1769480 | tf_op jit(solution)/shard_map/ppermute | solution.py:443
  104.5 30.5 %collective-permute-start.21 = (bf16[384,768]{1,0:T(8,128)(2,1)S(1)}, bf16[384,768]{1,0:T(8,128)(2,1)S(1)}, u32[]{:S(2)}, u32[]{:S(2)}) collective-permute-start(bf16[384,768]{1,0:T(8,128)(2,1)S(1)} %collective-permute-done.20), channel_id=1, source_target_pairs={{0,4},{2,6},{4,0},{6,2},{8,12},{10,14},{12,8},{14,10},{16,20},{18,... | collective-permute-start | bytes 1769480 | tf_op jit(solution)/shard_map/ppermute | solution.py:443
  109.9 34.9 %copy-start.34 = (bf16[384,1152]{1,0:T(8,128)(2,1)}, bf16[384,1152]{1,0:T(8,128)(2,1)S(1)}, u32[]{:S(2)}) copy-start(bf16[384,1152]{1,0:T(8,128)(2,1)S(1)} %maximum_select_fusion.8) | copy-start | bytes 2654212
  110.0 34.9 %collective-permute-start.3 = (bf16[384,1152]{1,0:T(8,128)(2,1)S(1)}, bf16[384,1152]{1,0:T(8,128)(2,1)S(1)}, u32[]{:S(2)}, u32[]{:S(2)}) collective-permute-start(bf16[384,1152]{1,0:T(8,128)(2,1)S(1)} %maximum_select_fusion.8), channel_id=1, source_target_pairs={{0,2},{2,0},{4,6},{6,4},{8,10},{10,8},{12,14},{14,12},{16,18},{18,... | collective-permute-start | bytes 2654216 | tf_op jit(solution)/shard_map/ppermute | solution.py:443
  123.8 52.0 %collective-permute-start.19 = (bf16[192,3072]{1,0:T(8,128)(2,1)S(1)}, bf16[192,3072]{1,0:T(8,128)(2,1)}, u32[]{:S(2)}, u32[]{:S(2)}) collective-permute-start(bf16[192,3072]{1,0:T(8,128)(2,1)S(1)} %maximum_select_fusion.6), channel_id=1, source_target_pairs={{0,2},{2,0},{4,6},{6,4},{8,10},{10,8},{12,14},{14,12},{16,18},{18,... | collective-permute-start | bytes 3538952 | tf_op jit(solution)/shard_map/ppermute | solution.py:443
  126.0 11.4 %copy-start.48 = (bf16[768,384]{1,0:T(8,128)(2,1)S(1)}, bf16[768,384]{1,0:T(8,128)(2,1)}, u32[]{:S(2)}) copy-start(bf16[768,384]{1,0:T(8,128)(2,1)} %get-tuple-element.178) | copy-start | bytes 1769476
  126.1 11.4 %copy-start.52 = (bf16[768,384]{1,0:T(8,128)(2,1)S(1)}, bf16[768,384]{1,0:T(8,128)(2,1)}, u32[]{:S(2)}) copy-start(bf16[768,384]{1,0:T(8,128)(2,1)} %get-tuple-element.179) | copy-start | bytes 1769476
  126.1 11.3 %copy-start.90 = (bf16[16,128,768]{2,1,0:T(8,128)(2,1)S(1)}, bf16[16,128,768]{2,1,0:T(8,128)(2,1)}, u32[]{:S(2)}) copy-start(bf16[16,128,768]{2,1,0:T(8,128)(2,1)} %get-tuple-element.38) | copy-start | bytes 9437188
  126.2 18.7 %copy-start.56 = (bf16[768,384]{1,0:T(8,128)(2,1)}, bf16[768,384]{1,0:T(8,128)(2,1)S(1)}, u32[]{:S(2)}) copy-start(bf16[768,384]{1,0:T(8,128)(2,1)S(1)} %get-tuple-element.180) | copy-start | bytes 1769476
  126.2 18.7 %copy-start.60 = (bf16[768,384]{1,0:T(8,128)(2,1)}, bf16[768,384]{1,0:T(8,128)(2,1)S(1)}, u32[]{:S(2)}) copy-start(bf16[768,384]{1,0:T(8,128)(2,1)S(1)} %get-tuple-element.181) | copy-start | bytes 1769476
  136.4 36.6 %collective-permute-start.22 = (bf16[768,768]{1,0:T(8,128)(2,1)}, bf16[768,768]{1,0:T(8,128)(2,1)}, u32[]{:S(2)}, u32[]{:S(2)}) collective-permute-start(bf16[768,768]{1,0:T(8,128)(2,1)} %maximum_select_fusion.7), channel_id=1, source_target_pairs={{0,2},{2,0},{4,6},{6,4},{8,10},{10,8},{12,14},{14,12},{16,18},{18,... | collective-permute-start | bytes 3538952 | tf_op jit(solution)/shard_map/ppermute | solution.py:443
  137.4 8.4 %copy-start.23 = (bf16[1024,768]{1,0:T(8,128)(2,1)S(1)}, bf16[1024,768]{1,0:T(8,128)(2,1)}, u32[]{:S(2)}) copy-start(bf16[1024,768]{1,0:T(8,128)(2,1)} %copy-done.22) | copy-start | bytes 4718596
  274.4 4.7 copy-start.10
  327.3 17.3 %copy-start.24 = (bf16[1024,768]{1,0:T(8,128)(2,1)S(1)}, bf16[1024,768]{1,0:T(8,128)(2,1)}, u32[]{:S(2)}) copy-start(bf16[1024,768]{1,0:T(8,128)(2,1)} %copy-done.22) | copy-start | bytes 4718596
  373.0 5.1 slice-start.4
  426.1 9.8 %copy-start.50 = (bf16[768,384]{1,0:T(8,128)(2,1)S(1)}, bf16[768,384]{1,0:T(8,128)(2,1)}, u32[]{:S(2)}) copy-start(bf16[768,384]{1,0:T(8,128)(2,1)} %get-tuple-element.178) | copy-start | bytes 1769476
  426.1 9.8 %copy-start.54 = (bf16[768,384]{1,0:T(8,128)(2,1)S(1)}, bf16[768,384]{1,0:T(8,128)(2,1)}, u32[]{:S(2)}) copy-start(bf16[768,384]{1,0:T(8,128)(2,1)} %get-tuple-element.179) | copy-start | bytes 1769476
  426.1 9.8 %copy-start.58 = (bf16[768,384]{1,0:T(8,128)(2,1)S(1)}, bf16[768,384]{1,0:T(8,128)(2,1)}, u32[]{:S(2)}) copy-start(bf16[768,384]{1,0:T(8,128)(2,1)} %copy-done.56) | copy-start | bytes 1769476
  426.1 9.8 %copy-start.62 = (bf16[768,384]{1,0:T(8,128)(2,1)S(1)}, bf16[768,384]{1,0:T(8,128)(2,1)}, u32[]{:S(2)}) copy-start(bf16[768,384]{1,0:T(8,128)(2,1)} %copy-done.60) | copy-start | bytes 1769476
  456.4 5.5 copy-start.39
  457.6 7.2 slice-start.2
  461.9 5.4 slice-start
  656.1 69.7 %collective-permute-start.23 = (bf16[16,128,768]{2,1,0:T(8,128)(2,1)S(1)}, bf16[16,128,768]{2,1,0:T(8,128)(2,1)}, u32[]{:S(2)}, u32[]{:S(2)}) collective-permute-start(bf16[16,128,768]{2,1,0:T(8,128)(2,1)S(1)} %bitcast.122), channel_id=1, source_target_pairs={{0,1},{1,0},{2,3},{3,2},{4,5},{5,4},{6,7},{7,6},{8,9},{9,8},{10,11... | collective-permute-start | bytes 9437192 | tf_op jit(solution)/shard_map/ppermute | solution.py:440
  671.6 4.5 copy-start.18
  671.6 6.9 slice-start.6
  725.8 21.1 %copy-start.1 = (s32[1,2]{1,0:T(1,128)S(1)}, s32[1,2]{1,0:T(1,128)}, u32[]{:S(2)}) copy-start(s32[1,2]{1,0:T(1,128)} %param.22) | copy-start | bytes 28
  (64 other events, 174.2 us)

commit v2 on v1

v2 whole, which is shorter than its diff:
```python
import functools

import jax
import jax.numpy as jnp
from jax import lax
from jax.experimental import pallas as pl
from jax.experimental.pallas import tpu as pltpu
from jax.sharding import PartitionSpec as P

HEAD = 64
SPAN = 64
LEN = 1024
NBR = 256
EPS = 1e-05
BF = jnp.bfloat16
F32 = jnp.float32
DEAD = -1e30
LN2 = 0.6931471805599453
SCORE = 0.125 / LN2
VMEM_LIMIT = 60 * 1024 * 1024

NN = (((1,), (0,)), ((), ()))
NT = (((1,), (1,)), ((), ()))
TN = (((0,), (0,)), ((), ()))


def mm(a, b, dims=NN):
    return lax.dot_general(a, b, dims, preferred_element_type=F32)


def iota(shape, dim):
    return lax.broadcasted_iota(jnp.int32, shape, dim)


def cost(flops, nbytes, exps=0):
    return pl.CostEstimate(flops=flops, bytes_accessed=nbytes, transcendentals=exps)


def params(n=1):
    return pltpu.CompilerParams(
        dimension_semantics=("arbitrary",) * n, vmem_limit_bytes=VMEM_LIMIT
    )


def three(x):
    hi = x.astype(BF)
    rest = x - hi.astype(F32)
    mid = rest.astype(BF)
    return hi.astype(F32), mid.astype(F32), rest - mid.astype(F32)


def self_fwd_kernel(len_ref, q_ref, k_ref, v_ref, o_ref, lse_ref):
    bq = 512
    length = len_ref[0]
    low = iota((LEN, 128), 1) < HEAD
    lane = iota((LEN, 128), 1)
    q, k, v = (ref[...] for ref in (q_ref, k_ref, v_ref))
    one = jnp.ones((LEN, 128), BF)
    zero = jnp.zeros((LEN, 128), BF)
    dead = jnp.where(iota((LEN, 128), 0) < length, 0.0, DEAD).astype(BF)
    at = lambda x, first: jnp.where(lane == first, x, zero)
    qs = (jnp.where(low, q, at(one, HEAD)), jnp.where(low, at(one, 0), q))
    ks = (jnp.where(low, k, at(dead, HEAD)), jnp.where(low, at(dead, 0), k))
    vs = (jnp.where(low, v, one), jnp.where(low, one, v))
    tri = iota((bq, bq), 1) <= iota((bq, bq), 0)
    low_q = low[:bq]
    for i in range(LEN // bq):
        lo, hi = i * bq, (i + 1) * bq
        outs, tops = [], []
        for h in range(2):
            here = jnp.where(tri, mm(qs[h][lo:hi], ks[h][lo:hi], NT), DEAD)
            m = jnp.max(here, axis=1, keepdims=True)
            if i:
                left = mm(qs[h][lo:hi], ks[h][:lo], NT)
                m = jnp.maximum(m, jnp.max(left, axis=1, keepdims=True))
            o = mm(jnp.exp2(here - m).astype(BF), vs[h][lo:hi])
            if i:
                o += mm(jnp.exp2(left - m).astype(BF), vs[h][:lo])
            outs.append(o)
            tops.append(m)
        a, b = outs
        o_ref[lo:hi, :] = (jnp.where(low_q, a, b) / pltpu.roll(jnp.where(low_q, b, a), HEAD, 1)).astype(BF)
        lse_ref[lo:hi, :] = jnp.where(low_q, tops[1], tops[0]) + jnp.log2(jnp.where(low_q, b, a))


def self_fwd(qkv, length):
    pairs = qkv.shape[1] // 3 // 128
    block = lambda part: pl.BlockSpec((LEN, 128), lambda i, n: (0, part * pairs + i))
    return pl.pallas_call(
        self_fwd_kernel,
        grid_spec=pltpu.PrefetchScalarGridSpec(
            num_scalar_prefetch=1,
            grid=(pairs,),
            in_specs=[block(0), block(1), block(2)],
            out_specs=[block(0), block(0)],
        ),
        out_shape=[
            jax.ShapeDtypeStruct((LEN, pairs * 128), BF),
            jax.ShapeDtypeStruct((LEN, pairs * 128), F32),
        ],
        compiler_params=params(),
        cost_estimate=cost(pairs * 2 * 4 * LEN * LEN * 128, pairs * 8 * LEN * 128),
    )(length, qkv, qkv, qkv)


def self_bwd_kernel(len_ref, q_ref, k_ref, v_ref, f_ref, o_ref, lse_ref, d_ref, dq_ref):
    bk = 256
    length = len_ref[0]
    lane = iota((LEN, 128), 1)
    low = lane < HEAD
    q, k, v, f = (ref[...] for ref in (q_ref, k_ref, v_ref, f_ref))
    zero = jnp.zeros((LEN, 128), BF)
    place = lax.rem(lane, HEAD)
    prod = f.astype(F32) * o_ref[...].astype(F32)
    crossed = jnp.where((iota((128, 128), 0) < HEAD) == (iota((128, 128), 1) < HEAD), 0.0, 1.0).astype(BF)
    prod_hi = prod.astype(BF)
    delta = mm(prod_hi, crossed) + mm((prod - prod_hi.astype(F32)).astype(BF), crossed)

    def free(x, last):
        hi, mid, rest = three(-x)
        out = jnp.where(place == 0, hi, jnp.where(place == 1, mid, jnp.where(place == 2, rest, last)))
        return out.astype(BF)

    q_free = free(lse_ref[...], jnp.where(place == 3, 1.0, 0.0))
    f_free = free(delta, jnp.zeros((LEN, 128), F32))
    dead = jnp.where(iota((LEN, 128), 0) < length, 0.0, DEAD)
    ones = jnp.where(place < 3, 1.0, 0.0)
    k_free = jnp.where(place == 3, dead, ones).astype(BF)
    v_free = ones.astype(BF)
    pick = lambda x, y: (jnp.where(low, x, y), jnp.where(low, y, x))
    qx, fx, kx, vx = pick(q, q_free), pick(f, f_free), pick(k, k_free), pick(v, v_free)
    qs, fs, ks = pick(q, zero), pick(f, zero), pick(k, zero)
    tri = iota((bk, bk), 0) <= iota((bk, bk), 1)
    for j in range(LEN // bk):
        lo, hi = j * bk, (j + 1) * bk
        ps, dss = [], []
        for h in range(2):
            p = jnp.exp2(mm(kx[h][lo:hi], qx[h][lo:], NT))
            first = jnp.where(tri, p[:, :bk], 0.0)
            p = jnp.concatenate([first, p[:, bk:]], axis=1) if hi < LEN else first
            ds = (p * mm(vx[h][lo:hi], fx[h][lo:], NT)).astype(BF)
            ps.append(p.astype(BF))
            dss.append(ds)
        dv = mm(jnp.concatenate(ps, axis=1), jnp.concatenate([fs[0][lo:], fs[1][lo:]], axis=0))
        dk = mm(jnp.concatenate(dss, axis=1), jnp.concatenate([qs[0][lo:], qs[1][lo:]], axis=0))
        kk = jnp.concatenate([ks[0][lo:hi], ks[1][lo:hi]], axis=0)
        part = mm(jnp.concatenate(dss, axis=0), kk, TN)
        if j:
            dq_ref[lo:, :] += part
        else:
            dq_ref[...] = part
        d_ref[1, lo:hi, :] = (dk * LN2).astype(BF)
        d_ref[2, lo:hi, :] = dv.astype(BF)
    d_ref[0] = (dq_ref[...] * 0.125).astype(BF)


def self_bwd(qkv, back, ctx, lse, length):
    pairs = qkv.shape[1] // 3 // 128
    block = lambda part: pl.BlockSpec((LEN, 128), lambda i, n: (0, part * pairs + i))
    return pl.pallas_call(
        self_bwd_kernel,
        grid_spec=pltpu.PrefetchScalarGridSpec(
            num_scalar_prefetch=1,
            grid=(pairs,),
            in_specs=[block(0), block(1), block(2), block(0), block(0), block(0)],
            out_specs=pl.BlockSpec((3, LEN, 128), lambda i, n: (0, 0, i)),
            scratch_shapes=[pltpu.VMEM((LEN, 128), F32)],
        ),
        out_shape=jax.ShapeDtypeStruct((3, LEN, pairs * 128), BF),
        compiler_params=params(),
        cost_estimate=cost(pairs * 2 * 10 * LEN * LEN * 128, pairs * 16 * LEN * 128),
    )(length, qkv, qkv, qkv, back, ctx, lse)


PER_STEP = 4


def own_heads():
    return jnp.where(iota((256, 256), 0) // SPAN == iota((256, 256), 1) // HEAD, 1.0, 0.0).astype(BF)


def spread(rows, mask):
    return jnp.concatenate([rows] * 4, axis=0) * mask


def gathered(rows, lanes):
    out = jnp.where(lanes == 0, rows[:SPAN], 0.0)
    for g in range(1, 4):
        out = jnp.where(lanes == g, rows[g * SPAN : (g + 1) * SPAN], out)
    return out


def fours(count, width, rows):
    for u in range(count):
        for t in range(width // 256):
            yield slice(u * SPAN, (u + 1) * SPAN), slice(u * rows, (u + 1) * rows), t * 256


def cross_fwd_kernel(q_ref, own_ref, oth_ref, o_ref):
    width = q_ref.shape[1]
    rows = own_ref.shape[0] // PER_STEP
    mask = own_heads()
    lanes = iota((SPAN, 256), 1) // HEAD
    one = jnp.ones((2 * rows, 128), BF)
    both = lambda at, lo: jnp.concatenate(
        [own_ref[at, lo : lo + 256], oth_ref[at, lo : lo + 256]], axis=0
    )
    jobs = list(fours(PER_STEP, width, rows))
    scores = [mm(spread(q_ref[q, lo : lo + 256], mask), both(kv, lo), NT) for q, kv, lo in jobs]
    probs = [jnp.exp2(s - jnp.max(s, axis=1, keepdims=True)).astype(BF) for s in scores]
    for p, (q, kv, lo) in zip(probs, jobs):
        o = mm(p, both(kv, width + lo))
        total = 1.0 / mm(p, one)
        o = o * jnp.concatenate([total, total], axis=1)
        o_ref[q, lo : lo + 256] = gathered(o, lanes).astype(BF)


def cross_fwd(q, own, oth):
    width = q.shape[1]
    spans = q.shape[0] // SPAN
    rows = own.shape[0] // spans
    row = pl.BlockSpec((PER_STEP * SPAN, width), lambda i: (i, 0))
    kv = pl.BlockSpec((PER_STEP * rows, 2 * width), lambda i: (i, 0))
    return pl.pallas_call(
        cross_fwd_kernel,
        grid=(spans // PER_STEP,),
        in_specs=[row, kv, kv],
        out_specs=row,
        out_shape=jax.ShapeDtypeStruct(q.shape, BF),
        compiler_params=params(),
        cost_estimate=cost(spans * 3 * 4 * 256**3, spans * 1000000),
    )(q, own, oth)


def cross_bwd_kernel(q_ref, own_ref, oth_a_ref, oth_b_ref, e_ref, dq_ref, down_ref, doth_ref):
    width = q_ref.shape[1]
    rows = own_ref.shape[0] // PER_STEP
    early = pl.program_id(0) < pl.num_programs(0) // 2
    oth = jnp.where(early, oth_a_ref[...], oth_b_ref[...])
    mask = own_heads()
    lanes = iota((SPAN, 256), 1) // HEAD
    both = lambda at, lo: jnp.concatenate([own_ref[at, lo : lo + 256], oth[at, lo : lo + 256]], axis=0)
    jobs = list(fours(PER_STEP, width, rows))
    q4 = [spread(q_ref[q, lo : lo + 256], mask) for q, kv, lo in jobs]
    e4 = [spread(e_ref[q, lo : lo + 256], mask) for q, kv, lo in jobs]
    scores = [mm(both(kv, lo), x, NT) for x, (q, kv, lo) in zip(q4, jobs)]
    backs = [mm(both(kv, width + lo), x, NT) for x, (q, kv, lo) in zip(e4, jobs)]
    for s, dp, x, y, (q, kv, lo) in zip(scores, backs, q4, e4, jobs):
        p = jnp.exp2(s - jnp.max(s, axis=0, keepdims=True))
        p = p * (1.0 / jnp.sum(p, axis=0, keepdims=True))
        delta = jnp.sum(p * dp, axis=0, keepdims=True)
        ds = (p * (dp - delta)).astype(BF)
        dk = (mm(ds, x) * LN2).astype(BF)
        dv = mm(p.astype(BF), y).astype(BF)
        down_ref[kv, lo : lo + 256] = dk[:rows]
        doth_ref[kv, lo : lo + 256] = dk[rows:]
        down_ref[kv, width + lo : width + lo + 256] = dv[:rows]
        doth_ref[kv, width + lo : width + lo + 256] = dv[rows:]
        dq_ref[q, lo : lo + 256] = (gathered(mm(ds, both(kv, lo), TN), lanes) * 0.125).astype(BF)


def cross_bwd(q, own, oth_a, oth_b, e):
    width = q.shape[1]
    spans = q.shape[0] // SPAN
    rows = own.shape[0] // spans
    steps = spans // PER_STEP
    row = pl.BlockSpec((PER_STEP * SPAN, width), lambda i: (i, 0))
    shape = (PER_STEP * rows, 2 * width)
    kv = pl.BlockSpec(shape, lambda i: (i, 0))
    return pl.pallas_call(
        cross_bwd_kernel,
        grid=(steps,),
        in_specs=[
            row,
            kv,
            pl.BlockSpec(shape, lambda i: (jnp.minimum(i, steps // 2 - 1), 0)),
            pl.BlockSpec(shape, lambda i: (jnp.maximum(i - steps // 2, 0), 0)),
            row,
        ],
        out_specs=[row, kv, kv],
        out_shape=[
            jax.ShapeDtypeStruct(q.shape, BF),
            jax.ShapeDtypeStruct(own.shape, BF),
            jax.ShapeDtypeStruct(own.shape, BF),
        ],
        compiler_params=params(),
        cost_estimate=cost(spans * 3 * 10 * 256**3, spans * 2000000),
    )(q, own, oth_a, oth_b, e)


def pick_kernel(keep_ref, send_ref, blocks_ref, keep_out, send_out, sems):
    count = keep_out.shape[0]
    copies = []
    for i in range(count):
        copies.append(
            pltpu.make_async_copy(blocks_ref.at[send_ref[i]], send_out.at[i], sems.at[0, i])
        )
    for i in range(count):
        copies.append(
            pltpu.make_async_copy(blocks_ref.at[keep_ref[i]], keep_out.at[i], sems.at[1, i])
        )
    for copy in copies:
        copy.start()
    for copy in copies:
        copy.wait()


def pick_blocks(neighbours, keep, send):
    count = keep.shape[0]
    smem = pl.BlockSpec(memory_space=pltpu.SMEM)
    anywhere = pl.BlockSpec(memory_space=pl.ANY)
    vmem = pl.BlockSpec(memory_space=pltpu.VMEM)
    return pl.pallas_call(
        pick_kernel,
        in_specs=[smem, smem, anywhere],
        out_specs=[vmem, vmem],
        out_shape=[jax.ShapeDtypeStruct((count,) + neighbours.shape[1:], BF)] * 2,
        scratch_shapes=[pltpu.SemaphoreType.DMA((2, count))],
        compiler_params=pltpu.CompilerParams(vmem_limit_bytes=VMEM_LIMIT),
        cost_estimate=cost(0, 4 * neighbours.size),
    )(keep, send, neighbours)


def pack_kernel(where_ref, qkv, kv, cq, wo, co, fin, fout, first, second, third, sems):
    core, p = where_ref[0], where_ref[1]
    d, hc = cq.shape
    e8, w8, o8 = d // 8, wo.shape[0] // 8, fout.shape[0] // 8
    take = lambda at, n: pl.ds(pl.multiple_of(at * n, 16), n)
    jobs = [(qkv.at[take(core, d // 2)], first)]
    to = 0
    for ref, count, n in ((kv, 2, e8), (cq, 1, e8), (wo, 2, w8), (co, 2, w8)):
        for i in range(count):
            jobs.append((ref.at[take(p, n), pl.ds(i * hc, hc)], second.at[pl.ds(to, n)]))
            to += n
    to = 0
    for i in range(fin.shape[1] // d):
        jobs.append((fin.at[take(p, w8), pl.ds(i * d, d)], third.at[pl.ds(to, w8)]))
        to += w8
    jobs.append((fout.at[take(p, o8)], third.at[pl.ds(to, o8)]))
    copies = [pltpu.make_async_copy(a, b, sems.at[i]) for i, (a, b) in enumerate(jobs)]
    for copy in copies:
        copy.start()
    for copy in copies:
        copy.wait()


def pack_weights(where, qkv, kv, cq, wo, co, fin, fout):
    anywhere = pl.BlockSpec(memory_space=pl.ANY)
    vmem = pl.BlockSpec(memory_space=pltpu.VMEM)
    d, hc = cq.shape
    n_in = fin.shape[1] // d
    return pl.pallas_call(
        pack_kernel,
        in_specs=[pl.BlockSpec(memory_space=pltpu.SMEM)] + [anywhere] * 7,
        out_specs=[vmem, vmem, vmem],
        out_shape=[
            jax.ShapeDtypeStruct((d // 2, 3 * hc), BF),
            jax.ShapeDtypeStruct((3 * (d // 8) + 4 * (wo.shape[0] // 8), hc), BF),
            jax.ShapeDtypeStruct((n_in * (fin.shape[0] // 8) + fout.shape[0] // 8, d), BF),
        ],
        scratch_shapes=[pltpu.SemaphoreType.DMA((9 + n_in,))],
        compiler_params=pltpu.CompilerParams(vmem_limit_bytes=VMEM_LIMIT),
        cost_estimate=cost(0, 4 * 1024 * 1024),
    )(where, qkv, kv, cq, wo, co, fin, fout)


def place_kernel(order_ref, mine_ref, theirs_ref, out_ref, wide, sems):
    count = mine_ref.shape[0]
    copies = []
    for i in range(count):
        copy = pltpu.make_async_copy(mine_ref.at[i], out_ref.at[order_ref[i]], sems.at[i])
        copy.start()
        copies.append(copy)
    for i in range(count):
        wide[i] = theirs_ref[i].astype(F32)
        copy = pltpu.make_async_copy(
            wide.at[i], out_ref.at[order_ref[count + i]], sems.at[count + i]
        )
        copy.start()
        copies.append(copy)
    for copy in copies:
        copy.wait()


def place_blocks(order, mine, theirs):
    count = order.shape[0]
    return pl.pallas_call(
        place_kernel,
        in_specs=[
            pl.BlockSpec(memory_space=pltpu.SMEM),
            pl.BlockSpec(memory_space=pltpu.VMEM),
            pl.BlockSpec(memory_space=pltpu.VMEM),
        ],
        out_specs=pl.BlockSpec(memory_space=pl.ANY),
        out_shape=jax.ShapeDtypeStruct((count,) + mine.shape[1:], F32),
        scratch_shapes=[
            pltpu.VMEM(mine.shape, F32),
            pltpu.SemaphoreType.DMA((count,)),
        ],
        compiler_params=pltpu.CompilerParams(vmem_limit_bytes=VMEM_LIMIT),
        cost_estimate=cost(0, 8 * mine.size),
    )(order, mine, theirs)


GELU_A = 0.7978845608028654
GELU_B = 0.044715


def feed_kernel(
    half_ref, h_ref, g_ref, r_ref, aa_ref, ab_ref, ba_ref, bb_ref, bina_ref, binb_ref,
    wouta_ref, woutb_ref, bout_ref,
    out_ref, dh_ref, keep_ref, send_ref, gbina_ref, gbinb_ref, h_t, acc, dacc, act_s, dpre_s,
):
    step = pl.program_id(0)
    hc = aa_ref.shape[0]
    bf = aa_ref.shape[1]

    @pl.when(step == 0)
    def _():
        h_t[...] = h_ref[...].T

    win = jnp.concatenate(
        [
            jnp.concatenate([aa_ref[...], ab_ref[...]], axis=1),
            jnp.concatenate([ba_ref[...], bb_ref[...]], axis=1),
        ],
        axis=0,
    )
    here = half_ref[0] == 0
    wa, wb = wouta_ref[...], woutb_ref[...]
    wout = jnp.concatenate([jnp.where(here, wa, wb), jnp.where(here, wb, wa)], axis=0)
    bias = jnp.concatenate([bina_ref[...], binb_ref[...]], axis=1)
    rows = h_ref.shape[0]
    first = step == 0
    total = jnp.zeros(bias.shape, F32)
    for lo in range(0, rows, 256):
        at = slice(lo, lo + 256)
        pre = mm(h_ref[at], win) + bias
        dact = mm(g_ref[at], wout, NT)
        square = pre * pre
        th = jnp.tanh(pre * (GELU_A + GELU_A * GELU_B * square))
        half = 0.5 + 0.5 * th
        act = (pre * half).astype(BF)
        slope = half + pre * (half - half * th) * (GELU_A + 3.0 * GELU_A * GELU_B * square)
        dpre = (dact * slope).astype(BF)
        total += jnp.sum(dpre.astype(F32), axis=0, keepdims=True)
        act_s[at] = act
        dpre_s[at] = dpre
        acc[at] = jnp.where(first, 0.0, acc[at]) + mm(act, wout)
        dacc[at] = jnp.where(first, 0.0, dacc[at]) + mm(dpre, win, NT)
    gbina_ref[0:1, :] = total[:, :bf]
    gbinb_ref[0:1, :] = total[:, bf:]
    gout = mm(act_s[...], g_ref[...], TN).astype(BF)
    gin = mm(h_t[...], dpre_s[...]).astype(BF)

    def put(into_in, into_out):
        into_in[0], into_in[1] = gin[:hc], gin[hc:]
        into_out[0] = jnp.where(here, gout[:bf], gout[bf:])
        into_out[1] = jnp.where(here, gout[bf:], gout[:bf])

    @pl.when(half_ref[1] == 0)
    def _():
        put(keep_ref, send_ref)

    @pl.when(half_ref[1] != 0)
    def _():
        put(send_ref, keep_ref)

    @pl.when(step == pl.num_programs(0) - 1)
    def _():
        out_ref[...] = (r_ref[...] + acc[...] + bout_ref[...]).astype(BF)
        dh_ref[...] = dacc[...]


def feed(where, h, g, r, win_own, win_oth, b_in, wout_own, wout_oth, b_out):
    rows, d = h.shape
    hc = win_own.shape[0]
    ff = win_own.shape[1]
    bf = 384
    n = ff // 2 // bf
    lower = lambda i, p: i
    upper = lambda i, p: n + i
    whole = pl.BlockSpec((rows, d), lambda i, p: (0, 0))
    side = lambda height, which: pl.BlockSpec((height, bf), lambda i, p: (0, which(i, p)))
    grad = pl.BlockSpec((2, bf, d), lambda i, p: (0, i, 0))
    wout = pl.BlockSpec((bf, d), lambda i, p: (i, 0))
    gb = pl.BlockSpec((8, bf), lambda i, p: (0, i))
    return pl.pallas_call(
        feed_kernel,
        grid_spec=pltpu.PrefetchScalarGridSpec(
            num_scalar_prefetch=1,
            grid=(n,),
            in_specs=[
                whole, whole, whole,
                side(hc, lower), side(hc, upper), side(hc, lower), side(hc, upper), side(1, lower), side(1, upper),
                wout, wout,
                pl.BlockSpec((1, d), lambda i, p: (0, 0)),
            ],
            out_specs=[whole, whole, grad, grad, gb, gb],
            scratch_shapes=[
                pltpu.VMEM((d, rows), BF),
                pltpu.VMEM((rows, d), F32),
                pltpu.VMEM((rows, d), F32),
                pltpu.VMEM((rows, 2 * bf), BF),
                pltpu.VMEM((rows, 2 * bf), BF),
            ],
        ),
        out_shape=[
            jax.ShapeDtypeStruct((rows, d), BF),
            jax.ShapeDtypeStruct((rows, d), F32),
            jax.ShapeDtypeStruct((2, ff // 2, d), BF),
            jax.ShapeDtypeStruct((2, ff // 2, d), BF),
            jax.ShapeDtypeStruct((8, ff // 2), F32),
            jax.ShapeDtypeStruct((8, ff // 2), F32),
        ],
        compiler_params=params(),
        cost_estimate=cost(12 * rows * d * ff, 8 * d * ff),
    )(where, h, g, r, win_own, win_own, win_oth, win_oth, b_in, b_in, wout_own, wout_oth, b_out)


def norm(rows, gain, bias):
    mean = jnp.mean(rows, axis=-1, keepdims=True)
    centred = rows - mean
    spread_ = jnp.mean(centred * centred, axis=-1, keepdims=True)
    return centred * lax.rsqrt(spread_ + EPS) * gain + bias


def norm_back(rows, gain, grad):
    mean = jnp.mean(rows, axis=-1, keepdims=True)
    centred = rows - mean
    rstd = lax.rsqrt(jnp.mean(centred * centred, axis=-1, keepdims=True) + EPS)
    hat = centred * rstd
    scaled = grad * gain
    inner = jnp.mean(scaled * hat, axis=-1, keepdims=True)
    back = rstd * (scaled - jnp.mean(scaled, axis=-1, keepdims=True) - hat * inner)
    return back, jnp.sum(grad * hat, axis=0), jnp.sum(grad, axis=0)


class Links:
    def __init__(self, dp, tp):
        self.dp = dp
        self.bits = dp.bit_length() - 1
        self.me = lax.axis_index("dp")
        self.core = self.me & 1
        self.half = lax.axis_index("tp")
        self.swap = [(i, tp - 1 - i) for i in range(tp)]
        rest = list(range(1, self.bits))
        turned = [2, 1] + rest[2:] if self.bits > 2 else rest
        self.steps = list(zip(rest, turned))

    def other(self, x):
        return lax.ppermute(x, "tp", self.swap)

    def across(self, x, step):
        return lax.ppermute(x, "dp", [(i, i ^ (1 << step[i & 1])) for i in range(self.dp)])

    def flag(self, step):
        return (self.me >> jnp.where(self.core == 0, step[0], step[1])) & 1

    def joined(self, mine, theirs, flag, axis=0):
        first = flag == 0
        return jnp.concatenate(
            [jnp.where(first, mine, theirs), jnp.where(first, theirs, mine)], axis=axis
        )

    def piece(self):
        return self.core * 4 + self.flag(self.steps[1]) * 2 + self.flag(self.steps[0])

    def spread(self, x, i):
        step = ([*self.steps[:2], (0, 0)])[i]
        return self.joined(x, self.across(x, step), self.flag(step))

    def fold(self, x, step):
        flag = self.flag(step)
        rows = x[0].shape[1] // 2
        part = lambda at: add(*(lax.dynamic_slice_in_dim(y, at * rows, rows, 1) for y in x))
        return part(flag), self.across(part(1 - flag), step)

    def meet(self, x):
        send = add(*(y[1:] for y in x))
        return add(*(y[:1] for y in x)), self.other(send)

    def halves(self, a, b):
        return jnp.where(self.core == 0, a, b), jnp.where(self.core == 0, b, a)

    def plane_sum(self):
        yield lambda x: (x[0], self.across(x[1], (0, 0)))
        for step in self.steps:
            yield functools.partial(self.fold, step=step)

    def plane_share(self):
        for step in reversed(self.steps):
            yield lambda x, step=step: self.joined(x, self.across(x, step), self.flag(step))
        yield lambda x: (x, self.across(x, (0, 0)))

    def pair(self, x):
        mine, theirs = x
        return jnp.where(self.core == 0, mine, theirs), jnp.where(self.core == 0, theirs, mine)


def add(a, b):
    return (a.astype(F32) + b.astype(F32)).astype(BF)


def tie(*arrays):
    return lax.optimization_barrier(arrays)


class Flow:
    def __init__(self, x, todo):
        self.x, self.todo = x, list(todo)

    def next(self):
        if self.todo:
            self.x = self.todo.pop(0)(self.x)


def advance(flows, *arrays):
    done = lax.optimization_barrier(([f.x for f in flows], *arrays))
    for f, x in zip(flows, done[0]):
        f.x = x
        f.next()
    return done[1] if len(arrays) == 1 else done[1:]


def shift_earlier(x):
    pad = jnp.zeros((SPAN - 1, x.shape[1]), x.dtype)
    return jnp.concatenate([x[SPAN - 1 :], pad], axis=0)


def shift_later(x):
    pad = jnp.zeros((SPAN - 1, x.shape[1]), x.dtype)
    return jnp.concatenate([pad, x[: x.shape[0] - SPAN + 1]], axis=0)


def on_device(
    tokens, neighbours, nbr_index, lengths, w_qkv, qv_bias, w_out, cross_q, cross_kv,
    cross_bias, cross_out, out_bias, ln_gain, ln_bias, fc_in, fc_in_bias, fc_out,
    fc_out_bias, cotangent,
):
    tp = lax.axis_size("tp")
    link = Links(lax.axis_size("dp"), tp)
    half = link.half
    d = tokens.shape[1]
    hc = w_qkv.shape[2]
    ffh = fc_in_bias.shape[0]
    ff = ffh * tp
    spans = nbr_index.shape[1] // tp
    length = lax.dynamic_slice_in_dim(lengths[0], half, 1)
    core = link.core

    small = jnp.concatenate(
        [fc_in_bias.reshape(-1, hc), fc_out_bias.reshape(1, hc), out_bias, ln_gain, ln_bias, qv_bias, cross_bias],
        axis=0,
    )
    small_oth = link.other(small)
    qkv_own = w_qkv.reshape(d, 3 * hc)
    eighth, w8, f8 = d // 8, hc // 8, hc // 8
    place = jnp.stack([core, link.piece()])
    first, second, third = pack_weights(
        place, qkv_own, cross_kv.reshape(d, 2 * hc), cross_q, w_out, cross_out, fc_in, fc_out
    )
    first = link.other(first)
    second = link.other(second)[None]

    order = nbr_index[0]
    keep = lax.dynamic_slice_in_dim(order, half * spans, spans)
    send = lax.dynamic_slice_in_dim(order, (1 - half) * spans, spans)
    nbr_own, nbr_send = pick_blocks(neighbours, keep, send)

    def whole(at, count, natural=True):
        a, b = small[at : at + count], small_oth[at : at + count]
        if natural:
            return link.joined(a, b, half, 1).astype(F32)
        return a.astype(F32), b.astype(F32)

    at = ffh // hc
    b_in = link.joined(small[:at].reshape(1, ffh), small_oth[:at].reshape(1, ffh), half, 1).astype(F32)
    b_out = whole(at, 1)
    out_b = whole(at + 1, 2)
    gains = whole(at + 3, 3)
    shifts = whole(at + 6, 3)
    qv_b = whole(at + 9, 2, False)
    cross_b = whole(at + 11, 2, False)

    tok = tokens.astype(F32)
    h1 = norm(tok, gains[0], shifts[0]).astype(BF)

    def project(w, which):
        bias = jnp.concatenate([qv_b[which][0], jnp.zeros((hc,), F32), qv_b[which][1]])
        scale = jnp.concatenate([jnp.full((hc,), SCORE, F32), jnp.ones((2 * hc,), F32)])
        return ((mm(h1, w) + bias) * scale).astype(BF)

    p_own = project(qkv_own, 0)
    ctx_own, lse_own = self_fwd(p_own, length)
    first, ctx_own, second, third, nbr_send = tie(first, ctx_own, second, third, nbr_send)
    qkv_pair = link.across(first, (0, 0))
    second = link.spread(second, 0)
    cutoff = spans // 2
    nbr_a = link.other(nbr_send[:cutoff])
    qkv_oth = link.joined(first, qkv_pair, core)
    p_oth = project(qkv_oth, 1)
    p_oth, second = tie(p_oth, second)
    second = link.spread(second, 1)
    ctx_oth, lse_oth = self_fwd(p_oth, length)
    ctx_oth, second, nbr_a, nbr_send, third = tie(ctx_oth, second, nbr_a, nbr_send, third)
    second = link.spread(second, 2)
    third = link.other(third)[None]
    nbr_b = link.other(nbr_send[cutoff:])

    rows = lambda lo, n: second[:, lo : lo + n].reshape(8 * n, hc)
    ctx = jnp.concatenate([ctx_own, ctx_oth], axis=1)
    pair = lambda at: jnp.concatenate([rows(at, w8), rows(at + w8, w8)], axis=1)
    wo = jnp.concatenate([w_out, pair(3 * eighth)], axis=0)
    co_w = jnp.concatenate([cross_out, pair(3 * eighth + 2 * w8)], axis=0)
    cq_w = jnp.concatenate([cross_q, rows(2 * eighth, eighth)], axis=1)
    kv_w = jnp.concatenate(
        [cross_kv[:, 0], rows(0, eighth), cross_kv[:, 1], rows(eighth, eighth)], axis=1
    )
    r1 = tok + mm(ctx, wo) + out_b[0]
    h2 = norm(r1, gains[1], shifts[1]).astype(BF)
    cb = [jnp.concatenate([cross_b[0][i], cross_b[1][i]]) for i in range(2)]
    cq = shift_earlier(((mm(h2, cq_w) + cb[0]) * SCORE).astype(BF))
    kv_b = jnp.concatenate([jnp.zeros((d,), F32), cb[1]])
    nbr_own = nbr_own.reshape(-1, d)
    ckv_own = (mm(nbr_own, kv_w) + kv_b).astype(BF)
    cq, ckv_own, third = tie(cq, ckv_own, third)
    third = link.spread(third, 0)
    half_rows = ckv_own.shape[0] // 2
    nbr_a = nbr_a.reshape(-1, d)
    ckv_a = (mm(nbr_a, kv_w) + kv_b).astype(BF)
    cq_rows = cutoff * SPAN
    c_a = cross_fwd(cq[:cq_rows], ckv_own[:half_rows], ckv_a)
    c_a, third, nbr_b = tie(c_a, third, nbr_b)
    third = link.spread(third, 1)
    nbr_b = nbr_b.reshape(-1, d)
    ckv_b = (mm(nbr_b, kv_w) + kv_b).astype(BF)
    c_b = cross_fwd(cq[cq_rows:], ckv_own[half_rows:], ckv_b)
    c_b, third = tie(c_b, third)
    third = link.spread(third, 2)
    cctx = shift_later(jnp.concatenate([c_a, c_b], axis=0))
    r2 = r1 + mm(cctx, co_w) + out_b[1]
    h3 = norm(r2, gains[2], shifts[2]).astype(BF)
    turn = lambda x: link.joined(x[:, :hc], x[:, hc:], half, 1)
    win_oth = jnp.concatenate(
        [third[:, i * f8 : (i + 1) * f8].reshape(hc, d) for i in range(ff // d)], axis=1
    )
    wout_oth = third[:, (ff // d) * f8 :].reshape(ffh, d)
    block_out, d_h3, fc_keep, fc_send, gb_low, gb_high = feed(
        jnp.stack([half, core]), turn(h3), cotangent, r2, fc_in, win_oth, b_in, fc_out, wout_oth, b_out
    )

    plane, share = link.plane_sum, link.plane_share

    share_steps = list(share())

    def sum_flow(keep, send):
        steps = list(plane())
        steps[3:3] = [link.meet]
        return Flow((keep, send), steps + [lambda x: share_steps[0](add(*x)[0])] + share_steps[1:])

    fc = sum_flow(fc_keep, fc_send)
    fc.next()
    cot = cotangent.astype(F32)
    back3, gain3, shift3 = norm_back(r2, gains[2], turn(d_h3))
    d_r2 = cot + back3
    z2 = d_r2.astype(BF)
    e = mm(z2, co_w, NT).astype(BF)
    e, z2 = advance([fc], e, z2)
    d_cq, d_own, d_oth = cross_bwd(cq, ckv_own, ckv_a, ckv_b, shift_earlier(e))
    g_co = mm(cctx, z2, TN).astype(BF)
    d_cq, d_own, d_oth, g_co = advance([fc], d_cq, d_own, d_oth, g_co)
    n_oth = mm(d_oth, kv_w, NT).astype(BF).reshape(spans, -1, d)
    d_cq = shift_later(d_cq)
    back2, gain2, shift2 = norm_back(r1, gains[1], mm(d_cq, cq_w, NT))
    d_r1 = d_r2 + back2
    z1 = d_r1.astype(BF)
    f = mm(z1, wo, NT).astype(BF)
    n_oth, f, d_own = advance([fc], n_oth, f, d_own)
    n_back = link.other(n_oth)
    o_rows = d_oth.shape[0] // 2
    g_kv = (
        mm(nbr_own, d_own, TN) + mm(nbr_a, d_oth[:o_rows], TN) + mm(nbr_b, d_oth[o_rows:], TN)
    ).astype(BF)
    g_kv, d_cq, z1, d_own, f = advance([fc], g_kv, d_cq, z1, d_own, f)
    g_cq = mm(h2, d_cq, TN).astype(BF)
    g_wo = mm(ctx, z1, TN).astype(BF)
    sides = (slice(0, hc), slice(hc, d))
    both = lambda parts: jnp.stack([jnp.concatenate(p, axis=0) for p in parts])
    g_cross = both([[g_kv[:, s], g_kv[:, d:][:, s]] for s in sides]), both(
        [[g_cq[:, s], g_co[s][:, :hc], g_co[s][:, hc:]] for s in sides]
    )
    g_cross, g_wo, f, d_own = tie(link.halves(*g_cross), g_wo, f, d_own)
    cross = sum_flow(*g_cross)
    cross.next()
    n_own = mm(d_own, kv_w, NT).reshape(spans, -1, d)
    n_own, g_wo, f = advance([fc, cross], n_own, g_wo, f)
    dq_oth = self_bwd(p_oth, f[:, hc:], ctx_oth, lse_oth, length)
    dq_oth, f = advance([fc, cross], dq_oth, f)
    dq_own = self_bwd(p_own, f[:, :hc], ctx_own, lse_own, length)
    dq_own, d_own, g_wo = advance([fc, cross], dq_own, d_own, g_wo)
    g_qkv = [[mm(h1, part[i], TN).astype(BF) for part in (dq_own, dq_oth)] for i in range(3)]
    g_self = both([[q, k] for q, k in zip(g_qkv[0], g_qkv[1])]), both(
        [[v, g_wo[s][:, :hc], g_wo[s][:, hc:]] for v, s in zip(g_qkv[2], sides)]
    )
    g_self, dq_own, dq_oth = tie(link.halves(*g_self), dq_own, dq_oth)
    own = sum_flow(*g_self)
    own.next()
    flat = lambda x: jnp.concatenate([x[0], x[1], x[2]], axis=1)
    d_h1 = mm(flat(dq_own), qkv_own, NT) + mm(flat(dq_oth), qkv_oth, NT)
    d_h1, n_own = advance([fc, cross, own], d_h1, n_own)
    back1, gain1, shift1 = norm_back(tok, gains[0], d_h1)
    tokens_grad = d_r1 + back1

    wide = lambda x: jnp.sum(x.astype(F32), axis=0)
    natural = [
        gb_low[0], gb_high[0], wide(cot), wide(d_r1), wide(d_r2), gain1, gain2, gain3, shift1, shift2, shift3,
    ]
    relative = [wide(dq_own[0]), wide(dq_oth[0]), wide(dq_own[2]), wide(dq_oth[2])]
    cqs, cvs = wide(d_cq), wide(d_own[:, d:]) + wide(d_oth[:, d:])
    relative += [cqs[:hc], cqs[hc:], cvs[:hc], cvs[hc:]]
    for i in range(0, len(relative), 2):
        natural.append(link.joined(relative[i], relative[i + 1], half))
    natural = [x[i : i + d] for x in natural for i in range(0, x.shape[0], d)]
    height = len(natural) + -len(natural) % 8
    row = iota((height, d), 0)
    table = jnp.zeros((height, d), F32)
    for i, x in enumerate(natural):
        table = jnp.where(row == i, x[None], table)
    natural = table
    every = [lambda x, b=b: x + link.across(x, (b, b)) for b in range(link.bits)]
    every.append(lambda x: x + link.other(x))
    nbr_grad = place_blocks(order_of(keep, send), n_own, n_back)
    tokens_grad, natural, nbr_grad = advance([fc, cross, own], tokens_grad, natural, nbr_grad)
    while fc.todo:
        advance([fc, cross, own])
    sums = Flow(natural, every)
    sums.next()
    wide_rows = lambda x, n: jnp.concatenate(
        [x[i * (x.shape[0] // n) : (i + 1) * (x.shape[0] // n)] for i in range(n)], axis=1
    )
    s_in, s_out = link.pair(fc.x)
    steps_in = s_in.shape[0] // hc
    fc_in_grad = jnp.concatenate(
        [wide_rows(s_in[:, :hc], steps_in), wide_rows(s_in[:, hc:], steps_in)], axis=1
    ).astype(F32)
    fc_in_grad, s_out = advance([cross, own, sums], fc_in_grad, s_out)
    fc_out_grad = s_out.astype(F32)
    fc_out_grad = advance([cross, own, sums], fc_out_grad)
    while cross.todo:
        advance([cross, own, sums])
    advance([cross, own, sums])
    s_kv, s_rest = link.pair(cross.x)
    cross_kv_grad = jnp.stack([s_kv[:d], s_kv[d:]], axis=1).astype(F32)
    cross_q_grad = s_rest[:d].astype(F32)
    co_grad = wide_rows(s_rest[d:], 2).astype(F32)
    while own.todo or sums.todo:
        cross_kv_grad, cross_q_grad, co_grad = advance([own, sums], cross_kv_grad, cross_q_grad, co_grad)
    s_qk, s_vw = link.pair(own.x)
    qkv_grad = jnp.stack([s_qk[:d], s_qk[d:], s_vw[:d]], axis=1).astype(F32)
    wo_grad = wide_rows(s_vw[d:], 2).astype(F32)
    sums = sums.x
    gb_in = lax.dynamic_slice_in_dim(sums[: ff // d].reshape(-1), half * ffh, ffh)
    rest = lax.dynamic_slice_in_dim(sums[ff // d : ff // d + 13], half * hc, hc, 1)
    return (
        block_out,
        tokens_grad,
        nbr_grad,
        qkv_grad,
        rest[9:11],
        wo_grad,
        cross_q_grad,
        cross_kv_grad,
        rest[11:13],
        co_grad,
        rest[1:3],
        rest[3:6],
        rest[6:9],
        fc_in_grad,
        gb_in,
        fc_out_grad,
        rest[0],
    )


def order_of(keep, send):
    return jnp.concatenate([keep, send])


def solution(mesh):
    return jax.shard_map(
        on_device,
        mesh=mesh,
        in_specs=(
            P(("dp", "tp"), None),
            P("dp", "tp", None),
            P("dp", None),
            P("dp", None),
            P(None, None, "tp"),
            P(None, "tp"),
            P("tp", None),
            P(None, "tp"),
            P(None, None, "tp"),
            P(None, "tp"),
            P("tp", None),
            P(None, "tp"),
            P(None, "tp"),
            P(None, "tp"),
            P("tp", None),
            P("tp"),
            P("tp", None),
            P("tp"),
            P(("dp", "tp"), None),
        ),
        out_specs=(
            P(("dp", "tp"), None),
            P(("dp", "tp"), None),
            P("dp", "tp", None),
            P(None, None, "tp"),
            P(None, "tp"),
            P("tp", None),
            P(None, "tp"),
            P(None, None, "tp"),
            P(None, "tp"),
            P("tp", None),
            P(None, "tp"),
            P(None, "tp"),
            P(None, "tp"),
            P("tp", None),
            P("tp"),
            P("tp", None),
            P("tp"),
        ),
        check_vma=False,
    )
```

time: 758 us -> 528 us (0.70)
  Pallas kernels: 370 us -> 142 us
  blocking collectives: 38.8 us -> 0 us
  other arithmetic: 63.6 us -> 87.1 us
  waiting for transfers between devices: 65.7 us -> 88.2 us
  starting transfers between devices: 30.1 us -> 48.5 us
  local copies, waits for them, and re-layouts: 75.7 us -> 61.6 us
  matrix products: 101 us -> 88.4 us
    pallas_call x6 -> x7, Pallas kernels: 313 us -> 89.5 us  [the longest x1 41.8 us: feed(): pl.pallas_call(feed_kernel, grid_spec=pltpu.PrefetchScalarGridSpec(num_sc...]
    psum x1 -> x0, blocking collectives: 38.8 us -> none  [on_device(): lax.psum(jnp.concatenate(natural).reshape(-1, 128), ('dp', 'tp'))]
    ppermute x14 -> x35, waiting for transfers between devices: 26 us -> 62.7 us  [across(): lax.ppermute(x, 'dp', [(i, i ^ 1 << step[i & 1]) for i in range(self.dp)])]
    ppermute x14 -> x35, starting transfers between devices: 20.6 us -> 40.6 us  [across(): lax.ppermute(x, 'dp', [(i, i ^ 1 << step[i & 1]) for i in range(self.dp)])]
    dynamic_slice x11 -> x1, local copies, waits for them, and re-layouts: 17.8 us -> 0.67 us  [on_device(): lax.dynamic_slice_in_dim(sums[:ff // d].reshape(-1), half * ffh, ffh)]
    convert_element_type x13 -> x25, other arithmetic: 10.9 us -> 26.3 us  [the longest x12 17.2 us: add(): return (a.astype(F32) + b.astype(F32)).astype(BF)]
    ppermute x10 -> x11, waiting for transfers between devices: 39.7 us -> 25.6 us  [other(): return lax.ppermute(x, 'tp', self.swap)]
    slice x10 -> x15, local copies, waits for them, and re-layouts: 2.55 us -> 15.7 us  [the longest x2 4.25 us: on_device(): c_a = cross_fwd(cq[:cq_rows], ckv_own[:half_rows], ckv_a)]
  transfers between devices with their start and end apart: 24 -> 46, of which waited for: 7 -> 19; matrix products, arithmetic and copies ran while one was open for 13% -> 36% of each run, Pallas kernels for 5% -> 19%
where the time goes in v2:
time: 528 us; the launch traced here: 519 us
  Pallas kernels  142 us (27%)
  matrix products  88.4 us (17%)
  waiting for transfers between devices  88.2 us (17%)
  other arithmetic  87.1 us (16%)
  local copies, waits for them, and re-layouts  61.6 us (12%)
  starting transfers between devices  48.5 us (9%)
    dot_general x27, matrix products, mm(): return lax.dot_general(a, b, dims, preferred_element_type=F32)  88.4 us
    ppermute x35, waiting for transfers between devices, across(): lax.ppermute(x, 'dp', [(i, i ^ 1 << step[i & 1]) for i in range(self.dp)])  62.7 us
    pallas_call x1, Pallas kernels, feed(): pl.pallas_call(feed_kernel, grid_spec=pltpu.PrefetchScalarGridSpec(num_sc...  41.8 us
    ppermute x35, starting transfers between devices, across(): lax.ppermute(x, 'dp', [(i, i ^ 1 << step[i & 1]) for i in range(self.dp)])  40.6 us
    pallas_call x2, Pallas kernels, self_bwd(): pl.pallas_call(self_bwd_kernel, grid_spec=pltpu.PrefetchScalarGridSpec(nu...  30.6 us
    ppermute x11, waiting for transfers between devices, other(): return lax.ppermute(x, 'tp', self.swap)  25.6 us
    unnamed x263, local copies, waits for them, and re-layouts  23.4 us
    pallas_call x2, Pallas kernels, self_fwd(): pl.pallas_call(self_fwd_kernel, grid_spec=pltpu.PrefetchScalarGridSpec(nu...  21.9 us
  transfers between devices with their start and end apart: 46, of which 19 were waited for; matrix products, arithmetic and copies ran while one was open for 36% of the time, Pallas kernels for 19%

profile of v2, /device:TPU:1, one launch (start us, length us, event | category | flops | bytes accessed | tf_op | source)
XLA Modules:
  0.0 519.1 jit_solution(6462433085778388159)
XLA Ops:
  2.1 3.0 concatenate.197
  7.2 2.5 copy.52
  9.7 2.6 copy.41
  12.4 2.4 copy.42.qkv
  15.4 3.6 shard_map.314
  22.7 6.7 %shard_map.316 = (bf16[16,128,768]{2,1,0:T(8,128)(2,1)}, bf16[16,128,768]{2,1,0:T(8,128)(2,1)}) custom-call(s32[16]{0:T(128)} %get-tuple-element.501.keep_ref, s32[16]{0:T(128)} %get-tuple-element.500.send_ref, bf16[32,128,768]{2,1,0:T(8,128)(2,1)} %blocks_ref.1), custom_call_target="tpu_custom_call" | custom-call | bytes 12582912 | tf_op jit(solution)/shard_map/pallas_call | solution.py:313
  30.3 3.7 multiply_convert_fusion.1.q_ref.k_ref.v_ref
  34.0 10.9 %shard_map.315 = (bf16[1024,384]{1,0:T(8,128)(2,1)}, f32[1024,384]{1,0:T(8,128)}) custom-call(s32[1]{0:T(128)} %bitcast.4.len_ref, bf16[1024,1152]{1,0:T(8,128)(2,1)} %multiply_convert_fusion.1.q_ref.k_ref.v_ref, bf16[1024,1152]{1,0:T(8,128)(2,1)} %multiply_convert_fusion.1.q_ref.k_ref.v_ref, bf16[1024,1152]{1,0:T(8,128)(2,1)} %multiply_convert_fusion.1.q_ref.k_ref.v_ref), custom_call_target="tpu_custom_call" | custom-call | flops 3221225472 | bytes 3145728 | tf_op jit(solution)/shard_map/pallas_call | solution.py:89
  44.9 2.6 collective-permute-done
  50.6 2.7 slice.449
  53.5 2.7 collective-permute-done.4
  59.3 3.7 multiply_convert_fusion.q_ref.k_ref.v_ref
  64.3 11.0 %shard_map.317 = (bf16[1024,384]{1,0:T(8,128)(2,1)}, f32[1024,384]{1,0:T(8,128)}) custom-call(s32[1]{0:T(128)} %bitcast.4.len_ref, bf16[1024,1152]{1,0:T(8,128)(2,1)} %multiply_convert_fusion.q_ref.k_ref.v_ref, bf16[1024,1152]{1,0:T(8,128)(2,1)} %multiply_convert_fusion.q_ref.k_ref.v_ref, bf16[1024,1152]{1,0:T(8,128)(2,1)} %multiply_convert_fusion.q_ref.k_ref.v_ref), custom_call_target="tpu_custom_call" | custom-call | flops 3221225472 | bytes 3145728 | tf_op jit(solution)/shard_map/pallas_call | solution.py:89
  77.9 11.5 %collective-permute-done.6 = bf16[8,128,768]{2,1,0:T(8,128)(2,1)} collective-permute-done((bf16[8,128,768]{2,1,0:T(8,128)(2,1)}, bf16[8,128,768]{2,1,0:T(8,128)(2,1)}, u32[]{:S(2)}, u32[]{:S(2)}) %collective-permute-start.6) | collective-permute-done | bytes 1572896 | tf_op jit(solution)/shard_map/ppermute | solution.py:552
  96.9 2.7 broadcast_select_fusion.9
  107.4 6.0 %add_convert_fusion.own_ref = bf16[2048,1536]{1,0:T(8,128)(2,1)S(1)} fusion(bf16[2048,768]{1,0:T(8,128)(2,1)S(1)} %bitcast.171, f32[1536]{0:T(1024)S(1)} %pad_maximum_fusion.37, bf16[768,384]{1,0:T(8,128)(2,1)S(1)} %bitcast.156, bf16[768,384]{1,0:T(8,128)(2,1)S(1)} %copy-done.58, bf16[768,384]{1,0:T(8,128)(2,1)S(1)} %bitcast.151, ...), kind=kOutput, calls=%fused_computation | convolution fusion | flops 4847566848 | bytes 11802624 | tf_op jit(solution)/shard_map/dot_general | solution.py:28
  116.1 3.0 fusion.92
  119.1 5.7 %add_convert_fusion.2.oth_ref.oth_a_ref = bf16[1024,1536]{1,0:T(8,128)(2,1)} fusion(bf16[1024,768]{1,0:T(8,128)(2,1)} %bitcast.17, f32[1536]{0:T(1024)S(1)} %pad_maximum_fusion.37, bf16[768,384]{1,0:T(8,128)(2,1)S(1)} %bitcast.157, bf16[768,384]{1,0:T(8,128)(2,1)S(1)} %copy-done.58, bf16[768,384]{1,0:T(8,128)(2,1)S(1)} %bitcast.152, ...), kind=kOutput, calls=%fused_computation.4 | convolution fusion | flops 2428502016 | bytes 7084032 | tf_op jit(solution)/shard_map/dot_general | solution.py:28
  126.1 5.9 %shard_map.318 = bf16[512,768]{1,0:T(8,128)(2,1)} custom-call(bf16[512,768]{1,0:T(8,128)(2,1)} %get-tuple-element.417.q_ref, bf16[1024,1536]{1,0:T(8,128)(2,1)} %get-tuple-element.357.own_ref, bf16[1024,1536]{1,0:T(8,128)(2,1)} %add_convert_fusion.2.oth_ref.oth_a_ref), custom_call_target="tpu_custom_call" | custom-call | flops 1610612736 | bytes 8000000 | tf_op jit(solution)/shard_map/pallas_call | solution.py:224
  133.4 9.2 %collective-permute-done.10 = bf16[8,128,768]{2,1,0:T(8,128)(2,1)} collective-permute-done((bf16[8,128,768]{2,1,0:T(8,128)(2,1)S(1)}, bf16[8,128,768]{2,1,0:T(8,128)(2,1)}, u32[]{:S(2)}, u32[]{:S(2)}) %collective-permute-start.10) | collective-permute-done | bytes 1572896 | tf_op jit(solution)/shard_map/ppermute | solution.py:552
  143.7 5.9 %add_convert_fusion.1.oth_ref.oth_b_ref = bf16[1024,1536]{1,0:T(8,128)(2,1)} fusion(bf16[1024,768]{1,0:T(8,128)(2,1)} %bitcast.18, f32[1536]{0:T(1024)S(1)} %pad_maximum_fusion.37, bf16[768,384]{1,0:T(8,128)(2,1)S(1)} %bitcast.158, bf16[768,384]{1,0:T(8,128)(2,1)S(1)} %copy-done.59, bf16[768,384]{1,0:T(8,128)(2,1)S(1)} %bitcast.153, ...), kind=kOutput, calls=%fused_computation.3 | convolution fusion | flops 2428502016 | bytes 7084032 | tf_op jit(solution)/shard_map/dot_general | solution.py:28
  149.6 5.9 %shard_map.319 = bf16[512,768]{1,0:T(8,128)(2,1)} custom-call(bf16[512,768]{1,0:T(8,128)(2,1)} %get-tuple-element.418.q_ref, bf16[1024,1536]{1,0:T(8,128)(2,1)} %get-tuple-element.358.own_ref, bf16[1024,1536]{1,0:T(8,128)(2,1)} %add_convert_fusion.1.oth_ref.oth_b_ref), custom_call_target="tpu_custom_call" | custom-call | flops 1610612736 | bytes 8000000 | tf_op jit(solution)/shard_map/pallas_call | solution.py:224
  155.4 2.5 collective-permute-done.11
  169.3 41.8 %shard_map.320 = (bf16[1024,768]{1,0:T(8,128)(2,1)}, f32[1024,768]{1,0:T(8,128)}, bf16[2,1536,768]{2,1,0:T(8,128)(2,1)}, bf16[2,1536,768]{2,1,0:T(8,128)(2,1)}, f32[8,1536]{1,0:T(8,128)}, /*index=5*/f32[8,1536]{1,0:T(8,128)}) custom-call(s32[2]{0:T(128)} %get-tuple-element.507.half_ref, bf16[1024,768]{1,0:T(8,128)(2,1)} %pad_maximum_fusion.11.h_ref, ...), custom_call_target="tpu_custom_call" | custom-call | flops 28991029248 | bytes 18874368 | tf_op jit(solution)/shard_map/pallas_call | solution.py:488
  212.6 2.2 slice_select_fusion.1
  215.5 2.4 multiply_reduce_fusion.1
  217.9 2.3 fusion.90
  221.1 2.7 convolution_convert_fusion.2
  223.9 5.7 %add_convert_fusion.4 = (bf16[2,768,768]{2,1,0:T(8,128)(2,1)}, bf16[2,768,768]{2,1,0:T(8,128)(2,1)}) fusion(bf16[2,1536,768]{2,1,0:T(8,128)(2,1)} %collective-permute-done.13, s32[]{:T(128)S(6)} %select_n.543, bf16[2,1536,768]{2,1,0:T(8,128)(2,1)S(1)} %bitcast.141, s32[]{:T(128)S(6)} %select_n.542), kind=kLoop, calls=%fused_computation.9 | loop fusion | flops 9437184 | bytes 14155784 | tf_op jit(solution)/shard_map/convert_element_type | solution.py:602
  239.9 2.5 convolution_convert_fusion.5
  242.4 17.2 %shard_map.321 = (bf16[1024,768]{1,0:T(8,128)(2,1)}, bf16[2048,1536]{1,0:T(8,128)(2,1)}, bf16[2048,1536]{1,0:T(8,128)(2,1)}) custom-call(bf16[1024,768]{1,0:T(8,128)(2,1)} %copy-done.18, bf16[2048,1536]{1,0:T(8,128)(2,1)} %copy-done.17, bf16[1024,1536]{1,0:T(8,128)(2,1)} %add_convert_fusion.2.oth_ref.oth_a_ref, ...), custom_call_target="tpu_custom_call" | custom-call | flops 8053063680 | bytes 32000000 | tf_op jit(solution)/shard_map/pallas_call | solution.py:270
  262.3 2.3 multiply_reduce_fusion
  266.3 2.2 add_convert_fusion.12
  275.6 4.7 fusion.21
  280.3 6.4 %convolution_convert_fusion = bf16[2048,768]{1,0:T(8,128)(2,1)} fusion(bf16[2048,1536]{1,0:T(8,128)(2,1)S(1)} %bitcast.137, bf16[768,384]{1,0:T(8,128)(2,1)S(1)} %bitcast.159, bf16[768,384]{1,0:T(8,128)(2,1)S(1)} %copy-done.60, bf16[768,384]{1,0:T(8,128)(2,1)S(1)} %bitcast.154, bf16[768,384]{1,0:T(8,128)(2,1)S(1)} %copy-done.63), kind=kOutput, calls=%fused_computation.29 | convolution fusion | flops 4842848256 | bytes 11796480 | tf_op jit(solution)/shard_map/dot_general | solution.py:28
  288.8 6.9 %fusion.106 = f32[768,1536]{1,0:T(8,128)} fusion(bf16[2048,768]{1,0:T(8,128)(2,1)S(1)} %bitcast.172, bf16[2048,1536]{1,0:T(8,128)(2,1)S(1)} %bitcast.148), kind=kOutput, calls=%fused_computation.385 | convolution fusion | flops 4831838208 | bytes 14155776 | tf_op jit(solution)/shard_map/dot_general | solution.py:28
  295.7 5.8 %add_convert_fusion.3 = bf16[768,1536]{1,0:T(8,128)(2,1)S(1)} fusion(f32[768,1536]{1,0:T(8,128)} %fusion.106, f32[768,1536]{1,0:T(8,128)S(1)} %fusion.21, bf16[1024,768]{1,0:T(8,128)(2,1)} %bitcast.18, bf16[2048,1536]{1,0:T(8,128)(2,1)S(1)} %bitcast.137), kind=kOutput, calls=%fused_computation.8 | convolution fusion | flops 2419458048 | bytes 16515072 | tf_op jit(solution)/shard_map/dot_general | solution.py:28
  303.8 2.5 convolution_convert_fusion.3
  311.8 2.4 collective-permute-start.17
  314.5 7.0 %fusion.89 = f32[2048,768]{1,0:T(8,128)} fusion(bf16[2048,1536]{1,0:T(8,128)(2,1)S(1)} %bitcast.148, bf16[768,384]{1,0:T(8,128)(2,1)S(1)} %bitcast.160, bf16[768,384]{1,0:T(8,128)(2,1)S(1)} %copy-done.60, bf16[768,384]{1,0:T(8,128)(2,1)S(1)} %bitcast.155, bf16[768,384]{1,0:T(8,128)(2,1)S(1)} %copy-done.63), kind=kOutput, calls=%fused_computation.368 | convolution fusion | flops 4841275392 | bytes 14942208 | tf_op jit(solution)/shard_map/dot_general | solution.py:28
  321.5 6.2 %collective-permute-done.17 = bf16[1,192,768]{2,1,0:T(8,128)(2,1)S(1)} collective-permute-done((bf16[1,192,768]{2,1,0:T(8,128)(2,1)S(1)}, bf16[1,192,768]{2,1,0:T(8,128)(2,1)S(1)}, u32[]{:S(2)}, u32[]{:S(2)}) %collective-permute-start.17) | collective-permute-done | bytes 294944 | tf_op jit(solution)/shard_map/ppermute | solution.py:555
  329.4 3.0 collective-permute-start.19
  333.4 15.4 %shard_map.322 = bf16[3,1024,384]{2,1,0:T(8,128)(2,1)} custom-call(s32[1]{0:T(128)} %bitcast.4.len_ref, bf16[1024,1152]{1,0:T(8,128)(2,1)} %multiply_convert_fusion.q_ref.k_ref.v_ref, bf16[1024,1152]{1,0:T(8,128)(2,1)} %multiply_convert_fusion.q_ref.k_ref.v_ref, bf16[1024,1152]{1,0:T(8,128)(2,1)} %multiply_convert_fusion.q_ref.k_ref.v_ref, ...), custom_call_target="tpu_custom_call" | custom-call | flops 8053063680 | bytes 6291456 | tf_op jit(solution)/shard_map/pallas_call | solution.py:160
  351.4 3.4 convolution_convert_fusion.6
  358.2 15.2 %shard_map.323 = bf16[3,1024,384]{2,1,0:T(8,128)(2,1)} custom-call(s32[1]{0:T(128)} %bitcast.4.len_ref, bf16[1024,1152]{1,0:T(8,128)(2,1)} %multiply_convert_fusion.1.q_ref.k_ref.v_ref, bf16[1024,1152]{1,0:T(8,128)(2,1)} %multiply_convert_fusion.1.q_ref.k_ref.v_ref, bf16[1024,1152]{1,0:T(8,128)(2,1)} %multiply_convert_fusion.1.q_ref.k_ref.v_ref, ...), custom_call_target="tpu_custom_call" | custom-call | flops 8053063680 | bytes 6291456 | tf_op jit(solution)/shard_map/pallas_call | solution.py:160
  378.7 5.6 %collective-permute-done.22 = bf16[2,384,384]{2,1,0:T(8,128)(2,1)S(1)} collective-permute-done((bf16[2,384,384]{2,1,0:T(8,128)(2,1)S(1)}, bf16[2,384,384]{2,1,0:T(8,128)(2,1)S(1)}, u32[]{:S(2)}, u32[]{:S(2)}) %collective-permute-start.22) | collective-permute-done | bytes 589856 | tf_op jit(solution)/shard_map/ppermute | solution.py:555
  393.0 2.4 collective-permute-start.25
  397.1 2.2 fusion.25
  399.3 3.9 fusion.37
  403.2 7.8 %collective-permute-done.23 = bf16[768,768]{1,0:T(8,128)(2,1)S(1)} collective-permute-done((bf16[768,768]{1,0:T(8,128)(2,1)S(1)}, bf16[768,768]{1,0:T(8,128)(2,1)S(1)}, u32[]{:S(2)}, u32[]{:S(2)}) %collective-permute-start.23) | collective-permute-done | bytes 1179680 | tf_op jit(solution)/shard_map/ppermute | solution.py:555
  416.5 8.5 %shard_map.324 = f32[32,128,768]{2,1,0:T(8,128)} custom-call(s32[32]{0:T(128)} %pad_add_fusion.2.order_ref, f32[16,128,768]{2,1,0:T(8,128)} %bitcast.138, bf16[16,128,768]{2,1,0:T(8,128)(2,1)} %collective-permute-done.29.theirs_ref), custom_call_target="tpu_custom_call" | custom-call | bytes 12582912 | tf_op jit(solution)/shard_map/pallas_call | solution.py:387
  425.1 3.3 fusion.12
  428.7 4.1 fusion.11
  434.5 2.2 collective-permute-start.30
  441.5 2.8 convert_element_type.498
  444.4 2.9 collective-permute-done.31
  449.2 2.5 convert_element_type.505
  456.7 10.6 %collective-permute-done.38 = f32[24,768]{1,0:T(8,128)S(1)} collective-permute-done((f32[24,768]{1,0:T(8,128)S(1)}, f32[24,768]{1,0:T(8,128)S(1)}, u32[]{:S(2)}, u32[]{:S(2)}) %collective-permute-start.38) | collective-permute-done | bytes 73760 | tf_op jit(solution)/shard_map/ppermute | solution.py:555
  467.6 2.8 collective-permute-start.39
  472.9 10.4 %collective-permute-done.41 = f32[24,768]{1,0:T(8,128)S(1)} collective-permute-done((f32[24,768]{1,0:T(8,128)S(1)}, f32[24,768]{1,0:T(8,128)S(1)}, u32[]{:S(2)}, u32[]{:S(2)}) %collective-permute-start.41) | collective-permute-done | bytes 73760 | tf_op jit(solution)/shard_map/ppermute | solution.py:555
  488.8 2.3 collective-permute-done.42
  491.4 9.0 %collective-permute-done.44 = bf16[768,384]{1,0:T(8,128)(2,1)S(1)} collective-permute-done((bf16[768,384]{1,0:T(8,128)(2,1)S(1)}, bf16[768,384]{1,0:T(8,128)(2,1)S(1)}, u32[]{:S(2)}, u32[]{:S(2)}) %collective-permute-start.44) | collective-permute-done | bytes 589856 | tf_op jit(solution)/shard_map/ppermute | solution.py:555
  500.6 2.8 collective-permute-start.45
  505.5 3.2 copy.47
  (528 shorter events, 150.3 us)
Async XLA Ops:
  0.7 21.5 %copy-start = (s32[1,2]{1,0:T(1,128)S(1)}, s32[1,2]{1,0:T(1,128)}, u32[]{:S(2)}) copy-start(s32[1,2]{1,0:T(1,128)} %param.22) | copy-start | bytes 28
  5.1 24.3 %collective-permute-start.1 = (bf16[17,384]{1,0:T(8,128)(2,1)S(1)}, bf16[17,384]{1,0:T(8,128)(2,1)S(1)}, u32[]{:S(2)}, u32[]{:S(2)}) collective-permute-start(bf16[17,384]{1,0:T(8,128)(2,1)S(1)} %concatenate.197), channel_id=1, source_target_pairs={{0,1},{1,0},{2,3},{3,2},{4,5},{5,4},{6,7},{7,6},{8,9},{9,8},{10,11... | collective-permute-start | bytes 39176 | tf_op jit(solution)/shard_map/ppermute | solution.py:552
  12.4 18.0 %copy-start.13 = (bf16[768,3,384]{0,2,1:T(8,128)(2,1)}, bf16[768,3,384]{0,2,1:T(8,128)(2,1)S(1)}, u32[]{:S(2)}) copy-start(bf16[768,3,384]{0,2,1:T(8,128)(2,1)S(1)} %copy.41) | copy-start | bytes 5308420
  19.0 25.9 %collective-permute-start.2 = (bf16[480,384]{1,0:T(8,128)(2,1)}, bf16[480,384]{1,0:T(8,128)(2,1)}, u32[]{:S(2)}, u32[]{:S(2)}) collective-permute-start(bf16[480,384]{1,0:T(8,128)(2,1)} %get-tuple-element.151), channel_id=1, source_target_pairs={{0,1},{1,0},{2,3},{3,2},{4,5},{5,4},{6,7},{7,6},{8,9},{9,8},{10,11... | collective-permute-start | bytes 1105928 | tf_op jit(solution)/shard_map/ppermute | solution.py:552
  19.1 28.4 %collective-permute-start = (bf16[384,1152]{1,0:T(8,128)(2,1)}, bf16[384,1152]{1,0:T(8,128)(2,1)}, u32[]{:S(2)}, u32[]{:S(2)}) collective-permute-start(bf16[384,1152]{1,0:T(8,128)(2,1)} %get-tuple-element.149), channel_id=1, source_target_pairs={{0,1},{1,0},{2,3},{3,2},{4,5},{5,4},{6,7},{7,6},{8,9},{9,8},{10,11... | collective-permute-start | bytes 2654216 | tf_op jit(solution)/shard_map/ppermute | solution.py:552
  47.5 9.9 %collective-permute-start.3 = (bf16[384,1152]{1,0:T(8,128)(2,1)}, bf16[384,1152]{1,0:T(8,128)(2,1)}, u32[]{:S(2)}, u32[]{:S(2)}) collective-permute-start(bf16[384,1152]{1,0:T(8,128)(2,1)} %collective-permute-done), channel_id=1, source_target_pairs={{0,2},{2,0},{4,6},{6,4},{8,10},{10,8},{12,14},{14,12},{16,18},{18,... | collective-permute-start | bytes 2654216 | tf_op jit(solution)/shard_map/ppermute | solution.py:555
  49.4 6.9 %collective-permute-start.4 = (bf16[1,480,384]{2,1,0:T(8,128)(2,1)}, bf16[1,480,384]{2,1,0:T(8,128)(2,1)S(1)}, u32[]{:S(2)}, u32[]{:S(2)}) collective-permute-start(bf16[1,480,384]{2,1,0:T(8,128)(2,1)} %bitcast.5), channel_id=1, source_target_pairs={{0,4},{2,10},{4,0},{6,14},{8,12},{10,2},{12,8},{14,6},{16,20},{18,... | collective-permute-start | bytes 1105928 | tf_op jit(solution)/shard_map/ppermute | solution.py:555
  53.3 36.1 %collective-permute-start.6 = (bf16[8,128,768]{2,1,0:T(8,128)(2,1)}, bf16[8,128,768]{2,1,0:T(8,128)(2,1)}, u32[]{:S(2)}, u32[]{:S(2)}) collective-permute-start(bf16[8,128,768]{2,1,0:T(8,128)(2,1)} %slice.449), channel_id=1, source_target_pairs={{0,1},{1,0},{2,3},{3,2},{4,5},{5,4},{6,7},{7,6},{8,9},{9,8},{10,11... | collective-permute-start | bytes 4718600 | tf_op jit(solution)/shard_map/ppermute | solution.py:552
  62.9 12.3 %collective-permute-start.5 = (bf16[2,480,384]{2,1,0:T(8,128)(2,1)S(1)}, bf16[2,480,384]{2,1,0:T(8,128)(2,1)}, u32[]{:S(2)}, u32[]{:S(2)}) collective-permute-start(bf16[2,480,384]{2,1,0:T(8,128)(2,1)S(1)} %pad_maximum_fusion.22), channel_id=1, source_target_pairs={{0,8},{2,6},{4,12},{6,2},{8,0},{10,14},{12,4},{14,10},{16,24},{18,... | collective-permute-start | bytes 2211848 | tf_op jit(solution)/shard_map/ppermute | solution.py:555
  75.2 15.2 %copy-start.11 = (bf16[768,2,384]{2,1,0:T(2,128)(2,1)S(1)}, bf16[768,2,384]{2,1,0:T(2,128)(2,1)}, u32[]{:S(2)}) copy-start(bf16[768,2,384]{2,1,0:T(2,128)(2,1)} %param.27) | copy-start | bytes 3538948
  89.4 7.4 %collective-permute-start.7 = (bf16[4,480,384]{2,1,0:T(8,128)(2,1)}, bf16[4,480,384]{2,1,0:T(8,128)(2,1)}, u32[]{:S(2)}, u32[]{:S(2)}) collective-permute-start(bf16[4,480,384]{2,1,0:T(8,128)(2,1)} %pad_maximum_fusion.12), channel_id=1, source_target_pairs={{0,2},{2,0},{4,6},{6,4},{8,10},{10,8},{12,14},{14,12},{16,18},{18,... | collective-permute-start | bytes 4423688 | tf_op jit(solution)/shard_map/ppermute | solution.py:555
  93.6 21.8 %collective-permute-start.8 = (bf16[384,768]{1,0:T(8,128)(2,1)}, bf16[384,768]{1,0:T(8,128)(2,1)}, u32[]{:S(2)}, u32[]{:S(2)}) collective-permute-start(bf16[384,768]{1,0:T(8,128)(2,1)} %get-tuple-element.165), channel_id=1, source_target_pairs={{0,1},{1,0},{2,3},{3,2},{4,5},{5,4},{6,7},{7,6},{8,9},{9,8},{10,11... | collective-permute-start | bytes 1769480 | tf_op jit(solution)/shard_map/ppermute | solution.py:552
  95.4 47.2 %collective-permute-start.10 = (bf16[8,128,768]{2,1,0:T(8,128)(2,1)S(1)}, bf16[8,128,768]{2,1,0:T(8,128)(2,1)}, u32[]{:S(2)}, u32[]{:S(2)}) collective-permute-start(bf16[8,128,768]{2,1,0:T(8,128)(2,1)S(1)} %slice.469), channel_id=1, source_target_pairs={{0,1},{1,0},{2,3},{3,2},{4,5},{5,4},{6,7},{7,6},{8,9},{9,8},{10,11... | collective-permute-start | bytes 4718600 | tf_op jit(solution)/shard_map/ppermute | solution.py:552
  100.6 12.7 %copy-start.56 = (bf16[8,96,384]{2,1,0:T(8,128)(2,1)}, bf16[8,96,384]{2,1,0:T(8,128)(2,1)S(1)}, u32[]{:S(2)}) copy-start(bf16[8,96,384]{2,1,0:T(8,128)(2,1)S(1)} %get-tuple-element.380) | copy-start | bytes 1769476
  100.6 18.4 %copy-start.50 = (bf16[8,96,384]{2,1,0:T(8,128)(2,1)}, bf16[8,96,384]{2,1,0:T(8,128)(2,1)S(1)}, u32[]{:S(2)}) copy-start(bf16[8,96,384]{2,1,0:T(8,128)(2,1)S(1)} %get-tuple-element.379) | copy-start | bytes 1769476
  100.6 18.4 %copy-start.53 = (bf16[8,96,384]{2,1,0:T(8,128)(2,1)}, bf16[8,96,384]{2,1,0:T(8,128)(2,1)S(1)}, u32[]{:S(2)}) copy-start(bf16[8,96,384]{2,1,0:T(8,128)(2,1)S(1)} %get-tuple-element.381) | copy-start | bytes 1769476
  115.4 9.5 %copy-start.18 = (bf16[1024,768]{1,0:T(8,128)(2,1)}, bf16[1024,768]{1,0:T(8,128)(2,1)S(1)}, u32[]{:S(2)}) copy-start(bf16[1024,768]{1,0:T(8,128)(2,1)S(1)} %concatenate.212.q_ref) | copy-start | bytes 4718596
  115.4 16.6 %collective-permute-start.9 = (bf16[1,384,768]{2,1,0:T(8,128)(2,1)}, bf16[1,384,768]{2,1,0:T(8,128)(2,1)S(1)}, u32[]{:S(2)}, u32[]{:S(2)}) collective-permute-start(bf16[1,384,768]{2,1,0:T(8,128)(2,1)} %bitcast.16), channel_id=1, source_target_pairs={{0,4},{2,10},{4,0},{6,14},{8,12},{10,2},{12,8},{14,6},{16,20},{18,... | collective-permute-start | bytes 1769480 | tf_op jit(solution)/shard_map/ppermute | solution.py:555
  131.9 11.1 %copy-start.85 = (bf16[1536]{0:T(1024)(128)(2,1)S(1)}, bf16[1536]{0:T(1024)(128)(2,1)}, u32[]{:S(2)}) copy-start(bf16[1536]{0:T(1024)(128)(2,1)} %param.34) | copy-start | bytes 9220
  131.9 11.1 %copy-start.93 = (bf16[384]{0:T(512)(128)(2,1)S(1)}, bf16[384]{0:T(512)(128)(2,1)}, u32[]{:S(2)}) copy-start(bf16[384]{0:T(512)(128)(2,1)} %param.36) | copy-start | bytes 2308
  131.9 11.8 %copy-start.51 = (bf16[8,96,384]{2,1,0:T(8,128)(2,1)S(1)}, bf16[8,96,384]{2,1,0:T(8,128)(2,1)}, u32[]{:S(2)}) copy-start(bf16[8,96,384]{2,1,0:T(8,128)(2,1)} %copy-done.50) | copy-start | bytes 1769476
  131.9 11.8 %copy-start.54 = (bf16[8,96,384]{2,1,0:T(8,128)(2,1)S(1)}, bf16[8,96,384]{2,1,0:T(8,128)(2,1)}, u32[]{:S(2)}) copy-start(bf16[8,96,384]{2,1,0:T(8,128)(2,1)} %copy-done.53) | copy-start | bytes 1769476
  132.0 11.7 %copy-start.59 = (bf16[768,384]{1,0:T(8,128)(2,1)S(1)}, bf16[768,384]{1,0:T(8,128)(2,1)}, u32[]{:S(2)}) copy-start(bf16[768,384]{1,0:T(8,128)(2,1)} %get-tuple-element.514) | copy-start | bytes 1769476
  132.0 11.7 %copy-start.62 = (bf16[768,384]{1,0:T(8,128)(2,1)S(1)}, bf16[768,384]{1,0:T(8,128)(2,1)}, u32[]{:S(2)}) copy-start(bf16[768,384]{1,0:T(8,128)(2,1)} %get-tuple-element.515) | copy-start | bytes 1769476
  142.6 15.3 %collective-permute-start.11 = (bf16[2,384,768]{2,1,0:T(8,128)(2,1)S(1)}, bf16[2,384,768]{2,1,0:T(8,128)(2,1)S(1)}, u32[]{:S(2)}, u32[]{:S(2)}) collective-permute-start(bf16[2,384,768]{2,1,0:T(8,128)(2,1)S(1)} %pad_maximum_fusion.14), channel_id=1, source_target_pairs={{0,8},{2,6},{4,12},{6,2},{8,0},{10,14},{12,4},{14,10},{16,24},{18,... | collective-permute-start | bytes 3538952 | tf_op jit(solution)/shard_map/ppermute | solution.py:555
  158.4 7.1 %collective-permute-start.12 = (bf16[4,384,768]{2,1,0:T(8,128)(2,1)S(1)}, bf16[4,384,768]{2,1,0:T(8,128)(2,1)S(1)}, u32[]{:S(2)}, u32[]{:S(2)}) collective-permute-start(bf16[4,384,768]{2,1,0:T(8,128)(2,1)S(1)} %pad_maximum_fusion.3), channel_id=1, source_target_pairs={{0,2},{2,0},{4,6},{6,4},{8,10},{10,8},{12,14},{14,12},{16,18},{18,... | collective-permute-start | bytes 7077896 | tf_op jit(solution)/shard_map/ppermute | solution.py:555
  211.1 12.8 %collective-permute-start.13 = (bf16[2,1536,768]{2,1,0:T(8,128)(2,1)}, bf16[2,1536,768]{2,1,0:T(8,128)(2,1)}, u32[]{:S(2)}, u32[]{:S(2)}) collective-permute-start(bf16[2,1536,768]{2,1,0:T(8,128)(2,1)} %get-tuple-element.178), channel_id=1, source_target_pairs={{0,2},{2,0},{4,6},{6,4},{8,10},{10,8},{12,14},{14,12},{16,18},{18,... | collective-permute-start | bytes 14155784 | tf_op jit(solution)/shard_map/ppermute | solution.py:555
  229.5 30.1 %collective-permute-start.14 = (bf16[2,768,768]{2,1,0:T(8,128)(2,1)}, bf16[2,768,768]{2,1,0:T(8,128)(2,1)}, u32[]{:S(2)}, u32[]{:S(2)}) collective-permute-start(bf16[2,768,768]{2,1,0:T(8,128)(2,1)} %get-tuple-element.355), channel_id=1, source_target_pairs={{0,4},{2,10},{4,0},{6,14},{8,12},{10,2},{12,8},{14,6},{16,20},{18,... | collective-permute-start | bytes 7077896 | tf_op jit(solution)/shard_map/ppermute | solution.py:555
  268.6 18.2 %collective-permute-start.15 = (bf16[2,384,768]{2,1,0:T(8,128)(2,1)S(1)}, bf16[2,384,768]{2,1,0:T(8,128)(2,1)S(1)}, u32[]{:S(2)}, u32[]{:S(2)}) collective-permute-start(bf16[2,384,768]{2,1,0:T(8,128)(2,1)S(1)} %get-tuple-element.369), channel_id=1, source_target_pairs={{0,8},{2,6},{4,12},{6,2},{8,0},{10,14},{12,4},{14,10},{16,24},{18,... | collective-permute-start | bytes 3538952 | tf_op jit(solution)/shard_map/ppermute | solution.py:555
  275.5 56.9 %copy-start.24 = (bf16[1024,768]{1,0:T(8,128)(2,1)}, bf16[1024,768]{1,0:T(8,128)(2,1)S(1)}, u32[]{:S(2)}) copy-start(bf16[1024,768]{1,0:T(8,128)(2,1)S(1)} %convolution_convert_fusion.1) | copy-start | bytes 4718596
  275.6 12.5 %slice-start.4 = ((s8[6291456]{0:T(1024)(128)(4,1)}), s8[4194304]{0:T(1024)(128)(4,1)S(1)}, s32[]{:S(2)}) async-start(s8[6291456]{0:T(1024)(128)(4,1)} %bitcast.147), calls=%async_computation.4 | async-start | bytes 8388608
  287.8 14.5 %collective-permute-start.16 = (bf16[1,384,768]{2,1,0:T(8,128)(2,1)}, bf16[1,384,768]{2,1,0:T(8,128)(2,1)S(1)}, u32[]{:S(2)}, u32[]{:S(2)}) collective-permute-start(bf16[1,384,768]{2,1,0:T(8,128)(2,1)} %get-tuple-element.408), channel_id=1, source_target_pairs={{0,1},{1,0},{2,3},{3,2},{4,5},{5,4},{6,7},{7,6},{8,9},{9,8},{10,11... | collective-permute-start | bytes 1769480 | tf_op jit(solution)/shard_map/ppermute | solution.py:552
  308.6 19.1 %collective-permute-start.18 = (bf16[2,1536,384]{2,1,0:T(8,128)(2,1)S(1)}, bf16[2,1536,384]{2,1,0:T(8,128)(2,1)S(1)}, u32[]{:S(2)}, u32[]{:S(2)}) collective-permute-start(bf16[2,1536,384]{2,1,0:T(8,128)(2,1)S(1)} %get-tuple-element.205), channel_id=1, source_target_pairs={{0,2},{2,0},{4,6},{6,4},{8,10},{10,8},{12,14},{14,12},{16,18},{18,... | collective-permute-start | bytes 7077896 | tf_op jit(solution)/shard_map/ppermute | solution.py:555
  311.4 105.1 %collective-permute-start.29 = (bf16[16,128,768]{2,1,0:T(8,128)(2,1)}, bf16[16,128,768]{2,1,0:T(8,128)(2,1)}, u32[]{:S(2)}, u32[]{:S(2)}) collective-permute-start(bf16[16,128,768]{2,1,0:T(8,128)(2,1)} %bitcast.26), channel_id=1, source_target_pairs={{0,1},{1,0},{2,3},{3,2},{4,5},{5,4},{6,7},{7,6},{8,9},{9,8},{10,11... | collective-permute-start | bytes 9437192 | tf_op jit(solution)/shard_map/ppermute | solution.py:552
  311.8 15.9 %collective-permute-start.17 = (bf16[1,192,768]{2,1,0:T(8,128)(2,1)S(1)}, bf16[1,192,768]{2,1,0:T(8,128)(2,1)S(1)}, u32[]{:S(2)}, u32[]{:S(2)}) collective-permute-start(bf16[1,192,768]{2,1,0:T(8,128)(2,1)S(1)} %get-tuple-element.449), channel_id=1, source_target_pairs={{0,16},{2,18},{4,20},{6,22},{8,24},{10,26},{12,28},{14,30},{16,0},... | collective-permute-start | bytes 884744 | tf_op jit(solution)/shard_map/ppermute | solution.py:555
  329.4 22.0 %collective-permute-start.20 = (bf16[2,768,384]{2,1,0:T(8,128)(2,1)}, bf16[2,768,384]{2,1,0:T(8,128)(2,1)}, u32[]{:S(2)}, u32[]{:S(2)}) collective-permute-start(bf16[2,768,384]{2,1,0:T(8,128)(2,1)} %get-tuple-element.365), channel_id=1, source_target_pairs={{0,4},{2,10},{4,0},{6,14},{8,12},{10,2},{12,8},{14,6},{16,20},{18,... | collective-permute-start | bytes 3538952 | tf_op jit(solution)/shard_map/ppermute | solution.py:555
  329.4 19.6 %collective-permute-start.19 = (bf16[192,768]{1,0:T(8,128)(2,1)S(1)}, bf16[192,768]{1,0:T(8,128)(2,1)}, u32[]{:S(2)}, u32[]{:S(2)}) collective-permute-start(bf16[192,768]{1,0:T(8,128)(2,1)S(1)} %fusion.60), channel_id=1, source_target_pairs={{0,16},{2,18},{4,20},{6,22},{8,24},{10,26},{12,28},{14,30},{16,0},... | collective-permute-start | bytes 884744 | tf_op jit(solution)/shard_map/ppermute | solution.py:555
  356.5 20.6 %collective-permute-start.21 = (bf16[384,768]{1,0:T(8,128)(2,1)}, bf16[384,768]{1,0:T(8,128)(2,1)}, u32[]{:S(2)}, u32[]{:S(2)}) collective-permute-start(bf16[384,768]{1,0:T(8,128)(2,1)} %pad_maximum_fusion.27), channel_id=1, source_target_pairs={{0,8},{2,6},{4,12},{6,2},{8,0},{10,14},{12,4},{14,10},{16,24},{18,... | collective-permute-start | bytes 1769480 | tf_op jit(solution)/shard_map/ppermute | solution.py:555
  375.2 9.1 %collective-permute-start.22 = (bf16[2,384,384]{2,1,0:T(8,128)(2,1)S(1)}, bf16[2,384,384]{2,1,0:T(8,128)(2,1)S(1)}, u32[]{:S(2)}, u32[]{:S(2)}) collective-permute-start(bf16[2,384,384]{2,1,0:T(8,128)(2,1)S(1)} %get-tuple-element.402), channel_id=1, source_target_pairs={{0,8},{2,6},{4,12},{6,2},{8,0},{10,14},{12,4},{14,10},{16,24},{18,... | collective-permute-start | bytes 1769480 | tf_op jit(solution)/shard_map/ppermute | solution.py:555
  391.7 19.7 %collective-permute-start.24 = (bf16[1,384,384]{2,1,0:T(8,128)(2,1)S(1)}, bf16[1,384,384]{2,1,0:T(8,128)(2,1)S(1)}, u32[]{:S(2)}, u32[]{:S(2)}) collective-permute-start(bf16[1,384,384]{2,1,0:T(8,128)(2,1)S(1)} %get-tuple-element.439), channel_id=1, source_target_pairs={{0,1},{1,0},{2,3},{3,2},{4,5},{5,4},{6,7},{7,6},{8,9},{9,8},{10,11... | collective-permute-start | bytes 884744 | tf_op jit(solution)/shard_map/ppermute | solution.py:552
  393.0 18.4 %collective-permute-start.25 = (bf16[2,1536,384]{2,1,0:T(8,128)(2,1)S(1)}, bf16[2,1536,384]{2,1,0:T(8,128)(2,1)S(1)}, u32[]{:S(2)}, u32[]{:S(2)}) collective-permute-start(bf16[2,1536,384]{2,1,0:T(8,128)(2,1)S(1)} %get-tuple-element.228), channel_id=1, source_target_pairs={{0,2},{2,0},{4,6},{6,4},{8,10},{10,8},{12,14},{14,12},{16,18},{18,... | collective-permute-start | bytes 7077896 | tf_op jit(solution)/shard_map/ppermute | solution.py:555
  395.6 15.4 %collective-permute-start.23 = (bf16[768,768]{1,0:T(8,128)(2,1)S(1)}, bf16[768,768]{1,0:T(8,128)(2,1)S(1)}, u32[]{:S(2)}, u32[]{:S(2)}) collective-permute-start(bf16[768,768]{1,0:T(8,128)(2,1)S(1)} %pad_maximum_fusion.15), channel_id=1, source_target_pairs={{0,4},{2,10},{4,0},{6,14},{8,12},{10,2},{12,8},{14,6},{16,20},{18,... | collective-permute-start | bytes 3538952 | tf_op jit(solution)/shard_map/ppermute | solution.py:555
  411.4 21.8 %collective-permute-start.26 = (bf16[1536,768]{1,0:T(8,128)(2,1)S(1)}, bf16[1536,768]{1,0:T(8,128)(2,1)}, u32[]{:S(2)}, u32[]{:S(2)}) collective-permute-start(bf16[1536,768]{1,0:T(8,128)(2,1)S(1)} %pad_maximum_fusion.7), channel_id=1, source_target_pairs={{0,2},{2,0},{4,6},{6,4},{8,10},{10,8},{12,14},{14,12},{16,18},{18,... | collective-permute-start | bytes 7077896 | tf_op jit(solution)/shard_map/ppermute | solution.py:555
  413.1 20.1 %collective-permute-start.27 = (bf16[1,192,384]{2,1,0:T(8,128)(2,1)}, bf16[1,192,384]{2,1,0:T(8,128)(2,1)}, u32[]{:S(2)}, u32[]{:S(2)}) collective-permute-start(bf16[1,192,384]{2,1,0:T(8,128)(2,1)} %get-tuple-element.463), channel_id=1, source_target_pairs={{0,16},{2,18},{4,20},{6,22},{8,24},{10,26},{12,28},{14,30},{16,0},... | collective-permute-start | bytes 442376 | tf_op jit(solution)/shard_map/ppermute | solution.py:555
  415.7 9.4 %copy-start.77 = (f32[768]{0:T(1024)S(1)}, f32[768]{0:T(1024)}, u32[]{:S(2)}) copy-start(f32[768]{0:T(1024)} %copy-done.76) | copy-start | bytes 9220
  415.7 9.4 %copy-start.79 = (f32[1024]{0:T(1024)S(1)}, f32[1024]{0:T(1024)}, u32[]{:S(2)}) copy-start(f32[1024]{0:T(1024)} %copy-done.78) | copy-start | bytes 12292
  415.7 17.5 %collective-permute-start.28 = (bf16[2,768,384]{2,1,0:T(8,128)(2,1)}, bf16[2,768,384]{2,1,0:T(8,128)(2,1)}, u32[]{:S(2)}, u32[]{:S(2)}) collective-permute-start(bf16[2,768,384]{2,1,0:T(8,128)(2,1)} %get-tuple-element.361), channel_id=1, source_target_pairs={{0,4},{2,10},{4,0},{6,14},{8,12},{10,2},{12,8},{14,6},{16,20},{18,... | collective-permute-start | bytes 3538952 | tf_op jit(solution)/shard_map/ppermute | solution.py:555
  433.2 11.1 %collective-permute-start.32 = (f32[24,768]{1,0:T(8,128)S(1)}, f32[24,768]{1,0:T(8,128)S(1)}, u32[]{:S(2)}, u32[]{:S(2)}) collective-permute-start(f32[24,768]{1,0:T(8,128)S(1)} %select_select_fusion), channel_id=1, source_target_pairs={{0,2},{2,0},{4,6},{6,4},{8,10},{10,8},{12,14},{14,12},{16,18},{18,... | collective-permute-start | bytes 221192 | tf_op jit(solution)/shard_map/ppermute | solution.py:555
  434.5 9.8 %collective-permute-start.30 = (bf16[192,384]{1,0:T(8,128)(2,1)S(1)}, bf16[192,384]{1,0:T(8,128)(2,1)S(1)}, u32[]{:S(2)}, u32[]{:S(2)}) collective-permute-start(bf16[192,384]{1,0:T(8,128)(2,1)S(1)} %fusion.63), channel_id=1, source_target_pairs={{0,16},{2,18},{4,20},{6,22},{8,24},{10,26},{12,28},{14,30},{16,0},... | collective-permute-start | bytes 442376 | tf_op jit(solution)/shard_map/ppermute | solution.py:555
  438.2 9.1 %collective-permute-start.31 = (bf16[2,384,384]{2,1,0:T(8,128)(2,1)S(1)}, bf16[2,384,384]{2,1,0:T(8,128)(2,1)S(1)}, u32[]{:S(2)}, u32[]{:S(2)}) collective-permute-start(bf16[2,384,384]{2,1,0:T(8,128)(2,1)S(1)} %get-tuple-element.392), channel_id=1, source_target_pairs={{0,8},{2,6},{4,12},{6,2},{8,0},{10,14},{12,4},{14,10},{16,24},{18,... | collective-permute-start | bytes 1769480 | tf_op jit(solution)/shard_map/ppermute | solution.py:555
  447.3 6.4 %collective-permute-start.33 = (bf16[384,384]{1,0:T(8,128)(2,1)S(1)}, bf16[384,384]{1,0:T(8,128)(2,1)S(1)}, u32[]{:S(2)}, u32[]{:S(2)}) collective-permute-start(bf16[384,384]{1,0:T(8,128)(2,1)S(1)} %pad_maximum_fusion.33), channel_id=1, source_target_pairs={{0,8},{2,6},{4,12},{6,2},{8,0},{10,14},{12,4},{14,10},{16,24},{18,... | collective-permute-start | bytes 884744 | tf_op jit(solution)/shard_map/ppermute | solution.py:555
  448.0 5.7 %collective-permute-start.35 = (f32[24,768]{1,0:T(8,128)S(1)}, f32[24,768]{1,0:T(8,128)S(1)}, u32[]{:S(2)}, u32[]{:S(2)}) collective-permute-start(f32[24,768]{1,0:T(8,128)S(1)} %add.394), channel_id=1, source_target_pairs={{0,4},{2,6},{4,0},{6,2},{8,12},{10,14},{12,8},{14,10},{16,20},{18,... | collective-permute-start | bytes 221192 | tf_op jit(solution)/shard_map/ppermute | solution.py:555
  448.9 5.9 %collective-permute-start.34 = (bf16[1,384,384]{2,1,0:T(8,128)(2,1)S(1)}, bf16[1,384,384]{2,1,0:T(8,128)(2,1)S(1)}, u32[]{:S(2)}, u32[]{:S(2)}) collective-permute-start(bf16[1,384,384]{2,1,0:T(8,128)(2,1)S(1)} %get-tuple-element.433), channel_id=1, source_target_pairs={{0,1},{1,0},{2,3},{3,2},{4,5},{5,4},{6,7},{7,6},{8,9},{9,8},{10,11... | collective-permute-start | bytes 884744 | tf_op jit(solution)/shard_map/ppermute | solution.py:552
  454.9 12.5 %collective-permute-start.36 = (bf16[768,384]{1,0:T(8,128)(2,1)S(1)}, bf16[768,384]{1,0:T(8,128)(2,1)S(1)}, u32[]{:S(2)}, u32[]{:S(2)}) collective-permute-start(bf16[768,384]{1,0:T(8,128)(2,1)S(1)} %pad_maximum_fusion.28), channel_id=1, source_target_pairs={{0,4},{2,10},{4,0},{6,14},{8,12},{10,2},{12,8},{14,6},{16,20},{18,... | collective-permute-start | bytes 1769480 | tf_op jit(solution)/shard_map/ppermute | solution.py:555
  456.1 11.3 %collective-permute-start.38 = (f32[24,768]{1,0:T(8,128)S(1)}, f32[24,768]{1,0:T(8,128)S(1)}, u32[]{:S(2)}, u32[]{:S(2)}) collective-permute-start(f32[24,768]{1,0:T(8,128)S(1)} %add.397), channel_id=1, source_target_pairs={{0,8},{2,10},{4,12},{6,14},{8,0},{10,2},{12,4},{14,6},{16,24},{18,... | collective-permute-start | bytes 221192 | tf_op jit(solution)/shard_map/ppermute | solution.py:555
  456.4 11.2 %collective-permute-start.37 = (bf16[1,192,384]{2,1,0:T(8,128)(2,1)S(1)}, bf16[1,192,384]{2,1,0:T(8,128)(2,1)S(1)}, u32[]{:S(2)}, u32[]{:S(2)}) collective-permute-start(bf16[1,192,384]{2,1,0:T(8,128)(2,1)S(1)} %get-tuple-element.459), channel_id=1, source_target_pairs={{0,16},{2,18},{4,20},{6,22},{8,24},{10,26},{12,28},{14,30},{16,0},... | collective-permute-start | bytes 442376 | tf_op jit(solution)/shard_map/ppermute | solution.py:555
  467.6 15.8 %collective-permute-start.39 = (bf16[1536,384]{1,0:T(8,128)(2,1)S(1)}, bf16[1536,384]{1,0:T(8,128)(2,1)S(1)}, u32[]{:S(2)}, u32[]{:S(2)}) collective-permute-start(bf16[1536,384]{1,0:T(8,128)(2,1)S(1)} %pad_maximum_fusion.16), channel_id=1, source_target_pairs={{0,2},{2,0},{4,6},{6,4},{8,10},{10,8},{12,14},{14,12},{16,18},{18,... | collective-permute-start | bytes 3538952 | tf_op jit(solution)/shard_map/ppermute | solution.py:555
  470.4 12.9 %collective-permute-start.40 = (bf16[192,384]{1,0:T(8,128)(2,1)S(1)}, bf16[192,384]{1,0:T(8,128)(2,1)S(1)}, u32[]{:S(2)}, u32[]{:S(2)}) collective-permute-start(bf16[192,384]{1,0:T(8,128)(2,1)S(1)} %fusion.64), channel_id=1, source_target_pairs={{0,16},{2,18},{4,20},{6,22},{8,24},{10,26},{12,28},{14,30},{16,0},... | collective-permute-start | bytes 442376 | tf_op jit(solution)/shard_map/ppermute | solution.py:555
  471.3 11.9 %collective-permute-start.41 = (f32[24,768]{1,0:T(8,128)S(1)}, f32[24,768]{1,0:T(8,128)S(1)}, u32[]{:S(2)}, u32[]{:S(2)}) collective-permute-start(f32[24,768]{1,0:T(8,128)S(1)} %add.400), channel_id=1, source_target_pairs={{0,16},{2,18},{4,20},{6,22},{8,24},{10,26},{12,28},{14,30},{16,0},... | collective-permute-start | bytes 221192 | tf_op jit(solution)/shard_map/ppermute | solution.py:555
  484.9 3.3 collective-permute-start.43
  485.3 5.9 %collective-permute-start.42 = (bf16[384,384]{1,0:T(8,128)(2,1)S(1)}, bf16[384,384]{1,0:T(8,128)(2,1)S(1)}, u32[]{:S(2)}, u32[]{:S(2)}) collective-permute-start(bf16[384,384]{1,0:T(8,128)(2,1)S(1)} %pad_maximum_fusion.34), channel_id=1, source_target_pairs={{0,8},{2,6},{4,12},{6,2},{8,0},{10,14},{12,4},{14,10},{16,24},{18,... | collective-permute-start | bytes 884744 | tf_op jit(solution)/shard_map/ppermute | solution.py:555
  491.3 13.6 %slice-start.8 = ((f32[24,768]{1,0:T(8,128)}), f32[4,768]{1,0:T(4,128)S(1)}, s32[]{:S(2)}) async-start(f32[24,768]{1,0:T(8,128)} %add.403), calls=%async_computation.8 | async-start | bytes 24576 | tf_op jit(solution)/shard_map/slice | solution.py:863
  491.3 9.1 %collective-permute-start.44 = (bf16[768,384]{1,0:T(8,128)(2,1)S(1)}, bf16[768,384]{1,0:T(8,128)(2,1)S(1)}, u32[]{:S(2)}, u32[]{:S(2)}) collective-permute-start(bf16[768,384]{1,0:T(8,128)(2,1)S(1)} %pad_maximum_fusion.29), channel_id=1, source_target_pairs={{0,4},{2,10},{4,0},{6,14},{8,12},{10,2},{12,8},{14,6},{16,20},{18,... | collective-permute-start | bytes 1769480 | tf_op jit(solution)/shard_map/ppermute | solution.py:555
  500.6 13.0 %collective-permute-start.45 = (bf16[1536,384]{1,0:T(8,128)(2,1)S(1)}, bf16[1536,384]{1,0:T(8,128)(2,1)}, u32[]{:S(2)}, u32[]{:S(2)}) collective-permute-start(bf16[1536,384]{1,0:T(8,128)(2,1)S(1)} %pad_maximum_fusion.17), channel_id=1, source_target_pairs={{0,2},{2,0},{4,6},{6,4},{8,10},{10,8},{12,14},{14,12},{16,18},{18,... | collective-permute-start | bytes 3538952 | tf_op jit(solution)/shard_map/ppermute | solution.py:555
  (109 other events, 399.0 us)

commit v3 on v2

--- a/solution.py
+++ b/solution.py
@@ -794,7 +794,13 @@
     cross = sum_flow(*g_cross)
     cross.next()
     n_own = mm(d_own, kv_w, NT).reshape(spans, -1, d)
-    n_own, g_wo, f = advance([fc, cross], n_own, g_wo, f)
+    wide = lambda x: jnp.sum(x.astype(F32), axis=0)
+    cqs, cvs = wide(d_cq), wide(d_own[:, d:]) + wide(d_oth[:, d:])
+    early = jnp.concatenate(
+        [gb_low[0], gb_high[0], wide(cot), wide(d_r1), wide(d_r2), gain2, gain3, shift2, shift3]
+        + [link.joined(x[:hc], x[hc:], half) for x in (cqs, cvs)]
+    )
+    n_own, g_wo, f, early = advance([fc, cross], n_own, g_wo, f, early)
     dq_oth = self_bwd(p_oth, f[:, hc:], ctx_oth, lse_oth, length)
     dq_oth, f = advance([fc, cross], dq_oth, f)
     dq_own = self_bwd(p_own, f[:, :hc], ctx_own, lse_own, length)
@@ -808,29 +814,19 @@
     own.next()
     flat = lambda x: jnp.concatenate([x[0], x[1], x[2]], axis=1)
     d_h1 = mm(flat(dq_own), qkv_own, NT) + mm(flat(dq_oth), qkv_oth, NT)
-    d_h1, n_own = advance([fc, cross, own], d_h1, n_own)
+    d_h1, n_own, early = advance([own], d_h1, n_own, early)
+    nbr_grad = place_blocks(order_of(keep, send), n_own, n_back)
     back1, gain1, shift1 = norm_back(tok, gains[0], d_h1)
     tokens_grad = d_r1 + back1
 
-    wide = lambda x: jnp.sum(x.astype(F32), axis=0)
-    natural = [
-        gb_low[0], gb_high[0], wide(cot), wide(d_r1), wide(d_r2), gain1, gain2, gain3, shift1, shift2, shift3,
+    late = [gain1, shift1] + [
+        link.joined(wide(x), wide(y), half) for x, y in ((dq_own[0], dq_oth[0]), (dq_own[2], dq_oth[2]))
     ]
-    relative = [wide(dq_own[0]), wide(dq_oth[0]), wide(dq_own[2]), wide(dq_oth[2])]
-    cqs, cvs = wide(d_cq), wide(d_own[:, d:]) + wide(d_oth[:, d:])
-    relative += [cqs[:hc], cqs[hc:], cvs[:hc], cvs[hc:]]
-    for i in range(0, len(relative), 2):
-        natural.append(link.joined(relative[i], relative[i + 1], half))
-    natural = [x[i : i + d] for x in natural for i in range(0, x.shape[0], d)]
-    height = len(natural) + -len(natural) % 8
-    row = iota((height, d), 0)
-    table = jnp.zeros((height, d), F32)
-    for i, x in enumerate(natural):
-        table = jnp.where(row == i, x[None], table)
-    natural = table
+    natural = jnp.concatenate([early] + late)
+    pad = -natural.shape[0] % 1024
+    natural = jnp.concatenate([natural, jnp.zeros((pad,), F32)]).reshape(-1, 128)
     every = [lambda x, b=b: x + link.across(x, (b, b)) for b in range(link.bits)]
     every.append(lambda x: x + link.other(x))
-    nbr_grad = place_blocks(order_of(keep, send), n_own, n_back)
     tokens_grad, natural, nbr_grad = advance([fc, cross, own], tokens_grad, natural, nbr_grad)
     while fc.todo:
         advance([fc, cross, own])
@@ -854,28 +850,31 @@
     cross_kv_grad = jnp.stack([s_kv[:d], s_kv[d:]], axis=1).astype(F32)
     cross_q_grad = s_rest[:d].astype(F32)
     co_grad = wide_rows(s_rest[d:], 2).astype(F32)
-    while own.todo or sums.todo:
+    while len(own.todo) > 1 or sums.todo:
         cross_kv_grad, cross_q_grad, co_grad = advance([own, sums], cross_kv_grad, cross_q_grad, co_grad)
+    total = sums.x.reshape(-1)
+    gb_in = lax.dynamic_slice_in_dim(total[:ff], half * ffh, ffh)
+    rest = lax.dynamic_slice_in_dim(total[ff : ff + 13 * d].reshape(-1, d), half * hc, hc, 1)
+    while own.todo:
+        gb_in, rest = advance([own], gb_in, rest)
     s_qk, s_vw = link.pair(own.x)
     qkv_grad = jnp.stack([s_qk[:d], s_qk[d:], s_vw[:d]], axis=1).astype(F32)
     wo_grad = wide_rows(s_vw[d:], 2).astype(F32)
-    sums = sums.x
-    gb_in = lax.dynamic_slice_in_dim(sums[: ff // d].reshape(-1), half * ffh, ffh)
-    rest = lax.dynamic_slice_in_dim(sums[ff // d : ff // d + 13], half * hc, hc, 1)
+    pick = lambda *rows: jnp.stack([rest[i] for i in rows])
     return (
         block_out,
         tokens_grad,
         nbr_grad,
         qkv_grad,
-        rest[9:11],
+        rest[11:13],
         wo_grad,
         cross_q_grad,
         cross_kv_grad,
-        rest[11:13],
+        rest[7:9],
         co_grad,
         rest[1:3],
-        rest[3:6],
-        rest[6:9],
+        pick(9, 3, 4),
+        pick(10, 5, 6),
         fc_in_grad,
         gb_in,
         fc_out_grad,

time: 528 us -> 511 us (0.968)
  other arithmetic: 87.1 us -> 79.7 us
  local copies, waits for them, and re-layouts: 61.6 us -> 54.9 us
    ppermute x35, waiting for transfers between devices: 62.7 us -> 57.1 us  [across(): lax.ppermute(x, 'dp', [(i, i ^ 1 << step[i & 1]) for i in range(self.dp)])]
    unnamed x263 -> x235, local copies, waits for them, and re-layouts: 23.4 us -> 22.3 us
    select_n x26 -> x22, other arithmetic: 14.3 us -> 14.7 us  [joined(): jnp.where(first, mine, theirs)]
  transfers between devices with their start and end apart: 46 -> 46, of which waited for: 19 -> 24; matrix products, arithmetic and copies ran while one was open for 36% -> 35% of each run, Pallas kernels for 19% -> 20%
where the time goes in v3:
time: 511 us; the launch traced here: 503 us
  Pallas kernels  142 us (28%)
  matrix products  86 us (17%)
  waiting for transfers between devices  84.1 us (16%)
  other arithmetic  79.7 us (16%)
  local copies, waits for them, and re-layouts  54.9 us (11%)
  starting transfers between devices  52.8 us (10%)
    dot_general x27, matrix products, mm(): return lax.dot_general(a, b, dims, preferred_element_type=F32)  86 us
    ppermute x35, waiting for transfers between devices, across(): lax.ppermute(x, 'dp', [(i, i ^ 1 << step[i & 1]) for i in range(self.dp)])  57.1 us
    ppermute x35, starting transfers between devices, across(): lax.ppermute(x, 'dp', [(i, i ^ 1 << step[i & 1]) for i in range(self.dp)])  43.3 us
    pallas_call x1, Pallas kernels, feed(): pl.pallas_call(feed_kernel, grid_spec=pltpu.PrefetchScalarGridSpec(num_sc...  41.7 us
    pallas_call x2, Pallas kernels, self_bwd(): pl.pallas_call(self_bwd_kernel, grid_spec=pltpu.PrefetchScalarGridSpec(nu...  30.6 us
    ppermute x11, waiting for transfers between devices, other(): return lax.ppermute(x, 'tp', self.swap)  27 us
    unnamed x235, local copies, waits for them, and re-layouts  22.3 us
    pallas_call x2, Pallas kernels, self_fwd(): pl.pallas_call(self_fwd_kernel, grid_spec=pltpu.PrefetchScalarGridSpec(nu...  21.7 us
  transfers between devices with their start and end apart: 46, of which 24 were waited for; matrix products, arithmetic and copies ran while one was open for 35% of the time, Pallas kernels for 20%

profile of v3, /device:TPU:1, one launch (start us, length us, event | category | flops | bytes accessed | tf_op | source)
XLA Modules:
  0.0 502.6 jit_solution(11205601680595652054)
XLA Ops:
  2.1 3.0 concatenate.191
  5.1 2.1 collective-permute-start.1
  7.2 2.5 copy.52
  9.7 2.6 copy.41
  12.4 2.4 copy.42.qkv
  15.4 3.6 shard_map.314
  22.8 6.7 %shard_map.316 = (bf16[16,128,768]{2,1,0:T(8,128)(2,1)}, bf16[16,128,768]{2,1,0:T(8,128)(2,1)}) custom-call(s32[16]{0:T(128)} %get-tuple-element.480.keep_ref, s32[16]{0:T(128)} %get-tuple-element.479.send_ref, bf16[32,128,768]{2,1,0:T(8,128)(2,1)} %blocks_ref.1), custom_call_target="tpu_custom_call" | custom-call | bytes 12582912 | tf_op jit(solution)/shard_map/pallas_call | solution.py:313
  30.9 3.7 multiply_convert_fusion.1.q_ref.k_ref.v_ref
  34.6 10.8 %shard_map.315 = (bf16[1024,384]{1,0:T(8,128)(2,1)}, f32[1024,384]{1,0:T(8,128)}) custom-call(s32[1]{0:T(128)} %bitcast.4.len_ref, bf16[1024,1152]{1,0:T(8,128)(2,1)} %multiply_convert_fusion.1.q_ref.k_ref.v_ref, bf16[1024,1152]{1,0:T(8,128)(2,1)} %multiply_convert_fusion.1.q_ref.k_ref.v_ref, bf16[1024,1152]{1,0:T(8,128)(2,1)} %multiply_convert_fusion.1.q_ref.k_ref.v_ref), custom_call_target="tpu_custom_call" | custom-call | flops 3221225472 | bytes 3145728 | tf_op jit(solution)/shard_map/pallas_call | solution.py:89
  45.4 2.1 collective-permute-done
  50.6 2.7 slice.447
  53.5 2.7 collective-permute-done.4
  59.3 3.6 multiply_convert_fusion.q_ref.k_ref.v_ref
  64.2 10.9 %shard_map.317 = (bf16[1024,384]{1,0:T(8,128)(2,1)}, f32[1024,384]{1,0:T(8,128)}) custom-call(s32[1]{0:T(128)} %bitcast.4.len_ref, bf16[1024,1152]{1,0:T(8,128)(2,1)} %multiply_convert_fusion.q_ref.k_ref.v_ref, bf16[1024,1152]{1,0:T(8,128)(2,1)} %multiply_convert_fusion.q_ref.k_ref.v_ref, bf16[1024,1152]{1,0:T(8,128)(2,1)} %multiply_convert_fusion.q_ref.k_ref.v_ref), custom_call_target="tpu_custom_call" | custom-call | flops 3221225472 | bytes 3145728 | tf_op jit(solution)/shard_map/pallas_call | solution.py:89
  77.8 11.6 %collective-permute-done.6 = bf16[8,128,768]{2,1,0:T(8,128)(2,1)} collective-permute-done((bf16[8,128,768]{2,1,0:T(8,128)(2,1)}, bf16[8,128,768]{2,1,0:T(8,128)(2,1)}, u32[]{:S(2)}, u32[]{:S(2)}) %collective-permute-start.6) | collective-permute-done | bytes 1572896 | tf_op jit(solution)/shard_map/ppermute | solution.py:552
  96.9 2.7 broadcast_select_fusion.9
  107.3 6.0 %add_convert_fusion.own_ref = bf16[2048,1536]{1,0:T(8,128)(2,1)S(1)} fusion(bf16[2048,768]{1,0:T(8,128)(2,1)S(1)} %bitcast.174, f32[1536]{0:T(1024)S(1)} %pad_maximum_fusion.37, bf16[768,384]{1,0:T(8,128)(2,1)S(1)} %bitcast.157, bf16[768,384]{1,0:T(8,128)(2,1)S(1)} %copy-done.59, bf16[768,384]{1,0:T(8,128)(2,1)S(1)} %bitcast.152, ...), kind=kOutput, calls=%fused_computation | convolution fusion | flops 4847566848 | bytes 11802624 | tf_op jit(solution)/shard_map/dot_general | solution.py:28
  116.0 3.0 fusion.91
  119.0 5.8 %add_convert_fusion.2.oth_ref.oth_a_ref = bf16[1024,1536]{1,0:T(8,128)(2,1)} fusion(bf16[1024,768]{1,0:T(8,128)(2,1)} %bitcast.17, f32[1536]{0:T(1024)S(1)} %pad_maximum_fusion.37, bf16[768,384]{1,0:T(8,128)(2,1)S(1)} %bitcast.158, bf16[768,384]{1,0:T(8,128)(2,1)S(1)} %copy-done.59, bf16[768,384]{1,0:T(8,128)(2,1)S(1)} %bitcast.153, ...), kind=kOutput, calls=%fused_computation.4 | convolution fusion | flops 2428502016 | bytes 7084032 | tf_op jit(solution)/shard_map/dot_general | solution.py:28
  126.1 5.8 %shard_map.318 = bf16[512,768]{1,0:T(8,128)(2,1)} custom-call(bf16[512,768]{1,0:T(8,128)(2,1)} %get-tuple-element.401.q_ref, bf16[1024,1536]{1,0:T(8,128)(2,1)} %get-tuple-element.341.own_ref, bf16[1024,1536]{1,0:T(8,128)(2,1)} %add_convert_fusion.2.oth_ref.oth_a_ref), custom_call_target="tpu_custom_call" | custom-call | flops 1610612736 | bytes 8000000 | tf_op jit(solution)/shard_map/pallas_call | solution.py:224
  133.4 9.2 %collective-permute-done.10 = bf16[8,128,768]{2,1,0:T(8,128)(2,1)} collective-permute-done((bf16[8,128,768]{2,1,0:T(8,128)(2,1)S(1)}, bf16[8,128,768]{2,1,0:T(8,128)(2,1)}, u32[]{:S(2)}, u32[]{:S(2)}) %collective-permute-start.10) | collective-permute-done | bytes 1572896 | tf_op jit(solution)/shard_map/ppermute | solution.py:552
  143.7 5.8 %add_convert_fusion.1.oth_ref.oth_b_ref = bf16[1024,1536]{1,0:T(8,128)(2,1)} fusion(bf16[1024,768]{1,0:T(8,128)(2,1)} %bitcast.18, f32[1536]{0:T(1024)S(1)} %pad_maximum_fusion.37, bf16[768,384]{1,0:T(8,128)(2,1)S(1)} %bitcast.159, bf16[768,384]{1,0:T(8,128)(2,1)S(1)} %copy-done.60, bf16[768,384]{1,0:T(8,128)(2,1)S(1)} %bitcast.154, ...), kind=kOutput, calls=%fused_computation.3 | convolution fusion | flops 2428502016 | bytes 7084032 | tf_op jit(solution)/shard_map/dot_general | solution.py:28
  149.5 5.9 %shard_map.319 = bf16[512,768]{1,0:T(8,128)(2,1)} custom-call(bf16[512,768]{1,0:T(8,128)(2,1)} %get-tuple-element.402.q_ref, bf16[1024,1536]{1,0:T(8,128)(2,1)} %get-tuple-element.342.own_ref, bf16[1024,1536]{1,0:T(8,128)(2,1)} %add_convert_fusion.1.oth_ref.oth_b_ref), custom_call_target="tpu_custom_call" | custom-call | flops 1610612736 | bytes 8000000 | tf_op jit(solution)/shard_map/pallas_call | solution.py:224
  155.4 2.6 collective-permute-done.11
  169.3 41.7 %shard_map.320 = (bf16[1024,768]{1,0:T(8,128)(2,1)}, f32[1024,768]{1,0:T(8,128)}, bf16[2,1536,768]{2,1,0:T(8,128)(2,1)}, bf16[2,1536,768]{2,1,0:T(8,128)(2,1)}, f32[8,1536]{1,0:T(8,128)}, /*index=5*/f32[8,1536]{1,0:T(8,128)}) custom-call(s32[2]{0:T(128)} %get-tuple-element.486.half_ref, bf16[1024,768]{1,0:T(8,128)(2,1)} %pad_maximum_fusion.11.h_ref, ...), custom_call_target="tpu_custom_call" | custom-call | flops 28991029248 | bytes 18874368 | tf_op jit(solution)/shard_map/pallas_call | solution.py:488
  212.6 2.2 slice_select_fusion.1
  215.4 2.4 multiply_reduce_fusion
  217.8 2.3 fusion.89
  221.1 2.7 convolution_convert_fusion.2
  223.8 5.7 %add_convert_fusion.4 = (bf16[2,768,768]{2,1,0:T(8,128)(2,1)}, bf16[2,768,768]{2,1,0:T(8,128)(2,1)}) fusion(bf16[2,1536,768]{2,1,0:T(8,128)(2,1)} %collective-permute-done.13, s32[]{:T(128)S(6)} %select_n.491, bf16[2,1536,768]{2,1,0:T(8,128)(2,1)S(1)} %bitcast.144, s32[]{:T(128)S(6)} %select_n.490), kind=kLoop, calls=%fused_computation.9 | loop fusion | flops 9437184 | bytes 14155784 | tf_op jit(solution)/shard_map/convert_element_type | solution.py:602
  235.1 2.5 convolution_convert_fusion.5
  237.6 17.5 %shard_map.321 = (bf16[1024,768]{1,0:T(8,128)(2,1)}, bf16[2048,1536]{1,0:T(8,128)(2,1)}, bf16[2048,1536]{1,0:T(8,128)(2,1)}) custom-call(bf16[1024,768]{1,0:T(8,128)(2,1)} %copy-done.18, bf16[2048,1536]{1,0:T(8,128)(2,1)} %copy-done.17, bf16[1024,1536]{1,0:T(8,128)(2,1)} %add_convert_fusion.2.oth_ref.oth_a_ref, ...), custom_call_target="tpu_custom_call" | custom-call | flops 8053063680 | bytes 32000000 | tf_op jit(solution)/shard_map/pallas_call | solution.py:270
  255.1 2.7 collective-permute-done.14
  260.4 2.3 multiply_reduce_fusion.1
  263.3 4.2 fusion.21
  269.2 3.2 add_convert_fusion.12
  278.0 6.4 %convolution_convert_fusion = bf16[2048,768]{1,0:T(8,128)(2,1)} fusion(bf16[2048,1536]{1,0:T(8,128)(2,1)S(1)} %bitcast.140, bf16[768,384]{1,0:T(8,128)(2,1)S(1)} %bitcast.160, bf16[768,384]{1,0:T(8,128)(2,1)S(1)} %copy-done.61, bf16[768,384]{1,0:T(8,128)(2,1)S(1)} %bitcast.155, bf16[768,384]{1,0:T(8,128)(2,1)S(1)} %copy-done.64), kind=kOutput, calls=%fused_computation.29 | convolution fusion | flops 4842848256 | bytes 11796480 | tf_op jit(solution)/shard_map/dot_general | solution.py:28
  284.5 3.5 collective-permute-done.15
  289.4 7.3 %fusion.104 = f32[768,1536]{1,0:T(8,128)} fusion(bf16[2048,768]{1,0:T(8,128)(2,1)S(1)} %bitcast.175, bf16[2048,1536]{1,0:T(8,128)(2,1)S(1)} %bitcast.151), kind=kOutput, calls=%fused_computation.376 | convolution fusion | flops 4831838208 | bytes 14155776 | tf_op jit(solution)/shard_map/dot_general | solution.py:28
  297.9 5.3 %add_convert_fusion.3 = bf16[768,1536]{1,0:T(8,128)(2,1)S(1)} fusion(f32[768,1536]{1,0:T(8,128)} %fusion.104, f32[768,1536]{1,0:T(8,128)S(1)} %fusion.21, bf16[1024,768]{1,0:T(8,128)(2,1)} %bitcast.18, bf16[2048,1536]{1,0:T(8,128)(2,1)S(1)} %bitcast.140), kind=kOutput, calls=%fused_computation.8 | convolution fusion | flops 2419458048 | bytes 16515072 | tf_op jit(solution)/shard_map/dot_general | solution.py:28
  304.7 2.5 convolution_convert_fusion.3
  307.5 2.4 collective-permute-start.17
  312.5 4.4 collective-permute-start.18
  317.2 7.0 %fusion.88 = f32[2048,768]{1,0:T(8,128)} fusion(bf16[2048,1536]{1,0:T(8,128)(2,1)S(1)} %bitcast.151, bf16[768,384]{1,0:T(8,128)(2,1)S(1)} %bitcast.161, bf16[768,384]{1,0:T(8,128)(2,1)S(1)} %copy-done.61, bf16[768,384]{1,0:T(8,128)(2,1)S(1)} %bitcast.156, bf16[768,384]{1,0:T(8,128)(2,1)S(1)} %copy-done.64), kind=kOutput, calls=%fused_computation.360 | convolution fusion | flops 4841275392 | bytes 14942208 | tf_op jit(solution)/shard_map/dot_general | solution.py:28
  327.6 15.3 %shard_map.322 = bf16[3,1024,384]{2,1,0:T(8,128)(2,1)} custom-call(s32[1]{0:T(128)} %bitcast.4.len_ref, bf16[1024,1152]{1,0:T(8,128)(2,1)} %multiply_convert_fusion.q_ref.k_ref.v_ref, bf16[1024,1152]{1,0:T(8,128)(2,1)} %multiply_convert_fusion.q_ref.k_ref.v_ref, bf16[1024,1152]{1,0:T(8,128)(2,1)} %multiply_convert_fusion.q_ref.k_ref.v_ref, ...), custom_call_target="tpu_custom_call" | custom-call | flops 8053063680 | bytes 6291456 | tf_op jit(solution)/shard_map/pallas_call | solution.py:160
  342.9 2.8 collective-permute-done.19
  347.9 3.4 convolution_convert_fusion.6
  355.0 15.3 %shard_map.323 = bf16[3,1024,384]{2,1,0:T(8,128)(2,1)} custom-call(s32[1]{0:T(128)} %bitcast.4.len_ref, bf16[1024,1152]{1,0:T(8,128)(2,1)} %multiply_convert_fusion.1.q_ref.k_ref.v_ref, bf16[1024,1152]{1,0:T(8,128)(2,1)} %multiply_convert_fusion.1.q_ref.k_ref.v_ref, bf16[1024,1152]{1,0:T(8,128)(2,1)} %multiply_convert_fusion.1.q_ref.k_ref.v_ref, ...), custom_call_target="tpu_custom_call" | custom-call | flops 8053063680 | bytes 6291456 | tf_op jit(solution)/shard_map/pallas_call | solution.py:160
  375.4 5.8 %collective-permute-done.22 = bf16[2,384,384]{2,1,0:T(8,128)(2,1)S(1)} collective-permute-done((bf16[2,384,384]{2,1,0:T(8,128)(2,1)S(1)}, bf16[2,384,384]{2,1,0:T(8,128)(2,1)S(1)}, u32[]{:S(2)}, u32[]{:S(2)}) %collective-permute-start.22) | collective-permute-done | bytes 589856 | tf_op jit(solution)/shard_map/ppermute | solution.py:555
  389.6 2.2 fusion.25
  393.8 2.2 fusion.37
  396.0 7.4 %collective-permute-done.23 = bf16[768,768]{1,0:T(8,128)(2,1)S(1)} collective-permute-done((bf16[768,768]{1,0:T(8,128)(2,1)S(1)}, bf16[768,768]{1,0:T(8,128)(2,1)S(1)}, u32[]{:S(2)}, u32[]{:S(2)}) %collective-permute-start.23) | collective-permute-done | bytes 1179680 | tf_op jit(solution)/shard_map/ppermute | solution.py:555
  408.6 8.5 %shard_map.324 = f32[32,128,768]{2,1,0:T(8,128)} custom-call(s32[32]{0:T(128)} %pad_add_fusion.2.order_ref, f32[16,128,768]{2,1,0:T(8,128)} %bitcast.141, bf16[16,128,768]{2,1,0:T(8,128)(2,1)} %collective-permute-done.27.theirs_ref), custom_call_target="tpu_custom_call" | custom-call | bytes 12582912 | tf_op jit(solution)/shard_map/pallas_call | solution.py:387
  417.2 4.9 fusion.11
  429.2 2.8 convert_element_type.495
  432.0 2.6 collective-permute-done.28
  436.7 2.4 collective-permute-start.32
  440.5 2.5 convert_element_type.505
  448.6 2.2 collective-permute-done.35
  454.8 10.6 %collective-permute-done.40 = f32[104,128]{1,0:T(8,128)S(1)} collective-permute-done((f32[104,128]{1,0:T(8,128)S(1)}, f32[104,128]{1,0:T(8,128)S(1)}, u32[]{:S(2)}, u32[]{:S(2)}) %collective-permute-start.40) | collective-permute-done | bytes 53280 | tf_op jit(solution)/shard_map/ppermute | solution.py:555
  466.4 6.6 %collective-permute-start.41 = (bf16[1536,384]{1,0:T(8,128)(2,1)S(1)}, bf16[1536,384]{1,0:T(8,128)(2,1)S(1)}, u32[]{:S(2)}, u32[]{:S(2)}) collective-permute-start(bf16[1536,384]{1,0:T(8,128)(2,1)S(1)} %pad_maximum_fusion.16), channel_id=1, source_target_pairs={{0,2},{2,0},{4,6},{6,4},{8,10},{10,8},{12,14},{14,12},{16,18},{18,... | collective-permute-start | bytes 3538952 | tf_op jit(solution)/shard_map/ppermute | solution.py:555
  475.2 2.2 collective-permute-done.43
  482.3 6.5 %collective-permute-done.44 = bf16[768,384]{1,0:T(8,128)(2,1)S(1)} collective-permute-done((bf16[768,384]{1,0:T(8,128)(2,1)S(1)}, bf16[768,384]{1,0:T(8,128)(2,1)S(1)}, u32[]{:S(2)}, u32[]{:S(2)}) %collective-permute-start.44) | collective-permute-done | bytes 589856 | tf_op jit(solution)/shard_map/ppermute | solution.py:555
  490.7 3.2 copy.47
  (493 shorter events, 144.1 us)
Async XLA Ops:
  0.7 21.5 %copy-start = (s32[1,2]{1,0:T(1,128)S(1)}, s32[1,2]{1,0:T(1,128)}, u32[]{:S(2)}) copy-start(s32[1,2]{1,0:T(1,128)} %param.22) | copy-start | bytes 28
  5.1 24.4 %collective-permute-start.1 = (bf16[17,384]{1,0:T(8,128)(2,1)S(1)}, bf16[17,384]{1,0:T(8,128)(2,1)S(1)}, u32[]{:S(2)}, u32[]{:S(2)}) collective-permute-start(bf16[17,384]{1,0:T(8,128)(2,1)S(1)} %concatenate.191), channel_id=1, source_target_pairs={{0,1},{1,0},{2,3},{3,2},{4,5},{5,4},{6,7},{7,6},{8,9},{9,8},{10,11... | collective-permute-start | bytes 39176 | tf_op jit(solution)/shard_map/ppermute | solution.py:552
  12.4 18.6 %copy-start.13 = (bf16[768,3,384]{0,2,1:T(8,128)(2,1)}, bf16[768,3,384]{0,2,1:T(8,128)(2,1)S(1)}, u32[]{:S(2)}) copy-start(bf16[768,3,384]{0,2,1:T(8,128)(2,1)S(1)} %copy.41) | copy-start | bytes 5308420
  19.0 26.4 %collective-permute-start.2 = (bf16[480,384]{1,0:T(8,128)(2,1)}, bf16[480,384]{1,0:T(8,128)(2,1)}, u32[]{:S(2)}, u32[]{:S(2)}) collective-permute-start(bf16[480,384]{1,0:T(8,128)(2,1)} %get-tuple-element.145), channel_id=1, source_target_pairs={{0,1},{1,0},{2,3},{3,2},{4,5},{5,4},{6,7},{7,6},{8,9},{9,8},{10,11... | collective-permute-start | bytes 1105928 | tf_op jit(solution)/shard_map/ppermute | solution.py:552
  19.1 28.4 %collective-permute-start = (bf16[384,1152]{1,0:T(8,128)(2,1)}, bf16[384,1152]{1,0:T(8,128)(2,1)}, u32[]{:S(2)}, u32[]{:S(2)}) collective-permute-start(bf16[384,1152]{1,0:T(8,128)(2,1)} %get-tuple-element.143), channel_id=1, source_target_pairs={{0,1},{1,0},{2,3},{3,2},{4,5},{5,4},{6,7},{7,6},{8,9},{9,8},{10,11... | collective-permute-start | bytes 2654216 | tf_op jit(solution)/shard_map/ppermute | solution.py:552
  20.9 9.4 %copy-start.75 = (f32[1024]{0:T(1024)}, f32[1024]{0:T(1024)S(1)}, u32[]{:S(2)}) copy-start(f32[1024]{0:T(1024)S(1)} %broadcast_multiply_fusion.8) | copy-start | bytes 12292
  47.5 9.9 %collective-permute-start.3 = (bf16[384,1152]{1,0:T(8,128)(2,1)}, bf16[384,1152]{1,0:T(8,128)(2,1)}, u32[]{:S(2)}, u32[]{:S(2)}) collective-permute-start(bf16[384,1152]{1,0:T(8,128)(2,1)} %collective-permute-done), channel_id=1, source_target_pairs={{0,2},{2,0},{4,6},{6,4},{8,10},{10,8},{12,14},{14,12},{16,18},{18,... | collective-permute-start | bytes 2654216 | tf_op jit(solution)/shard_map/ppermute | solution.py:555
  49.4 6.9 %collective-permute-start.4 = (bf16[1,480,384]{2,1,0:T(8,128)(2,1)}, bf16[1,480,384]{2,1,0:T(8,128)(2,1)S(1)}, u32[]{:S(2)}, u32[]{:S(2)}) collective-permute-start(bf16[1,480,384]{2,1,0:T(8,128)(2,1)} %bitcast.5), channel_id=1, source_target_pairs={{0,4},{2,10},{4,0},{6,14},{8,12},{10,2},{12,8},{14,6},{16,20},{18,... | collective-permute-start | bytes 1105928 | tf_op jit(solution)/shard_map/ppermute | solution.py:555
  53.3 36.1 %collective-permute-start.6 = (bf16[8,128,768]{2,1,0:T(8,128)(2,1)}, bf16[8,128,768]{2,1,0:T(8,128)(2,1)}, u32[]{:S(2)}, u32[]{:S(2)}) collective-permute-start(bf16[8,128,768]{2,1,0:T(8,128)(2,1)} %slice.447), channel_id=1, source_target_pairs={{0,1},{1,0},{2,3},{3,2},{4,5},{5,4},{6,7},{7,6},{8,9},{9,8},{10,11... | collective-permute-start | bytes 4718600 | tf_op jit(solution)/shard_map/ppermute | solution.py:552
  62.9 12.2 %collective-permute-start.5 = (bf16[2,480,384]{2,1,0:T(8,128)(2,1)S(1)}, bf16[2,480,384]{2,1,0:T(8,128)(2,1)}, u32[]{:S(2)}, u32[]{:S(2)}) collective-permute-start(bf16[2,480,384]{2,1,0:T(8,128)(2,1)S(1)} %pad_maximum_fusion.22), channel_id=1, source_target_pairs={{0,8},{2,6},{4,12},{6,2},{8,0},{10,14},{12,4},{14,10},{16,24},{18,... | collective-permute-start | bytes 2211848 | tf_op jit(solution)/shard_map/ppermute | solution.py:555
  75.1 15.3 %copy-start.11 = (bf16[768,2,384]{2,1,0:T(2,128)(2,1)S(1)}, bf16[768,2,384]{2,1,0:T(2,128)(2,1)}, u32[]{:S(2)}) copy-start(bf16[768,2,384]{2,1,0:T(2,128)(2,1)} %param.27) | copy-start | bytes 3538948
  89.4 7.4 %collective-permute-start.7 = (bf16[4,480,384]{2,1,0:T(8,128)(2,1)}, bf16[4,480,384]{2,1,0:T(8,128)(2,1)}, u32[]{:S(2)}, u32[]{:S(2)}) collective-permute-start(bf16[4,480,384]{2,1,0:T(8,128)(2,1)} %pad_maximum_fusion.12), channel_id=1, source_target_pairs={{0,2},{2,0},{4,6},{6,4},{8,10},{10,8},{12,14},{14,12},{16,18},{18,... | collective-permute-start | bytes 4423688 | tf_op jit(solution)/shard_map/ppermute | solution.py:555
  93.6 21.8 %collective-permute-start.8 = (bf16[384,768]{1,0:T(8,128)(2,1)}, bf16[384,768]{1,0:T(8,128)(2,1)}, u32[]{:S(2)}, u32[]{:S(2)}) collective-permute-start(bf16[384,768]{1,0:T(8,128)(2,1)} %get-tuple-element.159), channel_id=1, source_target_pairs={{0,1},{1,0},{2,3},{3,2},{4,5},{5,4},{6,7},{7,6},{8,9},{9,8},{10,11... | collective-permute-start | bytes 1769480 | tf_op jit(solution)/shard_map/ppermute | solution.py:552
  95.4 47.2 %collective-permute-start.10 = (bf16[8,128,768]{2,1,0:T(8,128)(2,1)S(1)}, bf16[8,128,768]{2,1,0:T(8,128)(2,1)}, u32[]{:S(2)}, u32[]{:S(2)}) collective-permute-start(bf16[8,128,768]{2,1,0:T(8,128)(2,1)S(1)} %slice.467), channel_id=1, source_target_pairs={{0,1},{1,0},{2,3},{3,2},{4,5},{5,4},{6,7},{7,6},{8,9},{9,8},{10,11... | collective-permute-start | bytes 4718600 | tf_op jit(solution)/shard_map/ppermute | solution.py:552
  100.6 12.7 %copy-start.57 = (bf16[8,96,384]{2,1,0:T(8,128)(2,1)}, bf16[8,96,384]{2,1,0:T(8,128)(2,1)S(1)}, u32[]{:S(2)}) copy-start(bf16[8,96,384]{2,1,0:T(8,128)(2,1)S(1)} %get-tuple-element.364) | copy-start | bytes 1769476
  100.6 18.4 %copy-start.51 = (bf16[8,96,384]{2,1,0:T(8,128)(2,1)}, bf16[8,96,384]{2,1,0:T(8,128)(2,1)S(1)}, u32[]{:S(2)}) copy-start(bf16[8,96,384]{2,1,0:T(8,128)(2,1)S(1)} %get-tuple-element.363) | copy-start | bytes 1769476
  100.6 18.4 %copy-start.54 = (bf16[8,96,384]{2,1,0:T(8,128)(2,1)}, bf16[8,96,384]{2,1,0:T(8,128)(2,1)S(1)}, u32[]{:S(2)}) copy-start(bf16[8,96,384]{2,1,0:T(8,128)(2,1)S(1)} %get-tuple-element.365) | copy-start | bytes 1769476
  115.3 9.5 %copy-start.18 = (bf16[1024,768]{1,0:T(8,128)(2,1)}, bf16[1024,768]{1,0:T(8,128)(2,1)S(1)}, u32[]{:S(2)}) copy-start(bf16[1024,768]{1,0:T(8,128)(2,1)S(1)} %concatenate.206.q_ref) | copy-start | bytes 4718596
  115.3 16.6 %collective-permute-start.9 = (bf16[1,384,768]{2,1,0:T(8,128)(2,1)}, bf16[1,384,768]{2,1,0:T(8,128)(2,1)S(1)}, u32[]{:S(2)}, u32[]{:S(2)}) collective-permute-start(bf16[1,384,768]{2,1,0:T(8,128)(2,1)} %bitcast.16), channel_id=1, source_target_pairs={{0,4},{2,10},{4,0},{6,14},{8,12},{10,2},{12,8},{14,6},{16,20},{18,... | collective-permute-start | bytes 1769480 | tf_op jit(solution)/shard_map/ppermute | solution.py:555
  131.9 11.1 %copy-start.82 = (bf16[1536]{0:T(1024)(128)(2,1)S(1)}, bf16[1536]{0:T(1024)(128)(2,1)}, u32[]{:S(2)}) copy-start(bf16[1536]{0:T(1024)(128)(2,1)} %param.34) | copy-start | bytes 9220
  131.9 11.2 %copy-start.92 = (bf16[384]{0:T(512)(128)(2,1)S(1)}, bf16[384]{0:T(512)(128)(2,1)}, u32[]{:S(2)}) copy-start(bf16[384]{0:T(512)(128)(2,1)} %param.36) | copy-start | bytes 2308
  131.9 11.8 %copy-start.52 = (bf16[8,96,384]{2,1,0:T(8,128)(2,1)S(1)}, bf16[8,96,384]{2,1,0:T(8,128)(2,1)}, u32[]{:S(2)}) copy-start(bf16[8,96,384]{2,1,0:T(8,128)(2,1)} %copy-done.51) | copy-start | bytes 1769476
  131.9 11.8 %copy-start.55 = (bf16[8,96,384]{2,1,0:T(8,128)(2,1)S(1)}, bf16[8,96,384]{2,1,0:T(8,128)(2,1)}, u32[]{:S(2)}) copy-start(bf16[8,96,384]{2,1,0:T(8,128)(2,1)} %copy-done.54) | copy-start | bytes 1769476
  131.9 11.8 %copy-start.60 = (bf16[768,384]{1,0:T(8,128)(2,1)S(1)}, bf16[768,384]{1,0:T(8,128)(2,1)}, u32[]{:S(2)}) copy-start(bf16[768,384]{1,0:T(8,128)(2,1)} %get-tuple-element.493) | copy-start | bytes 1769476
  132.0 11.8 %copy-start.63 = (bf16[768,384]{1,0:T(8,128)(2,1)S(1)}, bf16[768,384]{1,0:T(8,128)(2,1)}, u32[]{:S(2)}) copy-start(bf16[768,384]{1,0:T(8,128)(2,1)} %get-tuple-element.494) | copy-start | bytes 1769476
  142.6 15.3 %collective-permute-start.11 = (bf16[2,384,768]{2,1,0:T(8,128)(2,1)S(1)}, bf16[2,384,768]{2,1,0:T(8,128)(2,1)S(1)}, u32[]{:S(2)}, u32[]{:S(2)}) collective-permute-start(bf16[2,384,768]{2,1,0:T(8,128)(2,1)S(1)} %pad_maximum_fusion.14), channel_id=1, source_target_pairs={{0,8},{2,6},{4,12},{6,2},{8,0},{10,14},{12,4},{14,10},{16,24},{18,... | collective-permute-start | bytes 3538952 | tf_op jit(solution)/shard_map/ppermute | solution.py:555
  158.4 7.1 %collective-permute-start.12 = (bf16[4,384,768]{2,1,0:T(8,128)(2,1)S(1)}, bf16[4,384,768]{2,1,0:T(8,128)(2,1)S(1)}, u32[]{:S(2)}, u32[]{:S(2)}) collective-permute-start(bf16[4,384,768]{2,1,0:T(8,128)(2,1)S(1)} %pad_maximum_fusion.3), channel_id=1, source_target_pairs={{0,2},{2,0},{4,6},{6,4},{8,10},{10,8},{12,14},{14,12},{16,18},{18,... | collective-permute-start | bytes 7077896 | tf_op jit(solution)/shard_map/ppermute | solution.py:555
  211.0 12.8 %collective-permute-start.13 = (bf16[2,1536,768]{2,1,0:T(8,128)(2,1)}, bf16[2,1536,768]{2,1,0:T(8,128)(2,1)}, u32[]{:S(2)}, u32[]{:S(2)}) collective-permute-start(bf16[2,1536,768]{2,1,0:T(8,128)(2,1)} %get-tuple-element.172), channel_id=1, source_target_pairs={{0,2},{2,0},{4,6},{6,4},{8,10},{10,8},{12,14},{14,12},{16,18},{18,... | collective-permute-start | bytes 14155784 | tf_op jit(solution)/shard_map/ppermute | solution.py:555
  229.5 28.3 %collective-permute-start.14 = (bf16[2,768,768]{2,1,0:T(8,128)(2,1)}, bf16[2,768,768]{2,1,0:T(8,128)(2,1)}, u32[]{:S(2)}, u32[]{:S(2)}) collective-permute-start(bf16[2,768,768]{2,1,0:T(8,128)(2,1)} %get-tuple-element.339), channel_id=1, source_target_pairs={{0,4},{2,10},{4,0},{6,14},{8,12},{10,2},{12,8},{14,6},{16,20},{18,... | collective-permute-start | bytes 7077896 | tf_op jit(solution)/shard_map/ppermute | solution.py:555
  272.4 15.6 %collective-permute-start.15 = (bf16[2,384,768]{2,1,0:T(8,128)(2,1)}, bf16[2,384,768]{2,1,0:T(8,128)(2,1)S(1)}, u32[]{:S(2)}, u32[]{:S(2)}) collective-permute-start(bf16[2,384,768]{2,1,0:T(8,128)(2,1)} %get-tuple-element.353), channel_id=1, source_target_pairs={{0,8},{2,6},{4,12},{6,2},{8,0},{10,14},{12,4},{14,10},{16,24},{18,... | collective-permute-start | bytes 3538952 | tf_op jit(solution)/shard_map/ppermute | solution.py:555
  277.9 48.8 %copy-start.24 = (bf16[1024,768]{1,0:T(8,128)(2,1)}, bf16[1024,768]{1,0:T(8,128)(2,1)S(1)}, u32[]{:S(2)}) copy-start(bf16[1024,768]{1,0:T(8,128)(2,1)S(1)} %convolution_convert_fusion.1) | copy-start | bytes 4718596
  278.0 11.4 %slice-start.4 = ((s8[6291456]{0:T(1024)(128)(4,1)}), s8[4194304]{0:T(1024)(128)(4,1)S(1)}, s32[]{:S(2)}) async-start(s8[6291456]{0:T(1024)(128)(4,1)} %bitcast.150), calls=%async_computation.4 | async-start | bytes 8388608
  278.0 11.3 %slice-start.5 = ((s8[6291456]{0:T(1024)(128)(4,1)}), s8[2097152]{0:T(1024)(128)(4,1)S(1)}, s32[]{:S(2)}) async-start(s8[6291456]{0:T(1024)(128)(4,1)} %bitcast.150), calls=%async_computation.5 | async-start | bytes 4194304
  289.1 14.1 %collective-permute-start.16 = (bf16[1,384,768]{2,1,0:T(8,128)(2,1)}, bf16[1,384,768]{2,1,0:T(8,128)(2,1)S(1)}, u32[]{:S(2)}, u32[]{:S(2)}) collective-permute-start(bf16[1,384,768]{2,1,0:T(8,128)(2,1)} %get-tuple-element.392), channel_id=1, source_target_pairs={{0,1},{1,0},{2,3},{3,2},{4,5},{5,4},{6,7},{7,6},{8,9},{9,8},{10,11... | collective-permute-start | bytes 1769480 | tf_op jit(solution)/shard_map/ppermute | solution.py:552
  296.7 111.9 %collective-permute-start.27 = (bf16[16,128,768]{2,1,0:T(8,128)(2,1)}, bf16[16,128,768]{2,1,0:T(8,128)(2,1)}, u32[]{:S(2)}, u32[]{:S(2)}) collective-permute-start(bf16[16,128,768]{2,1,0:T(8,128)(2,1)} %bitcast.26), channel_id=1, source_target_pairs={{0,1},{1,0},{2,3},{3,2},{4,5},{5,4},{6,7},{7,6},{8,9},{9,8},{10,11... | collective-permute-start | bytes 9437192 | tf_op jit(solution)/shard_map/ppermute | solution.py:552
  307.5 16.7 %collective-permute-start.17 = (bf16[1,192,768]{2,1,0:T(8,128)(2,1)S(1)}, bf16[1,192,768]{2,1,0:T(8,128)(2,1)S(1)}, u32[]{:S(2)}, u32[]{:S(2)}) collective-permute-start(bf16[1,192,768]{2,1,0:T(8,128)(2,1)S(1)} %get-tuple-element.433), channel_id=1, source_target_pairs={{0,16},{2,18},{4,20},{6,22},{8,24},{10,26},{12,28},{14,30},{16,0},... | collective-permute-start | bytes 884744 | tf_op jit(solution)/shard_map/ppermute | solution.py:555
  312.5 11.7 %collective-permute-start.18 = (bf16[2,1536,384]{2,1,0:T(8,128)(2,1)S(1)}, bf16[2,1536,384]{2,1,0:T(8,128)(2,1)S(1)}, u32[]{:S(2)}, u32[]{:S(2)}) collective-permute-start(bf16[2,1536,384]{2,1,0:T(8,128)(2,1)S(1)} %get-tuple-element.199), channel_id=1, source_target_pairs={{0,2},{2,0},{4,6},{6,4},{8,10},{10,8},{12,14},{14,12},{16,18},{18,... | collective-permute-start | bytes 7077896 | tf_op jit(solution)/shard_map/ppermute | solution.py:555
  325.9 22.0 %collective-permute-start.20 = (bf16[2,768,384]{2,1,0:T(8,128)(2,1)}, bf16[2,768,384]{2,1,0:T(8,128)(2,1)}, u32[]{:S(2)}, u32[]{:S(2)}) collective-permute-start(bf16[2,768,384]{2,1,0:T(8,128)(2,1)} %get-tuple-element.349), channel_id=1, source_target_pairs={{0,4},{2,10},{4,0},{6,14},{8,12},{10,2},{12,8},{14,6},{16,20},{18,... | collective-permute-start | bytes 3538952 | tf_op jit(solution)/shard_map/ppermute | solution.py:555
  326.2 19.6 %collective-permute-start.19 = (bf16[192,768]{1,0:T(8,128)(2,1)S(1)}, bf16[192,768]{1,0:T(8,128)(2,1)}, u32[]{:S(2)}, u32[]{:S(2)}) collective-permute-start(bf16[192,768]{1,0:T(8,128)(2,1)S(1)} %fusion.60), channel_id=1, source_target_pairs={{0,16},{2,18},{4,20},{6,22},{8,24},{10,26},{12,28},{14,30},{16,0},... | collective-permute-start | bytes 884744 | tf_op jit(solution)/shard_map/ppermute | solution.py:555
  353.1 20.8 %collective-permute-start.21 = (bf16[384,768]{1,0:T(8,128)(2,1)}, bf16[384,768]{1,0:T(8,128)(2,1)}, u32[]{:S(2)}, u32[]{:S(2)}) collective-permute-start(bf16[384,768]{1,0:T(8,128)(2,1)} %pad_maximum_fusion.27), channel_id=1, source_target_pairs={{0,8},{2,6},{4,12},{6,2},{8,0},{10,14},{12,4},{14,10},{16,24},{18,... | collective-permute-start | bytes 1769480 | tf_op jit(solution)/shard_map/ppermute | solution.py:555
  372.1 9.1 %collective-permute-start.22 = (bf16[2,384,384]{2,1,0:T(8,128)(2,1)S(1)}, bf16[2,384,384]{2,1,0:T(8,128)(2,1)S(1)}, u32[]{:S(2)}, u32[]{:S(2)}) collective-permute-start(bf16[2,384,384]{2,1,0:T(8,128)(2,1)S(1)} %get-tuple-element.386), channel_id=1, source_target_pairs={{0,8},{2,6},{4,12},{6,2},{8,0},{10,14},{12,4},{14,10},{16,24},{18,... | collective-permute-start | bytes 1769480 | tf_op jit(solution)/shard_map/ppermute | solution.py:555
  385.2 37.0 %collective-permute-start.24 = (bf16[1,384,384]{2,1,0:T(8,128)(2,1)}, bf16[1,384,384]{2,1,0:T(8,128)(2,1)}, u32[]{:S(2)}, u32[]{:S(2)}) collective-permute-start(bf16[1,384,384]{2,1,0:T(8,128)(2,1)} %get-tuple-element.423), channel_id=1, source_target_pairs={{0,1},{1,0},{2,3},{3,2},{4,5},{5,4},{6,7},{7,6},{8,9},{9,8},{10,11... | collective-permute-start | bytes 884744 | tf_op jit(solution)/shard_map/ppermute | solution.py:552
  388.0 15.4 %collective-permute-start.23 = (bf16[768,768]{1,0:T(8,128)(2,1)S(1)}, bf16[768,768]{1,0:T(8,128)(2,1)S(1)}, u32[]{:S(2)}, u32[]{:S(2)}) collective-permute-start(bf16[768,768]{1,0:T(8,128)(2,1)S(1)} %pad_maximum_fusion.15), channel_id=1, source_target_pairs={{0,4},{2,10},{4,0},{6,14},{8,12},{10,2},{12,8},{14,6},{16,20},{18,... | collective-permute-start | bytes 3538952 | tf_op jit(solution)/shard_map/ppermute | solution.py:555
  389.0 14.7 %collective-permute-start.25 = (bf16[2,1536,384]{2,1,0:T(8,128)(2,1)S(1)}, bf16[2,1536,384]{2,1,0:T(8,128)(2,1)S(1)}, u32[]{:S(2)}, u32[]{:S(2)}) collective-permute-start(bf16[2,1536,384]{2,1,0:T(8,128)(2,1)S(1)} %get-tuple-element.224), channel_id=1, source_target_pairs={{0,2},{2,0},{4,6},{6,4},{8,10},{10,8},{12,14},{14,12},{16,18},{18,... | collective-permute-start | bytes 7077896 | tf_op jit(solution)/shard_map/ppermute | solution.py:555
  396.0 10.8 %copy-start.10 = (f32[1024,768]{1,0:T(8,128)}, f32[1024,768]{1,0:T(8,128)S(1)}, u32[]{:S(2)}) copy-start(f32[1024,768]{1,0:T(8,128)S(1)} %fusion.37) | copy-start | bytes 9437188
  405.8 16.4 %collective-permute-start.26 = (bf16[2,768,384]{2,1,0:T(8,128)(2,1)}, bf16[2,768,384]{2,1,0:T(8,128)(2,1)}, u32[]{:S(2)}, u32[]{:S(2)}) collective-permute-start(bf16[2,768,384]{2,1,0:T(8,128)(2,1)} %get-tuple-element.345), channel_id=1, source_target_pairs={{0,4},{2,10},{4,0},{6,14},{8,12},{10,2},{12,8},{14,6},{16,20},{18,... | collective-permute-start | bytes 3538952 | tf_op jit(solution)/shard_map/ppermute | solution.py:555
  422.2 6.2 %collective-permute-start.31 = (bf16[1536,768]{1,0:T(8,128)(2,1)S(1)}, bf16[1536,768]{1,0:T(8,128)(2,1)S(1)}, u32[]{:S(2)}, u32[]{:S(2)}) collective-permute-start(bf16[1536,768]{1,0:T(8,128)(2,1)S(1)} %pad_maximum_fusion.7), channel_id=1, source_target_pairs={{0,2},{2,0},{4,6},{6,4},{8,10},{10,8},{12,14},{14,12},{16,18},{18,... | collective-permute-start | bytes 7077896 | tf_op jit(solution)/shard_map/ppermute | solution.py:555
  424.1 4.2 collective-permute-start.30
  425.2 9.4 %collective-permute-start.28 = (bf16[1,192,384]{2,1,0:T(8,128)(2,1)S(1)}, bf16[1,192,384]{2,1,0:T(8,128)(2,1)S(1)}, u32[]{:S(2)}, u32[]{:S(2)}) collective-permute-start(bf16[1,192,384]{2,1,0:T(8,128)(2,1)S(1)} %get-tuple-element.447), channel_id=1, source_target_pairs={{0,16},{2,18},{4,20},{6,22},{8,24},{10,26},{12,28},{14,30},{16,0},... | collective-permute-start | bytes 442376 | tf_op jit(solution)/shard_map/ppermute | solution.py:555
  426.9 9.1 %collective-permute-start.29 = (bf16[2,384,384]{2,1,0:T(8,128)(2,1)S(1)}, bf16[2,384,384]{2,1,0:T(8,128)(2,1)S(1)}, u32[]{:S(2)}, u32[]{:S(2)}) collective-permute-start(bf16[2,384,384]{2,1,0:T(8,128)(2,1)S(1)} %get-tuple-element.376), channel_id=1, source_target_pairs={{0,8},{2,6},{4,12},{6,2},{8,0},{10,14},{12,4},{14,10},{16,24},{18,... | collective-permute-start | bytes 1769480 | tf_op jit(solution)/shard_map/ppermute | solution.py:555
  436.0 7.0 %collective-permute-start.34 = (f32[104,128]{1,0:T(8,128)S(1)}, f32[104,128]{1,0:T(8,128)S(1)}, u32[]{:S(2)}, u32[]{:S(2)}) collective-permute-start(f32[104,128]{1,0:T(8,128)S(1)} %add.393), channel_id=1, source_target_pairs={{0,4},{2,6},{4,0},{6,2},{8,12},{10,14},{12,8},{14,10},{16,20},{18,... | collective-permute-start | bytes 159752 | tf_op jit(solution)/shard_map/ppermute | solution.py:555
  436.7 6.5 %collective-permute-start.32 = (bf16[192,384]{1,0:T(8,128)(2,1)S(1)}, bf16[192,384]{1,0:T(8,128)(2,1)S(1)}, u32[]{:S(2)}, u32[]{:S(2)}) collective-permute-start(bf16[192,384]{1,0:T(8,128)(2,1)S(1)} %fusion.63), channel_id=1, source_target_pairs={{0,16},{2,18},{4,20},{6,22},{8,24},{10,26},{12,28},{14,30},{16,0},... | collective-permute-start | bytes 442376 | tf_op jit(solution)/shard_map/ppermute | solution.py:555
  439.3 6.0 %collective-permute-start.33 = (bf16[1,384,384]{2,1,0:T(8,128)(2,1)S(1)}, bf16[1,384,384]{2,1,0:T(8,128)(2,1)S(1)}, u32[]{:S(2)}, u32[]{:S(2)}) collective-permute-start(bf16[1,384,384]{2,1,0:T(8,128)(2,1)S(1)} %get-tuple-element.417), channel_id=1, source_target_pairs={{0,1},{1,0},{2,3},{3,2},{4,5},{5,4},{6,7},{7,6},{8,9},{9,8},{10,11... | collective-permute-start | bytes 884744 | tf_op jit(solution)/shard_map/ppermute | solution.py:552
  445.3 5.6 %collective-permute-start.35 = (bf16[384,384]{1,0:T(8,128)(2,1)S(1)}, bf16[384,384]{1,0:T(8,128)(2,1)S(1)}, u32[]{:S(2)}, u32[]{:S(2)}) collective-permute-start(bf16[384,384]{1,0:T(8,128)(2,1)S(1)} %pad_maximum_fusion.33), channel_id=1, source_target_pairs={{0,8},{2,6},{4,12},{6,2},{8,0},{10,14},{12,4},{14,10},{16,24},{18,... | collective-permute-start | bytes 884744 | tf_op jit(solution)/shard_map/ppermute | solution.py:555
  445.6 3.0 collective-permute-start.37
  445.7 6.6 %collective-permute-start.36 = (bf16[1,192,384]{2,1,0:T(8,128)(2,1)S(1)}, bf16[1,192,384]{2,1,0:T(8,128)(2,1)S(1)}, u32[]{:S(2)}, u32[]{:S(2)}) collective-permute-start(bf16[1,192,384]{2,1,0:T(8,128)(2,1)S(1)} %get-tuple-element.443), channel_id=1, source_target_pairs={{0,16},{2,18},{4,20},{6,22},{8,24},{10,26},{12,28},{14,30},{16,0},... | collective-permute-start | bytes 442376 | tf_op jit(solution)/shard_map/ppermute | solution.py:555
  452.3 13.9 %collective-permute-start.38 = (bf16[768,384]{1,0:T(8,128)(2,1)S(1)}, bf16[768,384]{1,0:T(8,128)(2,1)S(1)}, u32[]{:S(2)}, u32[]{:S(2)}) collective-permute-start(bf16[768,384]{1,0:T(8,128)(2,1)S(1)} %pad_maximum_fusion.28), channel_id=1, source_target_pairs={{0,4},{2,10},{4,0},{6,14},{8,12},{10,2},{12,8},{14,6},{16,20},{18,... | collective-permute-start | bytes 1769480 | tf_op jit(solution)/shard_map/ppermute | solution.py:555
  452.4 13.1 %collective-permute-start.39 = (bf16[192,384]{1,0:T(8,128)(2,1)S(1)}, bf16[192,384]{1,0:T(8,128)(2,1)S(1)}, u32[]{:S(2)}, u32[]{:S(2)}) collective-permute-start(bf16[192,384]{1,0:T(8,128)(2,1)S(1)} %fusion.64), channel_id=1, source_target_pairs={{0,16},{2,18},{4,20},{6,22},{8,24},{10,26},{12,28},{14,30},{16,0},... | collective-permute-start | bytes 442376 | tf_op jit(solution)/shard_map/ppermute | solution.py:555
  453.9 11.5 %collective-permute-start.40 = (f32[104,128]{1,0:T(8,128)S(1)}, f32[104,128]{1,0:T(8,128)S(1)}, u32[]{:S(2)}, u32[]{:S(2)}) collective-permute-start(f32[104,128]{1,0:T(8,128)S(1)} %add.400), channel_id=1, source_target_pairs={{0,16},{2,18},{4,20},{6,22},{8,24},{10,26},{12,28},{14,30},{16,0},... | collective-permute-start | bytes 159752 | tf_op jit(solution)/shard_map/ppermute | solution.py:555
  466.4 12.6 %collective-permute-start.41 = (bf16[1536,384]{1,0:T(8,128)(2,1)S(1)}, bf16[1536,384]{1,0:T(8,128)(2,1)S(1)}, u32[]{:S(2)}, u32[]{:S(2)}) collective-permute-start(bf16[1536,384]{1,0:T(8,128)(2,1)S(1)} %pad_maximum_fusion.16), channel_id=1, source_target_pairs={{0,2},{2,0},{4,6},{6,4},{8,10},{10,8},{12,14},{14,12},{16,18},{18,... | collective-permute-start | bytes 3538952 | tf_op jit(solution)/shard_map/ppermute | solution.py:555
  473.1 5.9 %collective-permute-start.42 = (bf16[384,384]{1,0:T(8,128)(2,1)S(1)}, bf16[384,384]{1,0:T(8,128)(2,1)S(1)}, u32[]{:S(2)}, u32[]{:S(2)}) collective-permute-start(bf16[384,384]{1,0:T(8,128)(2,1)S(1)} %pad_maximum_fusion.34), channel_id=1, source_target_pairs={{0,8},{2,6},{4,12},{6,2},{8,0},{10,14},{12,4},{14,10},{16,24},{18,... | collective-permute-start | bytes 884744 | tf_op jit(solution)/shard_map/ppermute | solution.py:555
  474.1 3.3 collective-permute-start.43
  479.1 9.6 %collective-permute-start.44 = (bf16[768,384]{1,0:T(8,128)(2,1)S(1)}, bf16[768,384]{1,0:T(8,128)(2,1)S(1)}, u32[]{:S(2)}, u32[]{:S(2)}) collective-permute-start(bf16[768,384]{1,0:T(8,128)(2,1)S(1)} %pad_maximum_fusion.29), channel_id=1, source_target_pairs={{0,4},{2,10},{4,0},{6,14},{8,12},{10,2},{12,8},{14,6},{16,20},{18,... | collective-permute-start | bytes 1769480 | tf_op jit(solution)/shard_map/ppermute | solution.py:555
  489.0 9.5 %collective-permute-start.45 = (bf16[1536,384]{1,0:T(8,128)(2,1)S(1)}, bf16[1536,384]{1,0:T(8,128)(2,1)S(1)}, u32[]{:S(2)}, u32[]{:S(2)}) collective-permute-start(bf16[1536,384]{1,0:T(8,128)(2,1)S(1)} %pad_maximum_fusion.17), channel_id=1, source_target_pairs={{0,2},{2,0},{4,6},{6,4},{8,10},{10,8},{12,14},{14,12},{16,18},{18,... | collective-permute-start | bytes 3538952 | tf_op jit(solution)/shard_map/ppermute | solution.py:555
  (88 other events, 278.2 us)
